TPU v7x, 256 devices: a whole 4x4x8 slice. The times are simulated.
256 devices in a mesh: member: 4 (over x), tile: 32 (over y_hi, z, core), grp: 2 (over y_lo).
Axes of the slice: x: 4, y: 4 (y_hi: 2, y_lo: 2; y = y_hi * 2 + y_lo), z: 8, core: 2. Of those that a mesh axis runs over, the one named last changes fastest.
Arguments:
- members: float32 [80, 1024, 1024], P(('member', 'grp'), 'tile'), may hold values from -6 to 6
- courant_x: float32 [1024, 1024], P('tile'), may hold values from -0.48 to 0.48
- courant_y: float32 [1024, 1024], P('tile'), may hold values from -0.48 to 0.48
- obs_cell: int32 [32, 8, 1024], P('tile', ('member', 'grp')), may hold values from 0 to 4095
- innovation: float32 [32, 8, 1024], P('tile', ('member', 'grp')), may hold values from -6 to 6
- obs_weight: float32 [32, 8, 1024], P('tile', ('member', 'grp')), may hold values from 0.5 to 3
- stencil_offsets: int32 [9, 2], replicated, may hold values from -2 to 2, as said below
- stencil_weights: float32 [9], replicated, may hold values from 0.2 to 1
Outputs:
- analysis: float32 [80, 1024, 1024], P(('member', 'grp'), 'tile')
- increment: float32 [1024, 1024], P('tile', ('member', 'grp'))
Inputs may be any that keep to these rules, and one draw needn't show every extreme that they name: `stencil_offsets`: each row is a stencil entry's offsets along rows and columns; some entry reaches 2 cells along rows and some along columns. `obs_cell`: cells of a block are numbered row by row, 128 to a row.
All inputs are finite; a program needn't handle non-finite values.
Results may differ from a plain program's by a relative error of at most 0.0001.
Values sent between devices are 32-bit elements; how exact they have to be, the bound alone decides.
No kernel may reach another device: no remote copies, remote signals or barrier semaphores. Data moves between devices by JAX's collectives and lax.ppermute only.
A program may use at most 128 MiB of HBM per device.

v0:
```python
import math

import jax
import jax.numpy as jnp
from jax import lax
from jax.experimental import pallas as pl
from jax.experimental.pallas import tpu as pltpu
from jax.sharding import PartitionSpec as P

F32 = jnp.float32
BF16 = jnp.bfloat16
RADIUS = 2
STEP_SIZE = 0.25
GROUPS = 8
LOCAL = 10
ROWS = 32
LANES = 128
COLS = 1024
REACH = 4 * RADIUS
EDGE = REACH + 3
TALL = ROWS + 2 * REACH
WIDE = LANES + 2 * REACH
SLOTS = 12
SPARE = LOCAL * WIDE - (SLOTS - 1) * LANES
HALO = 136
VMEM = 48 * 1024 * 1024


def lane_ids(rows):
    return lax.broadcasted_iota(jnp.int32, (rows, LANES), 1)


def pieces(value, count):
    found = []
    for _ in range(count):
        part = value.astype(BF16)
        found.append(part)
        value = value - part.astype(F32)
    return found


def message_kernel(members, courant_x, courant_y, cell, innov, weight, up, down, fields):
    cells = cell[0]
    weights = weight[0]
    row_hit = lax.broadcasted_iota(jnp.int32, (ROWS, 1024), 0) == lax.shift_right_logical(cells, 7)
    col_hit = lax.broadcasted_iota(jnp.int32, (LANES, 1024), 0) == lax.bitwise_and(cells, LANES - 1)
    parts = pieces(weights * innov[0], 3) + pieces(weights, 3)
    hits = row_hit.astype(F32)
    left = jnp.concatenate([(hits * part.astype(F32)).astype(BF16) for part in parts], axis=0)
    sums = lax.dot_general(
        left, col_hit.astype(F32).astype(BF16), (((1,), (1,)), ((), ())), preferred_element_type=F32
    )
    for kind in range(2):
        base = 3 * ROWS * kind
        fields[kind] = (
            sums[base : base + ROWS]
            + sums[base + ROWS : base + 2 * ROWS]
            + sums[base + 2 * ROWS : base + 3 * ROWS]
        )
    for field in range(LOCAL + 2):
        if field < LOCAL:
            source = members.at[field]
        else:
            source = courant_x if field == LOCAL else courant_y
        up[field * EDGE : (field + 1) * EDGE, :] = source[0:EDGE, :]
        down[field * EDGE : (field + 1) * EDGE, :] = source[ROWS - EDGE : ROWS, :]
    base = (LOCAL + 2) * EDGE
    for kind in range(2):
        for row in range(REACH):
            lanes = slice(row * LANES, (row + 1) * LANES)
            up[base + kind : base + kind + 1, lanes] = fields[kind, row : row + 1, :]
            down[base + kind : base + kind + 1, lanes] = fields[
                kind, ROWS - REACH + row : ROWS - REACH + row + 1, :
            ]
    up[base + 2 : HALO, :] = jnp.zeros((HALO - base - 2, COLS), F32)
    down[base + 2 : HALO, :] = jnp.zeros((HALO - base - 2, COLS), F32)


TOP = 16
HEIGHT = 64


def send_plan():
    plan = [[] for _ in range(SLOTS)]
    for member in range(LOCAL):
        start = member * WIDE
        spans = (
            (start, start + REACH, -1),
            (start + REACH, start + REACH + LANES, 0),
            (start + REACH + LANES, start + WIDE, 1),
        )
        for low, high, offset in spans:
            while low < high:
                slot = low // LANES
                stop = min(high, (slot + 1) * LANES)
                plan[slot].append((member, offset, low - slot * LANES, stop - slot * LANES))
                low = stop
    return plan


def forecast_kernel(
    members, courant_x, courant_y, above, below, fields, out, send, fields_tall, old, new, coefs, rolled
):
    lane = lane_ids(8)
    first, last = lane == 0, lane == LANES - 1
    base = (LOCAL + 2) * EDGE
    for block in range(GROUPS):
        lanes = slice(block * LANES, (block + 1) * LANES)
        for kind, own in enumerate((courant_x, courant_y)):
            at = (LOCAL + kind) * EDGE
            new[kind, block + 1, TOP : TOP + ROWS, :] = own[:, lanes]
            new[kind, block + 1, TOP - EDGE : TOP, :] = above[at : at + EDGE, lanes]
            new[kind, block + 1, TOP + ROWS : TOP + ROWS + EDGE, :] = below[at : at + EDGE, lanes]
        for member in range(LOCAL):
            at = member * EDGE
            old[member, block + 1, TOP : TOP + ROWS, :] = members[member, :, lanes]
            old[member, block + 1, TOP - EDGE : TOP, :] = above[at : at + EDGE, lanes]
            old[member, block + 1, TOP + ROWS : TOP + ROWS + EDGE, :] = below[at : at + EDGE, lanes]
    nothing = jnp.zeros((HEIGHT, LANES), F32)
    for member in range(LOCAL):
        for side in (0, GROUPS + 1):
            old[member, side] = nothing
            rolled[member, side] = nothing[:TALL]

    @pl.loop(0, GROUPS)
    def _(block):
        for part in range(HEIGHT // 8):
            rows = slice(part * 8, part * 8 + 8)
            cx = new[0, block + 1, rows, :]
            cy = new[1, block + 1, rows, :]
            x_plus, x_minus = jnp.maximum(cx, 0.0), jnp.minimum(cx, 0.0)
            y_plus, y_minus = jnp.maximum(cy, 0.0), jnp.minimum(cy, 0.0)
            coefs[0, block, rows, :] = 1.0 - x_plus + x_minus - y_plus + y_minus
            coefs[1, block, rows, :] = x_plus
            coefs[2, block, rows, :] = -x_minus
            coefs[3, block, rows, :] = y_plus
            coefs[4, block, rows, :] = -y_minus

    for member in range(LOCAL):
        for side in (0, GROUPS + 1):
            new[member, side] = nothing

    buffers = (old, new)
    for step in range(3):
        source, target = buffers[step % 2], buffers[(step + 1) % 2]
        starts = range(TOP - EDGE + 1 + step, TOP + ROWS + EDGE - 1 - step, 8)

        @pl.loop(0, GROUPS)
        def _(block):
            for low in starts:
                rows = slice(low, low + 8)
                k_mid, k_up, k_down, k_left, k_right = (
                    coefs[kind, block, rows, :] for kind in range(5)
                )
                above_rows = slice(low - 1, low + 7)
                below_rows = slice(low + 1, low + 9)
                for member in range(LOCAL):
                    mid = source[member, block + 1, rows, :]
                    before = source[member, block, rows, :]
                    after = source[member, block + 2, rows, :]
                    value = (
                        k_mid * mid
                        + k_up * source[member, block + 1, above_rows, :]
                        + k_down * source[member, block + 1, below_rows, :]
                        + k_left * pltpu.roll(jnp.where(last, before, mid), 1, 1)
                        + k_right * pltpu.roll(jnp.where(first, after, mid), LANES - 1, 1)
                    )
                    if step < 2:
                        target[member, block + 1, rows, :] = value
                    else:
                        shift = (member * WIDE + REACH) % LANES
                        rolled[member, block + 1, low - 8 : low, :] = (
                            pltpu.roll(value, shift, 1) if shift else value
                        )
                        if TOP <= low < TOP + ROWS:
                            target[member, block + 1, rows, :] = value

    final = buffers[1]
    for member in range(LOCAL):
        for block in range(GROUPS):
            out[member, :, block * LANES : (block + 1) * LANES] = final[
                member, block + 1, TOP : TOP + ROWS, :
            ]

    for kind in range(2):
        for row in range(REACH):
            lanes = slice(row * LANES, (row + 1) * LANES)
            fields_tall[kind, row : row + 1, :] = above[base + kind : base + kind + 1, lanes]
            fields_tall[kind, REACH + ROWS + row : REACH + ROWS + row + 1, :] = below[
                base + kind : base + kind + 1, lanes
            ]
        fields_tall[kind, REACH : REACH + ROWS, :] = fields[kind]

    tall_lane = lane_ids(TALL)
    ends = jnp.where(
        tall_lane < SPARE + 2 * REACH,
        pltpu.roll(fields_tall[0], SPARE + REACH, 1),
        pltpu.roll(fields_tall[1], SPARE + 3 * REACH, 1),
    )
    plan = send_plan()

    @pl.loop(0, GROUPS)
    def _(block):
        for slot in range(SLOTS):
            value = ends if slot == SLOTS - 1 else None
            for member, offset, low, high in plan[slot]:
                part = rolled[member, block + 1 + offset]
                if value is None:
                    value = part
                else:
                    value = jnp.where((tall_lane >= low) & (tall_lane < high), part, value)
            send[block, slot] = value


DEEP = 56


def member_place(member):
    return member * WIDE // LANES, member * WIDE % LANES


def folded(slots, lane):
    near, far = None, None
    for member in range(LOCAL):
        base, shift = member_place(member)
        here, there = slots(base), slots(base + 1)
        if shift:
            here = pltpu.roll(jnp.where(lane >= shift, here, there), LANES - shift, 1)
            there = pltpu.roll(there, LANES - shift, 1)
        near = here if near is None else near + here
        far = there if far is None else far + there
    return near, far


def spread_out(near, far, lane, store):
    slots = [None] * SLOTS
    for member in range(LOCAL):
        base, shift = member_place(member)
        moved = pltpu.roll(near, shift, 1) if shift else near
        tail = pltpu.roll(far, shift, 1) if shift else far
        slots[base] = moved if slots[base] is None else jnp.where(lane >= shift, moved, slots[base])
        slots[base + 1] = jnp.where(
            lane < shift, moved, jnp.where(lane < shift + 2 * REACH, tail, 0.0)
        )
    for slot in range(SLOTS):
        store(slot, slots[slot])


def shifted_copies(copies, slots, rows):
    lane = lane_ids(rows)

    @pl.loop(0, slots)
    def _(slot):
        mid = copies[RADIUS, slot, 0:rows, :]
        after = copies[RADIUS, jnp.minimum(slot + 1, SLOTS - 1), 0:rows, :]
        before = copies[RADIUS, jnp.maximum(slot - 1, 0), 0:rows, :]
        for shift in (1, 2):
            copies[RADIUS + shift, slot, 0:rows, :] = pltpu.roll(
                jnp.where(lane < shift, after, mid), LANES - shift, 1
            )
            copies[RADIUS - shift, slot, 0:rows, :] = pltpu.roll(
                jnp.where(lane >= LANES - shift, before, mid), shift, 1
            )


def analysis_kernel(
    place, offsets, weights, got, fields, increment, spread_copies,
    spread, averages, gains, inside, products, localized, total, plane,
):
    tile, block = place[0], place[1]
    lane = lane_ids(TALL)
    entries = offsets.shape[0]
    tap_row = [offsets[entry, 0] for entry in range(entries)]
    tap_col = [offsets[entry, 1] for entry in range(entries)]
    tap = [weights[entry] for entry in range(entries)]
    weight_sum = tap[0]
    for entry in range(1, entries):
        weight_sum = weight_sum + tap[entry]
    scale = 1.0 / jnp.full((1, LANES), weight_sum, F32)
    scale = scale * scale

    @pl.loop(0, SLOTS)
    def _(slot):
        value = got[0, slot]
        for source in range(1, GROUPS):
            value = value + got[source, slot]
        averages[slot] = value

    near, far = folded(lambda slot: averages[slot], lane)
    count = GROUPS * LOCAL

    def store_average(slot, value):
        averages[slot] = value

    spread_out(near / count, far / count, lane, store_average)
    deviation = 1.0 / math.sqrt(count - 1)

    @pl.loop(0, SLOTS)
    def _(slot):
        for source in range(GROUPS):
            spread[source, slot] = (got[source, slot] - averages[slot]) * deviation

    row = lax.broadcasted_iota(jnp.int32, (TALL, LANES), 0) + (tile * ROWS - REACH)
    col = lane + (block * LANES - REACH)
    row_ok = (row >= 0) & (row < ROWS * 32)
    near_ok = row_ok & (col >= 0) & (col < COLS)
    far_ok = row_ok & (col + LANES < COLS)

    def store_inside(slot, value):
        inside[slot, 0:TALL, :] = value
        inside[slot, TALL:DEEP, :] = jnp.zeros((DEEP - TALL, LANES), F32)

    spread_out(near_ok.astype(F32), far_ok.astype(F32), lane, store_inside)

    left_ends = got[jnp.maximum(block - 1, 0), SLOTS - 1]
    right_ends = got[jnp.minimum(block + 1, GROUPS - 1), SLOTS - 1]
    left_ends = jnp.where(block > 0, left_ends, 0.0)
    right_ends = jnp.where(block < GROUPS - 1, right_ends, 0.0)
    planes = []
    for kind in range(2):
        back = LANES - SPARE - 2 * REACH * kind
        own = pltpu.roll(fields[kind], REACH, 1)
        near = jnp.where(lane < REACH, pltpu.roll(left_ends, back, 1), own)
        far = jnp.where(lane < REACH, own, pltpu.roll(right_ends, back, 1))
        far = jnp.where(lane < 2 * REACH, far, 0.0)
        planes.append((near, far))

    def store_gain(slot, value):
        gains[slot] = value

    def sweep(slots, multiplier, z_low, z_rows, x_low, x_rows, finish):
        @pl.loop(0, slots)
        def _(slot):
            products[RADIUS, slot, 0:TALL, :] = multiplier(slot)

        shifted_copies(products, slots, TALL)

        @pl.loop(0, slots)
        def _(slot):
            value = None
            for entry in range(entries):
                term = tap[entry] * products[
                    RADIUS - tap_col[entry], slot, pl.ds(z_low - tap_row[entry], z_rows), :
                ]
                value = term if value is None else value + term
            rows = slice(z_low, z_low + z_rows)
            localized[RADIUS, slot, rows, :] = value * inside[slot, rows, :]

        shifted_copies(localized, slots, DEEP)

        @pl.loop(0, slots)
        def _(slot):
            value = None
            for entry in range(entries):
                term = tap[entry] * localized[
                    RADIUS + tap_col[entry], slot, pl.ds(x_low + tap_row[entry], x_rows), :
                ]
                value = term if value is None else value + term
            finish(slot, value)

    def apply(near, far, z_low, z_rows, x_low, x_rows):
        spread_out(near, far, lane, store_gain)
        ones = []

        def finish_ones(slot, value):
            plane[slot, 0:x_rows, :] = value

        sweep(2, lambda slot: gains[slot], z_low, z_rows, x_low, x_rows, finish_ones)

        @pl.loop(0, SLOTS)
        def _(slot):
            total[slot, 0:x_rows, :] = jnp.zeros((x_rows, LANES), F32)

        @pl.loop(0, GROUPS)
        def _(source):
            def finish(slot, value):
                total[slot, 0:x_rows, :] += value * spread[source, slot, x_low : x_low + x_rows, :]

            sweep(
                SLOTS, lambda slot: gains[slot] * spread[source, slot],
                z_low, z_rows, x_low, x_rows, finish,
            )

        near, far = folded(lambda slot: total[slot, 0:x_rows, :], lane_ids(x_rows))
        return (near + plane[0, 0:x_rows, :]) * scale, (far + plane[1, 0:x_rows, :]) * scale

    for slot in range(SLOTS):
        for kind in range(2 * RADIUS + 1):
            products[kind, slot, TALL:DEEP, :] = jnp.zeros((DEEP - TALL, LANES), F32)
        localized[RADIUS, slot] = jnp.zeros((DEEP, LANES), F32)

    (near_v, far_v), (near_w, far_w) = planes
    near, far = apply(near_v, far_v, 2, 48, 4, 40)
    for part, value in enumerate((near, far)):
        plane[2 + part, 0:TALL, :] = jnp.zeros((TALL, LANES), F32)
        plane[2 + part, 4:44, :] = value
    near = (STEP_SIZE * near_w) * plane[2, 0:TALL, :] - (2.0 - STEP_SIZE) * near_v
    far = (STEP_SIZE * far_w) * plane[3, 0:TALL, :] - (2.0 - STEP_SIZE) * far_v
    far = jnp.where(lane < 2 * REACH, far, 0.0)
    near, far = apply(near, far, 6, 40, 8, 32)
    short_lane = lane_ids(ROWS)
    result = pltpu.roll(jnp.where(short_lane < REACH, far, near), LANES - REACH, 1) * -STEP_SIZE
    increment[...] = result
    for target in range(GROUPS):
        spread_copies[target] = result


def recentre_kernel(fields, increments, out):
    for block in range(GROUPS):
        lanes = slice(block * LANES, (block + 1) * LANES)
        value = increments[block]
        for member in range(LOCAL):
            out[member, :, lanes] = fields[member, :, lanes] + value


def on_vmem(count):
    return [pl.BlockSpec(memory_space=pltpu.VMEM)] * count


def on_device(
    members, courant_x, courant_y, obs_cell, innovation, obs_weight, stencil_offsets, stencil_weights
):
    both = ("member", "grp")
    params = pltpu.CompilerParams(vmem_limit_bytes=VMEM)
    tiles = lax.axis_size("tile")
    up, down, fields = pl.pallas_call(
        message_kernel,
        out_shape=[
            jax.ShapeDtypeStruct((HALO, COLS), F32),
            jax.ShapeDtypeStruct((HALO, COLS), F32),
            jax.ShapeDtypeStruct((2, ROWS, LANES), F32),
        ],
        in_specs=on_vmem(6),
        out_specs=on_vmem(3),
        compiler_params=params,
        name="messages",
    )(members, courant_x, courant_y, obs_cell, innovation, obs_weight)
    above = lax.ppermute(down, "tile", [(i, i + 1) for i in range(tiles - 1)])
    below = lax.ppermute(up, "tile", [(i + 1, i) for i in range(tiles - 1)])
    forecast, send, fields_tall = pl.pallas_call(
        forecast_kernel,
        out_shape=[
            jax.ShapeDtypeStruct(members.shape, F32),
            jax.ShapeDtypeStruct((GROUPS, SLOTS, TALL, LANES), F32),
            jax.ShapeDtypeStruct((2, TALL, LANES), F32),
        ],
        in_specs=on_vmem(6),
        out_specs=on_vmem(3),
        scratch_shapes=[
            pltpu.VMEM((LOCAL, GROUPS + 2, HEIGHT, LANES), F32),
            pltpu.VMEM((LOCAL, GROUPS + 2, HEIGHT, LANES), F32),
            pltpu.VMEM((5, GROUPS, HEIGHT, LANES), F32),
            pltpu.VMEM((LOCAL, GROUPS + 2, TALL, LANES), F32),
        ],
        compiler_params=params,
        name="forecast",
    )(members, courant_x, courant_y, above, below, fields)
    got = lax.all_to_all(
        send.reshape(GROUPS, SLOTS * TALL, LANES), both, 0, 0, tiled=True
    ).reshape(GROUPS, SLOTS, TALL, LANES)
    place = jnp.stack([lax.axis_index("tile"), lax.axis_index(both)]).astype(jnp.int32)
    increment, copies = pl.pallas_call(
        analysis_kernel,
        out_shape=[
            jax.ShapeDtypeStruct((ROWS, LANES), F32),
            jax.ShapeDtypeStruct((GROUPS, ROWS, LANES), F32),
        ],
        in_specs=[pl.BlockSpec(memory_space=pltpu.SMEM)] * 3 + on_vmem(2),
        out_specs=on_vmem(2),
        scratch_shapes=[
            pltpu.VMEM((GROUPS, SLOTS, TALL, LANES), F32),
            pltpu.VMEM((SLOTS, TALL, LANES), F32),
            pltpu.VMEM((SLOTS, TALL, LANES), F32),
            pltpu.VMEM((SLOTS, DEEP, LANES), F32),
            pltpu.VMEM((2 * RADIUS + 1, SLOTS, DEEP, LANES), F32),
            pltpu.VMEM((2 * RADIUS + 1, SLOTS, DEEP, LANES), F32),
            pltpu.VMEM((SLOTS, TALL, LANES), F32),
            pltpu.VMEM((4, TALL, LANES), F32),
        ],
        compiler_params=params,
        name="analysis",
    )(place, stencil_offsets, stencil_weights, got, fields_tall)
    increments = lax.all_to_all(copies, both, 0, 0, tiled=True)
    analysis = pl.pallas_call(
        recentre_kernel,
        out_shape=jax.ShapeDtypeStruct(members.shape, F32),
        in_specs=on_vmem(2),
        out_specs=pl.BlockSpec(memory_space=pltpu.VMEM),
        compiler_params=params,
        name="recentre",
    )(forecast, increments)
    return analysis, increment


def solution(mesh):
    both = ("member", "grp")
    placed = (
        P(both, "tile", None),
        P("tile", None),
        P("tile", None),
        P("tile", both, None),
        P("tile", both, None),
        P("tile", both, None),
        P(),
        P(),
    )
    return jax.shard_map(
        on_device,
        mesh=mesh,
        in_specs=placed,
        out_specs=(P(both, "tile", None), P("tile", both)),
        check_vma=False,
    )
```

profile of v0, /device:TPU:16, one launch (start us, length us, event | category | flops | bytes accessed | tf_op | source)
XLA Modules:
  0.0 138.8 jit_solution(17329069617739409654)
XLA Ops:
  0.6 0.0 copy-start
  0.6 1.3 copy-done
  1.9 0.0 copy-start.3
  2.0 0.9 copy-done.3
  2.9 0.0 copy-start.4
  2.9 0.9 copy-done.4
  3.8 0.0 copy-start.5
  3.8 0.7 copy-done.5
  4.4 0.0 copy-start.6
  4.4 0.7 copy-done.6
  5.1 0.0 copy-start.7
  5.1 0.7 copy-done.7
  5.8 0.3 messages.1
  6.1 1.9 %collective-permute-start = (f32[136,1024]{1,0:T(8,128)S(1)}, f32[136,1024]{1,0:T(8,128)S(1)}, u32[]{:S(2)}, u32[]{:S(2)}) collective-permute-start(f32[136,1024]{1,0:T(8,128)S(1)} %get-tuple-element.10), channel_id=1, source_target_pairs={{0,2},{2,4},{4,6},{6,8},{8,10},{10,12},{12,14},{14,16},{16,18},{18... | collective-permute-start | bytes 1671176 | tf_op jit(solution)/shard_map/ppermute | solution.py:438
  8.1 7.3 %collective-permute-start.1 = (f32[136,1024]{1,0:T(8,128)S(1)}, f32[136,1024]{1,0:T(8,128)S(1)}, u32[]{:S(2)}, u32[]{:S(2)}) collective-permute-start(f32[136,1024]{1,0:T(8,128)S(1)} %get-tuple-element.11), channel_id=1, source_target_pairs={{2,0},{4,2},{6,4},{8,6},{10,8},{12,10},{14,12},{16,14},{18,16},{20... | collective-permute-start | bytes 1671176 | tf_op jit(solution)/shard_map/ppermute | solution.py:439
  15.3 5.3 %collective-permute-done.above = f32[136,1024]{1,0:T(8,128)S(1)} collective-permute-done((f32[136,1024]{1,0:T(8,128)S(1)}, f32[136,1024]{1,0:T(8,128)S(1)}, u32[]{:S(2)}, u32[]{:S(2)}) %collective-permute-start) | collective-permute-done | bytes 557088 | tf_op jit(solution)/shard_map/ppermute | solution.py:438
  20.6 1.8 %collective-permute-done.1.below = f32[136,1024]{1,0:T(8,128)S(1)} collective-permute-done((f32[136,1024]{1,0:T(8,128)S(1)}, f32[136,1024]{1,0:T(8,128)S(1)}, u32[]{:S(2)}, u32[]{:S(2)}) %collective-permute-start.1) | collective-permute-done | bytes 557088 | tf_op jit(solution)/shard_map/ppermute | solution.py:439
  22.4 15.7 %forecast.1 = (f32[10,32,1024]{2,1,0:T(8,128)S(1)}, f32[8,12,48,128]{3,2,1,0:T(8,128)}, f32[2,48,128]{2,1,0:T(8,128)S(1)}) custom-call(f32[10,32,1024]{2,1,0:T(8,128)S(1)} %copy-done, f32[32,1024]{1,0:T(8,128)S(1)} %copy-done.3, f32[32,1024]{1,0:T(8,128)S(1)} %copy-done.4, f32[136,1024]{1,0:T(8,128)S(1)} %collective-permute-done.above, ...), custom_call_target="tpu_custom_call" | custom-call | tf_op jit(solution)/shard_map/forecast/pallas_call | solution.py:440
  38.0 0.0 copy-start.1
  38.1 1.1 copy-done.1
  39.1 0.0 copy-start.9
  39.1 0.0 copy-start.8
  39.1 5.8 %all-to-all-start = ((f32[8,576,128]{2,1,0:T(8,128)}), f32[8,576,128]{2,1,0:T(8,128)S(1)}, u32[]{:S(2)}, u32[]{:S(2)}) async-start(f32[8,576,128]{2,1,0:T(8,128)} %bitcast.5), calls=%async_computation | async-start | bytes 4718592 | tf_op jit(solution)/shard_map/all_to_all | solution.py:458
  44.9 0.0 copy-done.9
  44.9 0.1 copy.10.offsets
  45.0 0.1 pad_add_fusion.place
  45.1 31.9 %all-to-all-done = f32[8,576,128]{2,1,0:T(8,128)S(1)} async-done(((f32[8,576,128]{2,1,0:T(8,128)}), f32[8,576,128]{2,1,0:T(8,128)S(1)}, u32[]{:S(2)}, u32[]{:S(2)}) %all-to-all-start) | async-done | bytes 2359328 | tf_op jit(solution)/shard_map/all_to_all | solution.py:458
  77.0 0.0 copy-done.8
  77.0 0.0 copy-start.2
  77.0 51.7 %analysis.1 = (f32[32,128]{1,0:T(8,128)}, f32[8,32,128]{2,1,0:T(8,128)S(1)}) custom-call(s32[2]{0:T(128)S(1)} %pad_add_fusion.place, s32[9,2]{1,0:T(8,128)S(1)} %copy.10.offsets, f32[9]{0:T(128)S(1)} %copy-done.8, f32[8,12,48,128]{3,2,1,0:T(8,128)S(1)} %bitcast.4, f32[2,48,128]{2,1,0:T(8,128)S(1)} %get-tuple-element.15.fields), custom_call_target="tpu_custom_call" | custom-call | tf_op jit(solution)/shard_map/analysis/pallas_call | solution.py:462
  128.7 8.8 %all_to_all.10.increments = f32[8,32,128]{2,1,0:T(8,128)S(1)} all-to-all(f32[8,32,128]{2,1,0:T(8,128)S(1)} %get-tuple-element.16), channel_id=1, replica_groups=mesh['member'=4,'tile'=32,'grp'=2] {'member','grp'}, dimensions={0} | all-to-all | bytes 262144 | tf_op jit(solution)/shard_map/all_to_all | solution.py:483
  137.5 0.0 copy-done.2
  137.5 1.3 recentre.1
Async XLA Ops:
  0.6 1.3 copy-start
  1.9 0.9 copy-start.3
  2.9 0.9 copy-start.4
  3.8 0.7 copy-start.5
  4.4 0.7 copy-start.6
  5.1 0.7 copy-start.7
  6.1 14.5 %collective-permute-start = (f32[136,1024]{1,0:T(8,128)S(1)}, f32[136,1024]{1,0:T(8,128)S(1)}, u32[]{:S(2)}, u32[]{:S(2)}) collective-permute-start(f32[136,1024]{1,0:T(8,128)S(1)} %get-tuple-element.10), channel_id=1, source_target_pairs={{0,2},{2,4},{4,6},{6,8},{8,10},{10,12},{12,14},{14,16},{16,18},{18... | collective-permute-start | bytes 1671176 | tf_op jit(solution)/shard_map/ppermute | solution.py:438
  8.1 14.3 %collective-permute-start.1 = (f32[136,1024]{1,0:T(8,128)S(1)}, f32[136,1024]{1,0:T(8,128)S(1)}, u32[]{:S(2)}, u32[]{:S(2)}) collective-permute-start(f32[136,1024]{1,0:T(8,128)S(1)} %get-tuple-element.11), channel_id=1, source_target_pairs={{2,0},{4,2},{6,4},{8,6},{10,8},{12,10},{14,12},{16,14},{18,16},{20... | collective-permute-start | bytes 1671176 | tf_op jit(solution)/shard_map/ppermute | solution.py:439
  38.0 1.1 copy-start.1
  39.1 5.8 %copy-start.9 = (s32[9,2]{0,1:T(2,128)S(1)}, s32[9,2]{0,1:T(2,128)}, u32[]{:S(2)}) copy-start(s32[9,2]{0,1:T(2,128)} %param.14) | copy-start | bytes 220
  39.1 37.9 %copy-start.8 = (f32[9]{0:T(128)S(1)}, f32[9]{0:T(128)}, u32[]{:S(2)}) copy-start(f32[9]{0:T(128)} %weights.1) | copy-start | bytes 112
  39.1 37.9 %all-to-all-start = ((f32[8,576,128]{2,1,0:T(8,128)}), f32[8,576,128]{2,1,0:T(8,128)S(1)}, u32[]{:S(2)}, u32[]{:S(2)}) async-start(f32[8,576,128]{2,1,0:T(8,128)} %bitcast.5), calls=%async_computation | async-start | bytes 4718592 | tf_op jit(solution)/shard_map/all_to_all | solution.py:458
  77.0 60.5 %copy-start.2 = (f32[10,32,1024]{2,1,0:T(8,128)S(1)}, f32[10,32,1024]{2,1,0:T(8,128)}, u32[]{:S(2)}) copy-start(f32[10,32,1024]{2,1,0:T(8,128)} %copy-done.1) | copy-start | bytes 3932164
where the time goes:
time: 140 us; the launch traced here: 139 us
  Pallas kernels  69 us (49%)
  waiting for transfers between devices  38.9 us (28%)
  starting transfers between devices  14.9 us (11%)
  blocking collectives  8.79 us (6%)
  local copies, waits for them, and re-layouts  6.34 us (5%)
    pallas_call x1, Pallas kernels, on_device(): pl.pallas_call(analysis_kernel, out_shape=[jax.ShapeDtypeStruct((ROWS, LA...  51.7 us
    all_to_all x1, waiting for transfers between devices, on_device(): lax.all_to_all(send.reshape(GROUPS, SLOTS * TALL, LANES), both, 0, 0, til...  31.9 us
    pallas_call x1, Pallas kernels, on_device(): pl.pallas_call(forecast_kernel, out_shape=[jax.ShapeDtypeStruct(members.s...  15.7 us
    all_to_all x1, blocking collectives, on_device(): increments = lax.all_to_all(copies, both, 0, 0, tiled=True)  8.79 us
    ppermute x1, starting transfers between devices, on_device(): below = lax.ppermute(up, 'tile', [(i + 1, i) for i in range(tiles - 1)])  7.26 us
    unnamed x21, local copies, waits for them, and re-layouts  6.34 us
    all_to_all x1, starting transfers between devices, on_device(): lax.all_to_all(send.reshape(GROUPS, SLOTS * TALL, LANES), both, 0, 0, til...  5.77 us
    ppermute x1, waiting for transfers between devices, on_device(): above = lax.ppermute(down, 'tile', [(i, i + 1) for i in range(tiles - 1)])  5.27 us
  transfers between devices with their start and end apart: 3, of which 3 were waited for; matrix products, arithmetic and copies ran while one was open for 0% of the time, Pallas kernels for 0%

commit v1 on v0

v1 whole, which is shorter than its diff:
```python
import math

import jax
import jax.numpy as jnp
from jax import lax
from jax.experimental import pallas as pl
from jax.experimental.pallas import tpu as pltpu
from jax.sharding import PartitionSpec as P

F32 = jnp.float32
BF16 = jnp.bfloat16
RADIUS = 2
STEP_SIZE = 0.25
GROUPS = 8
LOCAL = 10
ROWS = 32
LANES = 128
COLS = 1024
REACH = 4 * RADIUS
EDGE = REACH + 3
TALL = ROWS + 2 * REACH
WIDE = LANES + 2 * REACH
SLOTS = 12
SPARE = LOCAL * WIDE - (SLOTS - 1) * LANES
HALO = 136
MID = 24
RIM = (TALL - MID) // 2
VMEM = 48 * 1024 * 1024


def lane_ids(rows):
    return lax.broadcasted_iota(jnp.int32, (rows, LANES), 1)


def pieces(value, count):
    found = []
    for _ in range(count):
        part = value.astype(BF16)
        found.append(part)
        value = value - part.astype(F32)
    return found


def set_coefs(courants, coefs, rows):
    @pl.loop(0, GROUPS)
    def _(block):
        for low in rows:
            span = slice(low, low + 8)
            cx = courants[0, block, span, :]
            cy = courants[1, block, span, :]
            x_plus, x_minus = jnp.maximum(cx, 0.0), jnp.minimum(cx, 0.0)
            y_plus, y_minus = jnp.maximum(cy, 0.0), jnp.minimum(cy, 0.0)
            coefs[0, block, span, :] = 1.0 - x_plus + x_minus - y_plus + y_minus
            coefs[1, block, span, :] = x_plus
            coefs[2, block, span, :] = -x_minus
            coefs[3, block, span, :] = y_plus
            coefs[4, block, span, :] = -y_minus


def clear_sides(buffers):
    for buffer in buffers:
        nothing = jnp.zeros(buffer.shape[2:], F32)
        for member in range(LOCAL):
            for side in (0, GROUPS + 1):
                buffer[member, side] = nothing


def advance(source, target, coefs, starts):
    lane = lane_ids(8)
    first, last = lane == 0, lane == LANES - 1

    @pl.loop(0, GROUPS)
    def _(block):
        for low in starts:
            rows = slice(low, low + 8)
            k_mid, k_up, k_down, k_left, k_right = (coefs[kind, block, rows, :] for kind in range(5))
            for member in range(LOCAL):
                mid = source[member, block + 1, rows, :]
                before = source[member, block, rows, :]
                after = source[member, block + 2, rows, :]
                target[member, block + 1, rows, :] = (
                    k_mid * mid
                    + k_up * source[member, block + 1, low - 1 : low + 7, :]
                    + k_down * source[member, block + 1, low + 1 : low + 9, :]
                    + k_left * pltpu.roll(jnp.where(last, before, mid), 1, 1)
                    + k_right * pltpu.roll(jnp.where(first, after, mid), LANES - 1, 1)
                )


def send_plan():
    plan = [[] for _ in range(SLOTS)]
    for member in range(LOCAL):
        start = member * WIDE
        spans = (
            (start, start + REACH, -1),
            (start + REACH, start + REACH + LANES, 0),
            (start + REACH + LANES, start + WIDE, 1),
        )
        for low, high, offset in spans:
            while low < high:
                slot = low // LANES
                stop = min(high, (slot + 1) * LANES)
                plan[slot].append((member, offset, low - slot * LANES, stop - slot * LANES))
                low = stop
    return plan


def pack(final, pieces_of_rows, fields, rolled, send):
    @pl.loop(0, GROUPS)
    def _(block):
        for member in range(LOCAL):
            shift = (member * WIDE + REACH) % LANES
            for there, here, count in pieces_of_rows:
                value = final[member, block + 1, there : there + count, :]
                rolled[member, block + 1, here : here + count, :] = (
                    pltpu.roll(value, shift, 1) if shift else value
                )

    lane = lane_ids(MID)
    ends = jnp.where(
        lane < SPARE + 2 * REACH,
        pltpu.roll(fields[0], SPARE + REACH, 1),
        pltpu.roll(fields[1], SPARE + 3 * REACH, 1),
    )
    plan = send_plan()

    @pl.loop(0, GROUPS)
    def _(block):
        for slot in range(SLOTS):
            value = ends if slot == SLOTS - 1 else None
            for member, offset, low, high in plan[slot]:
                part = rolled[member, block + 1 + offset]
                if value is None:
                    value = part
                else:
                    value = jnp.where((lane >= low) & (lane < high), part, value)
            send[block, slot] = value


TOP = 16
HEIGHT = 56


def inner_kernel(
    members, courant_x, courant_y, cell, innov, weight,
    up, down, fields, out, send,
    old, new, courants, coefs, rolled, cells, values, member_sems, sems,
):
    own = slice(TOP, TOP + ROWS)
    small = [
        pltpu.make_async_copy(cell, cells, sems.at[0]),
        pltpu.make_async_copy(innov, values.at[0], sems.at[1]),
        pltpu.make_async_copy(weight, values.at[1], sems.at[2]),
    ]
    large, wind = [], []
    for copy in small:
        copy.start()
    for block in range(GROUPS):
        lanes = slice(block * LANES, (block + 1) * LANES)
        for kind, source in enumerate((courant_x, courant_y)):
            wind.append(
                pltpu.make_async_copy(
                    source.at[:, lanes], courants.at[kind, block, own, :],
                    sems.at[3 + 2 * block + kind],
                )
            )
        large.append(
            pltpu.make_async_copy(
                members.at[:, :, lanes], old.at[:, block + 1, own, :], member_sems.at[block]
            )
        )
    for copy in wind + large:
        copy.start()
    clear_sides((old, new, rolled))
    for copy in small:
        copy.wait()

    row_hit = lax.broadcasted_iota(jnp.int32, (ROWS, 1024), 0) == lax.shift_right_logical(cells[0], 7)
    col_hit = lax.broadcasted_iota(jnp.int32, (LANES, 1024), 0) == lax.bitwise_and(
        cells[0], LANES - 1
    )
    parts = pieces(values[1, 0] * values[0, 0], 3) + pieces(values[1, 0], 3)
    hits = row_hit.astype(F32)
    left = jnp.concatenate([(hits * part.astype(F32)).astype(BF16) for part in parts], axis=0)
    sums = lax.dot_general(
        left, col_hit.astype(F32).astype(BF16), (((1,), (1,)), ((), ())), preferred_element_type=F32
    )
    for kind in range(2):
        base = 3 * ROWS * kind
        fields[kind] = (
            sums[base : base + ROWS]
            + sums[base + ROWS : base + 2 * ROWS]
            + sums[base + 2 * ROWS : base + 3 * ROWS]
        )

    for copy in wind:
        copy.wait()
    set_coefs(courants, coefs, range(TOP, TOP + ROWS, 8))
    for copy in large:
        copy.wait()

    @pl.loop(0, GROUPS)
    def _(block):
        for field in range(LOCAL + 2):
            span = slice(field * EDGE, (field + 1) * EDGE)
            if field < LOCAL:
                up[block, span, :] = old[field, block + 1, TOP : TOP + EDGE, :]
                down[block, span, :] = old[field, block + 1, TOP + ROWS - EDGE : TOP + ROWS, :]
            else:
                kind = field - LOCAL
                up[block, span, :] = courants[kind, block, TOP : TOP + EDGE, :]
                down[block, span, :] = courants[kind, block, TOP + ROWS - EDGE : TOP + ROWS, :]

    base = (LOCAL + 2) * EDGE
    for row in range(REACH):
        for kind in range(2):
            up[row, base + kind : base + kind + 1, :] = fields[kind, row : row + 1, :]
            down[row, base + kind : base + kind + 1, :] = fields[
                kind, ROWS - REACH + row : ROWS - REACH + row + 1, :
            ]
        up[row, base + 2 : HALO, :] = jnp.zeros((HALO - base - 2, LANES), F32)
        down[row, base + 2 : HALO, :] = jnp.zeros((HALO - base - 2, LANES), F32)

    advance(old, new, coefs, range(TOP, TOP + ROWS, 8))
    advance(new, old, coefs, range(TOP, TOP + ROWS, 8))
    skip = (ROWS - MID) // 2
    advance(old, new, coefs, range(TOP + skip, TOP + skip + MID, 8))
    for member in range(LOCAL):
        for block in range(GROUPS):
            out[member, block] = new[member, block + 1, TOP + skip : TOP + skip + MID, :]
    middle = [fields[kind, skip : skip + MID, :] for kind in range(2)]
    pack(new, ((TOP + skip, 0, MID),), middle, rolled, send)


LOW = 8


def outer_kernel(
    members, courant_x, courant_y, above, below, fields,
    out, send, fields_tall,
    old, new, courants, coefs, rolled, rims, member_sems, sems,
):
    top, end = slice(TOP, TOP + 8), slice(ROWS - 8 + LOW, ROWS + LOW)
    copies = []
    for block in range(GROUPS):
        lanes = slice(block * LANES, (block + 1) * LANES)
        for part, span in enumerate((top, end)):
            rows = slice(0, 8) if part == 0 else slice(ROWS - 8, ROWS)
            copies.append(
                pltpu.make_async_copy(
                    members.at[:, rows, lanes], old.at[:, block + 1, span, :],
                    member_sems.at[part, block],
                )
            )
            for kind, source in enumerate((courant_x, courant_y)):
                copies.append(
                    pltpu.make_async_copy(
                        source.at[rows, lanes], courants.at[kind, block, span, :],
                        sems.at[kind, part, block],
                    )
                )
    for copy in copies:
        copy.start()
    clear_sides((old, new, rolled))
    base = (LOCAL + 2) * EDGE

    @pl.loop(0, GROUPS)
    def _(block):
        for field in range(LOCAL + 2):
            span = slice(field * EDGE, (field + 1) * EDGE)
            before, after = above[block, span, :], below[block, span, :]
            if field < LOCAL:
                old[field, block + 1, TOP - EDGE : TOP, :] = before
                old[field, block + 1, ROWS + LOW : ROWS + LOW + EDGE, :] = after
            else:
                courants[field - LOCAL, block, TOP - EDGE : TOP, :] = before
                courants[field - LOCAL, block, ROWS + LOW : ROWS + LOW + EDGE, :] = after

    for kind in range(2):
        for row in range(REACH):
            fields_tall[kind, row : row + 1, :] = above[row, base + kind : base + kind + 1, :]
            fields_tall[kind, REACH + ROWS + row : REACH + ROWS + row + 1, :] = below[
                row, base + kind : base + kind + 1, :
            ]
        fields_tall[kind, REACH : REACH + ROWS, :] = fields[kind]
        rims[kind, 0:RIM, :] = fields_tall[kind, 0:RIM, :]
        rims[kind, RIM:MID, :] = fields_tall[kind, TALL - RIM : TALL, :]
    for copy in copies:
        copy.wait()
    set_coefs(courants, coefs, range(0, HEIGHT, 8))
    for step in range(3):
        high, low = TOP - EDGE + 1 + step, ROWS - 6 + step + LOW
        pair = (old, new) if step % 2 == 0 else (new, old)
        advance(*pair, coefs, (high, high + 8, low, low + 8))
    keep = (ROWS - MID) // 2
    low = ROWS - keep + LOW
    for member in range(LOCAL):
        for block in range(GROUPS):
            out[member, block, 0:keep, :] = new[member, block + 1, TOP : TOP + keep, :]
            out[member, block, keep : 2 * keep, :] = new[member, block + 1, low : low + keep, :]
    pack(new, ((TOP - REACH, 0, RIM), (low, RIM, RIM)), rims, rolled, send)


DEEP = 56
MID_ROWS = ((RIM, 0, MID),)
RIM_ROWS = ((0, 0, RIM), (TALL - RIM, RIM, RIM))


def member_place(member):
    return member * WIDE // LANES, member * WIDE % LANES


def folded(slots, lane):
    near, far = None, None
    for member in range(LOCAL):
        base, shift = member_place(member)
        here, there = slots(base), slots(base + 1)
        if shift:
            here = pltpu.roll(jnp.where(lane >= shift, here, there), LANES - shift, 1)
            there = pltpu.roll(there, LANES - shift, 1)
        near = here if near is None else near + here
        far = there if far is None else far + there
    return near, far


def spread_out(near, far, lane, store):
    slots = [None] * SLOTS
    for member in range(LOCAL):
        base, shift = member_place(member)
        moved = pltpu.roll(near, shift, 1) if shift else near
        tail = pltpu.roll(far, shift, 1) if shift else far
        slots[base] = moved if slots[base] is None else jnp.where(lane >= shift, moved, slots[base])
        slots[base + 1] = jnp.where(
            lane < shift, moved, jnp.where(lane < shift + 2 * REACH, tail, 0.0)
        )
    for slot in range(SLOTS):
        store(slot, slots[slot])


def shifted_copies(copies, slots, low, rows):
    lane = lane_ids(rows)

    for slot in range(slots):
        mid = copies[RADIUS, slot, low : low + rows, :]
        after = copies[RADIUS, min(slot + 1, SLOTS - 1), low : low + rows, :]
        before = copies[RADIUS, max(slot - 1, 0), low : low + rows, :]
        for shift in (1, 2):
            copies[RADIUS + shift, slot, low : low + rows, :] = pltpu.roll(
                jnp.where(lane < shift, after, mid), LANES - shift, 1
            )
            copies[RADIUS - shift, slot, low : low + rows, :] = pltpu.roll(
                jnp.where(lane >= LANES - shift, before, mid), shift, 1
            )


def analysis_kernel(
    place, offsets, weights, got_mid, got_rim, fields, increment, spread_copies,
    spread, averages, gains, inside, products, localized, total, plane, ends,
):
    tile, block = place[0], place[1]
    lane = lane_ids(TALL)
    entries = offsets.shape[0]
    tap_row = [offsets[entry, 0] for entry in range(entries)]
    tap_col = [offsets[entry, 1] for entry in range(entries)]
    tap = [weights[entry] for entry in range(entries)]
    weight_sum = tap[0]
    for entry in range(1, entries):
        weight_sum = weight_sum + tap[entry]
    scale = 1.0 / jnp.full((1, LANES), weight_sum, F32)
    scale = scale * scale

    @pl.loop(0, SLOTS)
    def _(slot):
        for got, parts in ((got_mid, MID_ROWS), (got_rim, RIM_ROWS)):
            value = got[0, slot]
            for source in range(1, GROUPS):
                value = value + got[source, slot]
            for here, there, count in parts:
                averages[slot, here : here + count, :] = value[there : there + count]

    near, far = folded(lambda slot: averages[slot], lane)
    count = GROUPS * LOCAL

    def store_average(slot, value):
        averages[slot] = value

    spread_out(near / count, far / count, lane, store_average)
    deviation = 1.0 / math.sqrt(count - 1)

    @pl.loop(0, SLOTS)
    def _(slot):
        for got, parts in ((got_mid, MID_ROWS), (got_rim, RIM_ROWS)):
            for here, there, count in parts:
                average = averages[slot, here : here + count, :]
                for source in range(GROUPS):
                    value = got[source, slot, there : there + count, :]
                    spread[source, slot, here : here + count, :] = (value - average) * deviation

    row = lax.broadcasted_iota(jnp.int32, (TALL, LANES), 0) + (tile * ROWS - REACH)
    col = lane + (block * LANES - REACH)
    row_ok = (row >= 0) & (row < ROWS * 32)
    near_ok = row_ok & (col >= 0) & (col < COLS)
    far_ok = row_ok & (col + LANES < COLS)

    def store_inside(slot, value):
        inside[slot, 0:TALL, :] = value
        inside[slot, TALL:DEEP, :] = jnp.zeros((DEEP - TALL, LANES), F32)

    spread_out(near_ok.astype(F32), far_ok.astype(F32), lane, store_inside)

    for got, parts in ((got_mid, MID_ROWS), (got_rim, RIM_ROWS)):
        for here, there, count in parts:
            rows = slice(there, there + count)
            ends[0, here : here + count, :] = got[jnp.maximum(block - 1, 0), SLOTS - 1, rows, :]
            ends[1, here : here + count, :] = got[
                jnp.minimum(block + 1, GROUPS - 1), SLOTS - 1, rows, :
            ]
    left_ends = jnp.where(block > 0, ends[0], 0.0)
    right_ends = jnp.where(block < GROUPS - 1, ends[1], 0.0)
    planes = []
    for kind in range(2):
        back = LANES - SPARE - 2 * REACH * kind
        own = pltpu.roll(fields[kind], REACH, 1)
        near = jnp.where(lane < REACH, pltpu.roll(left_ends, back, 1), own)
        far = jnp.where(lane < REACH, own, pltpu.roll(right_ends, back, 1))
        far = jnp.where(lane < 2 * REACH, far, 0.0)
        planes.append((near, far))

    def store_gain(slot, value):
        gains[slot] = value

    def sweep(slots, multiplier, y_rows, z_low, z_rows, x_low, x_rows, finish):
        @pl.loop(0, slots)
        def _(slot):
            products[RADIUS, slot, 0:TALL, :] = multiplier(slot)

        shifted_copies(products, slots, z_low - RADIUS, y_rows)

        @pl.loop(0, slots)
        def _(slot):
            value = None
            for entry in range(entries):
                term = tap[entry] * products[
                    RADIUS - tap_col[entry], slot, pl.ds(z_low - tap_row[entry], z_rows), :
                ]
                value = term if value is None else value + term
            rows = slice(z_low, z_low + z_rows)
            localized[RADIUS, slot, rows, :] = value * inside[slot, rows, :]

        shifted_copies(localized, slots, z_low, z_rows)

        @pl.loop(0, slots)
        def _(slot):
            value = None
            for entry in range(entries):
                term = tap[entry] * localized[
                    RADIUS + tap_col[entry], slot, pl.ds(x_low + tap_row[entry], x_rows), :
                ]
                value = term if value is None else value + term
            finish(slot, value)

    def apply(near, far, y_rows, z_low, z_rows, x_low, x_rows):
        spread_out(near, far, lane, store_gain)
        ones = []

        def finish_ones(slot, value):
            plane[slot, 0:x_rows, :] = value

        sweep(2, lambda slot: gains[slot], y_rows, z_low, z_rows, x_low, x_rows, finish_ones)

        @pl.loop(0, SLOTS)
        def _(slot):
            total[slot, 0:x_rows, :] = jnp.zeros((x_rows, LANES), F32)

        @pl.loop(0, GROUPS)
        def _(source):
            def finish(slot, value):
                total[slot, 0:x_rows, :] += value * spread[source, slot, x_low : x_low + x_rows, :]

            sweep(
                SLOTS, lambda slot: gains[slot] * spread[source, slot],
                y_rows, z_low, z_rows, x_low, x_rows, finish,
            )

        near, far = folded(lambda slot: total[slot, 0:x_rows, :], lane_ids(x_rows))
        return (near + plane[0, 0:x_rows, :]) * scale, (far + plane[1, 0:x_rows, :]) * scale

    for slot in range(SLOTS):
        for kind in range(2 * RADIUS + 1):
            products[kind, slot, TALL:DEEP, :] = jnp.zeros((DEEP - TALL, LANES), F32)
        localized[RADIUS, slot] = jnp.zeros((DEEP, LANES), F32)

    (near_v, far_v), (near_w, far_w) = planes
    near, far = apply(near_v, far_v, 48, 2, 48, 4, 40)
    for part, value in enumerate((near, far)):
        plane[2 + part, 0:TALL, :] = jnp.zeros((TALL, LANES), F32)
        plane[2 + part, 4:44, :] = value
    near = (STEP_SIZE * near_w) * plane[2, 0:TALL, :] - (2.0 - STEP_SIZE) * near_v
    far = (STEP_SIZE * far_w) * plane[3, 0:TALL, :] - (2.0 - STEP_SIZE) * far_v
    far = jnp.where(lane < 2 * REACH, far, 0.0)
    near, far = apply(near, far, 40, 6, 40, 8, 32)
    short_lane = lane_ids(ROWS)
    result = pltpu.roll(jnp.where(short_lane < REACH, far, near), LANES - REACH, 1) * -STEP_SIZE
    increment[...] = result
    for target in range(GROUPS):
        spread_copies[target] = result


def recentre_kernel(middle, rim, increments, out):
    keep = (ROWS - MID) // 2
    for block in range(GROUPS):
        lanes = slice(block * LANES, (block + 1) * LANES)
        for member in range(LOCAL):
            out[member, 0:keep, lanes] = rim[member, block, 0:keep, :] + increments[block, 0:keep, :]
            out[member, keep : keep + MID, lanes] = (
                middle[member, block] + increments[block, keep : keep + MID, :]
            )
            out[member, keep + MID : ROWS, lanes] = (
                rim[member, block, keep : 2 * keep, :] + increments[block, keep + MID : ROWS, :]
            )


def on_vmem(count):
    return [pl.BlockSpec(memory_space=pltpu.VMEM)] * count


def in_hbm(count):
    return [pl.BlockSpec(memory_space=pltpu.HBM)] * count


def array(*shape):
    return jax.ShapeDtypeStruct(shape, F32)


def on_device(
    members, courant_x, courant_y, obs_cell, innovation, obs_weight, stencil_offsets, stencil_weights
):
    both = ("member", "grp")
    params = pltpu.CompilerParams(vmem_limit_bytes=VMEM)
    tiles = lax.axis_size("tile")
    keep = (ROWS - MID) // 2
    buffers = [
        pltpu.VMEM((LOCAL, GROUPS + 2, HEIGHT, LANES), F32),
        pltpu.VMEM((LOCAL, GROUPS + 2, HEIGHT, LANES), F32),
        pltpu.VMEM((2, GROUPS, HEIGHT, LANES), F32),
        pltpu.VMEM((5, GROUPS, HEIGHT, LANES), F32),
        pltpu.VMEM((LOCAL, GROUPS + 2, MID, LANES), F32),
    ]
    up, down, fields, middle, send_mid = pl.pallas_call(
        inner_kernel,
        out_shape=[
            array(GROUPS, HALO, LANES),
            array(GROUPS, HALO, LANES),
            array(2, ROWS, LANES),
            array(LOCAL, GROUPS, MID, LANES),
            array(GROUPS, SLOTS, MID, LANES),
        ],
        in_specs=in_hbm(6),
        out_specs=on_vmem(5),
        scratch_shapes=buffers
        + [
            pltpu.VMEM((1, 1, 1024), jnp.int32),
            pltpu.VMEM((2, 1, 1, 1024), F32),
            pltpu.SemaphoreType.DMA((GROUPS,)),
            pltpu.SemaphoreType.DMA((3 + 2 * GROUPS,)),
        ],
        compiler_params=params,
        name="inner",
    )(members, courant_x, courant_y, obs_cell, innovation, obs_weight)
    got_mid = exchanged(send_mid, both)
    above = lax.ppermute(down, "tile", [(i, i + 1) for i in range(tiles - 1)])
    below = lax.ppermute(up, "tile", [(i + 1, i) for i in range(tiles - 1)])
    rim, send_rim, fields_tall = pl.pallas_call(
        outer_kernel,
        out_shape=[
            array(LOCAL, GROUPS, 2 * keep, LANES),
            array(GROUPS, SLOTS, MID, LANES),
            array(2, TALL, LANES),
        ],
        in_specs=in_hbm(3) + on_vmem(3),
        out_specs=on_vmem(3),
        scratch_shapes=buffers
        + [
            pltpu.VMEM((2, MID, LANES), F32),
            pltpu.SemaphoreType.DMA((2, GROUPS)),
            pltpu.SemaphoreType.DMA((2, 2, GROUPS)),
        ],
        compiler_params=params,
        name="outer",
    )(members, courant_x, courant_y, above, below, fields)
    got_rim = exchanged(send_rim, both)
    place = jnp.stack([lax.axis_index("tile"), lax.axis_index(both)]).astype(jnp.int32)
    increment, copies = pl.pallas_call(
        analysis_kernel,
        out_shape=[array(ROWS, LANES), array(GROUPS, ROWS, LANES)],
        in_specs=[pl.BlockSpec(memory_space=pltpu.SMEM)] * 3 + on_vmem(3),
        out_specs=on_vmem(2),
        scratch_shapes=[
            pltpu.VMEM((GROUPS, SLOTS, TALL, LANES), F32),
            pltpu.VMEM((SLOTS, TALL, LANES), F32),
            pltpu.VMEM((SLOTS, TALL, LANES), F32),
            pltpu.VMEM((SLOTS, DEEP, LANES), F32),
            pltpu.VMEM((2 * RADIUS + 1, SLOTS, DEEP, LANES), F32),
            pltpu.VMEM((2 * RADIUS + 1, SLOTS, DEEP, LANES), F32),
            pltpu.VMEM((SLOTS, TALL, LANES), F32),
            pltpu.VMEM((4, TALL, LANES), F32),
            pltpu.VMEM((2, TALL, LANES), F32),
        ],
        compiler_params=params,
        name="analysis",
    )(place, stencil_offsets, stencil_weights, got_mid, got_rim, fields_tall)
    increments = lax.all_to_all(copies, both, 0, 0, tiled=True)
    analysis = pl.pallas_call(
        recentre_kernel,
        out_shape=array(*members.shape),
        in_specs=on_vmem(3),
        out_specs=pl.BlockSpec(memory_space=pltpu.VMEM),
        compiler_params=params,
        name="recentre",
    )(middle, rim, increments)
    return analysis, increment


def exchanged(blocks, axes):
    flat = blocks.reshape(GROUPS, -1, LANES)
    return lax.all_to_all(flat, axes, 0, 0, tiled=True).reshape(blocks.shape)


def solution(mesh):
    both = ("member", "grp")
    placed = (
        P(both, "tile", None),
        P("tile", None),
        P("tile", None),
        P("tile", both, None),
        P("tile", both, None),
        P("tile", both, None),
        P(),
        P(),
    )
    return jax.shard_map(
        on_device,
        mesh=mesh,
        in_specs=placed,
        out_specs=(P(both, "tile", None), P("tile", both)),
        check_vma=False,
    )
```

time: 140 us -> 105 us (0.75)
  Pallas kernels: 69 us -> 38.7 us
  waiting for transfers between devices: 38.9 us -> 20.9 us
  starting transfers between devices: 14.9 us -> 23.2 us
  local copies, waits for them, and re-layouts: 6.34 us -> 11.5 us
    pallas_call x4, Pallas kernels: 69 us -> 38.7 us  [the longest x1 25.7 us: on_device(): pl.pallas_call(analysis_kernel, out_shape=[array(ROWS, LANES), array(GROU...]
    all_to_all x1 -> x2, waiting for transfers between devices: 31.9 us -> 12 us  [exchanged(): return lax.all_to_all(flat, axes, 0, 0, tiled=True).reshape(blocks.shape)]
    all_to_all x1 -> x2, starting transfers between devices: 5.77 us -> 14 us  [exchanged(): return lax.all_to_all(flat, axes, 0, 0, tiled=True).reshape(blocks.shape)]
    unnamed x21 -> x35, local copies, waits for them, and re-layouts: 6.34 us -> 11.5 us
    ppermute x1, waiting for transfers between devices: 5.27 us -> 8.68 us  [on_device(): above = lax.ppermute(down, 'tile', [(i, i + 1) for i in range(tiles - 1)])]
    ppermute x1, waiting for transfers between devices: 1.76 us -> 0.17 us  [on_device(): below = lax.ppermute(up, 'tile', [(i + 1, i) for i in range(tiles - 1)])]
  transfers between devices with their start and end apart: 3 -> 4, of which waited for: 3 -> 3; matrix products, arithmetic and copies ran while one was open for 0% -> 0% of each run, Pallas kernels for 0% -> 6%
where the time goes in v1:
time: 105 us; the launch traced here: 104 us
  Pallas kernels  38.7 us (37%)
  starting transfers between devices  23.2 us (22%)
  waiting for transfers between devices  20.9 us (20%)
  local copies, waits for them, and re-layouts  11.5 us (11%)
  blocking collectives  8.93 us (9%)
    pallas_call x1, Pallas kernels, on_device(): pl.pallas_call(analysis_kernel, out_shape=[array(ROWS, LANES), array(GROU...  25.7 us
    all_to_all x2, starting transfers between devices, exchanged(): return lax.all_to_all(flat, axes, 0, 0, tiled=True).reshape(blocks.shape)  14 us
    all_to_all x2, waiting for transfers between devices, exchanged(): return lax.all_to_all(flat, axes, 0, 0, tiled=True).reshape(blocks.shape)  12 us
    unnamed x35, local copies, waits for them, and re-layouts  11.5 us
    all_to_all x1, blocking collectives, on_device(): increments = lax.all_to_all(copies, both, 0, 0, tiled=True)  8.93 us
    ppermute x1, waiting for transfers between devices, on_device(): above = lax.ppermute(down, 'tile', [(i, i + 1) for i in range(tiles - 1)])  8.68 us
    ppermute x1, starting transfers between devices, on_device(): below = lax.ppermute(up, 'tile', [(i + 1, i) for i in range(tiles - 1)])  7.26 us
    pallas_call x1, Pallas kernels, on_device(): pl.pallas_call(outer_kernel, out_shape=[array(LOCAL, GROUPS, 2 * keep, LA...  5.98 us
  transfers between devices with their start and end apart: 4, of which 3 were waited for; matrix products, arithmetic and copies ran while one was open for 0% of the time, Pallas kernels for 6%

profile of v1, /device:TPU:16, one launch (start us, length us, event | category | flops | bytes accessed | tf_op | source)
XLA Modules:
  0.0 103.9 jit_solution(8265601488225918215)
XLA Ops:
  0.6 0.0 copy-start
  0.6 1.3 %copy-done = f32[10,32,1024]{2,1,0:T(8,128)S(1)} copy-done((f32[10,32,1024]{2,1,0:T(8,128)S(1)}, f32[10,32,1024]{2,1,0:T(8,128)}, u32[]{:S(2)}) %copy-start) | copy-done | bytes 1310744
  1.9 0.0 copy-start.4
  2.0 0.9 copy-done.4
  2.9 0.0 copy-start.6
  2.9 0.9 copy-done.6
  3.8 0.0 copy-start.10
  3.8 0.7 copy-done.10
  4.4 0.0 copy-start.11
  4.4 0.7 copy-done.11
  5.1 0.0 copy-start.12
  5.1 0.7 copy-done.12
  5.8 5.7 %inner.1 = (f32[8,136,128]{2,1,0:T(8,128)S(1)}, f32[8,136,128]{2,1,0:T(8,128)S(1)}, f32[2,32,128]{2,1,0:T(8,128)S(1)}, f32[10,8,24,128]{3,2,1,0:T(8,128)S(1)}, f32[8,12,24,128]{3,2,1,0:T(8,128)S(1)}) custom-call(f32[10,32,1024]{2,1,0:T(8,128)S(1)} %copy-done, f32[32,1024]{1,0:T(8,128)S(1)} %copy-done.4, f32[32,1024]{1,0:T(8,128)S(1)} %copy-done.6, ...), custom_call_target="tpu_custom_call" | custom-call | tf_op jit(solution)/shard_map/inner/pallas_call | solution.py:549
  11.5 0.0 copy-start.3
  11.6 1.0 copy-done.3
  12.6 0.0 copy-start.14
  12.6 0.8 copy-done.14
  13.4 0.0 copy-start.15
  13.4 0.8 copy-done.15
  14.2 0.0 copy-start.1
  14.2 5.1 %all-to-all-start = ((f32[8,288,128]{2,1,0:T(8,128)}), f32[8,288,128]{2,1,0:T(8,128)S(1)}, u32[]{:S(2)}, u32[]{:S(2)}) async-start(f32[8,288,128]{2,1,0:T(8,128)} %bitcast.9), calls=%async_computation | async-start | bytes 2359296 | tf_op jit(solution)/shard_map/all_to_all | solution.py:626
  19.4 1.9 %collective-permute-start = (f32[8,136,128]{2,1,0:T(8,128)}, f32[8,136,128]{2,1,0:T(8,128)S(1)}, u32[]{:S(2)}, u32[]{:S(2)}) collective-permute-start(f32[8,136,128]{2,1,0:T(8,128)} %copy-done.15), channel_id=1, source_target_pairs={{0,2},{2,4},{4,6},{6,8},{8,10},{10,12},{12,14},{14,16},{16,18},{18... | collective-permute-start | bytes 1671176 | tf_op jit(solution)/shard_map/ppermute | solution.py:571
  21.3 7.3 %collective-permute-start.1 = (f32[8,136,128]{2,1,0:T(8,128)}, f32[8,136,128]{2,1,0:T(8,128)S(1)}, u32[]{:S(2)}, u32[]{:S(2)}) collective-permute-start(f32[8,136,128]{2,1,0:T(8,128)} %copy-done.14), channel_id=1, source_target_pairs={{2,0},{4,2},{6,4},{8,6},{10,8},{12,10},{14,12},{16,14},{18,16},{20... | collective-permute-start | bytes 1671176 | tf_op jit(solution)/shard_map/ppermute | solution.py:572
  28.5 8.7 %collective-permute-done.above = f32[8,136,128]{2,1,0:T(8,128)S(1)} collective-permute-done((f32[8,136,128]{2,1,0:T(8,128)}, f32[8,136,128]{2,1,0:T(8,128)S(1)}, u32[]{:S(2)}, u32[]{:S(2)}) %collective-permute-start) | collective-permute-done | bytes 557088 | tf_op jit(solution)/shard_map/ppermute | solution.py:571
  37.2 0.2 collective-permute-done.1.below
  37.4 0.0 copy-done.1
  37.4 0.0 copy-start.5
  37.4 0.9 copy-done.5
  38.3 0.0 copy-start.7
  38.3 0.9 copy-done.7
  39.2 6.0 %outer.1 = (f32[10,8,8,128]{3,2,1,0:T(8,128)S(1)}, f32[8,12,24,128]{3,2,1,0:T(8,128)S(1)}, f32[2,48,128]{2,1,0:T(8,128)S(1)}) custom-call(f32[10,32,1024]{2,1,0:T(8,128)S(1)} %copy-done.1, f32[32,1024]{1,0:T(8,128)S(1)} %copy-done.5, f32[32,1024]{1,0:T(8,128)S(1)} %copy-done.7, f32[8,136,128]{2,1,0:T(8,128)S(1)} %collective-permute-done.above, ...), custom_call_target="tpu_custom_call" | custom-call | tf_op jit(solution)/shard_map/outer/pallas_call | solution.py:573
  45.2 0.0 copy-start.2
  45.2 1.0 copy-done.2
  46.2 0.0 copy-start.8
  46.2 0.7 copy-done.8
  46.9 0.0 all-to-all-done
  46.9 0.0 copy-start.16
  46.9 0.0 copy-start.13
  47.0 8.8 %all-to-all-start.1 = ((f32[8,288,128]{2,1,0:T(8,128)}), f32[8,288,128]{2,1,0:T(8,128)S(1)}, u32[]{:S(2)}, u32[]{:S(2)}) async-start(f32[8,288,128]{2,1,0:T(8,128)} %bitcast.8), calls=%async_computation.1 | async-start | bytes 2359296 | tf_op jit(solution)/shard_map/all_to_all | solution.py:626
  55.8 0.0 copy-done.16
  55.8 0.1 copy.10.offsets
  55.9 0.1 pad_add_fusion.place
  56.0 12.0 %all-to-all-done.1 = f32[8,288,128]{2,1,0:T(8,128)S(1)} async-done(((f32[8,288,128]{2,1,0:T(8,128)}), f32[8,288,128]{2,1,0:T(8,128)S(1)}, u32[]{:S(2)}, u32[]{:S(2)}) %all-to-all-start.1) | async-done | bytes 1179680 | tf_op jit(solution)/shard_map/all_to_all | solution.py:626
  68.0 0.0 copy-done.13
  68.0 25.7 %analysis.1 = (f32[32,128]{1,0:T(8,128)}, f32[8,32,128]{2,1,0:T(8,128)S(1)}) custom-call(s32[2]{0:T(128)S(1)} %pad_add_fusion.place, s32[9,2]{1,0:T(8,128)S(1)} %copy.10.offsets, f32[9]{0:T(128)S(1)} %copy-done.13, f32[8,12,24,128]{3,2,1,0:T(8,128)S(1)} %bitcast.6, f32[8,12,24,128]{3,2,1,0:T(8,128)S(1)} %bitcast.7, f32[2,48,128]{2,1,0:T(8,128)S(1)} %get-tuple-element.19.fields), custom_call_target="tpu_custom_call" | custom-call | tf_op jit(solution)/shard_map/analysis/pallas_call | solution.py:593
  93.7 8.9 %all_to_all.15.increments = f32[8,32,128]{2,1,0:T(8,128)S(1)} all-to-all(f32[8,32,128]{2,1,0:T(8,128)S(1)} %get-tuple-element.20), channel_id=1, replica_groups=mesh['member'=4,'tile'=32,'grp'=2] {'member','grp'}, dimensions={0} | all-to-all | bytes 262144 | tf_op jit(solution)/shard_map/all_to_all | solution.py:612
  102.6 0.0 copy-done.9
  102.7 1.3 %recentre.1 = f32[10,32,1024]{2,1,0:T(8,128)} custom-call(f32[10,8,24,128]{3,2,1,0:T(8,128)S(1)} %get-tuple-element.12.middle, f32[10,8,8,128]{3,2,1,0:T(8,128)S(1)} %copy-done.9, f32[8,32,128]{2,1,0:T(8,128)S(1)} %all_to_all.15.increments), custom_call_target="tpu_custom_call" | custom-call | tf_op jit(solution)/shard_map/recentre/pallas_call | solution.py:613
  (1 shorter events, 0.0 us)
Async XLA Ops:
  0.6 1.3 %copy-start = (f32[10,32,1024]{2,1,0:T(8,128)S(1)}, f32[10,32,1024]{2,1,0:T(8,128)}, u32[]{:S(2)}) copy-start(f32[10,32,1024]{2,1,0:T(8,128)} %members.3) | copy-start | bytes 3932164
  1.9 0.9 copy-start.4
  2.9 0.9 copy-start.6
  3.8 0.7 copy-start.10
  4.4 0.7 copy-start.11
  5.1 0.7 copy-start.12
  11.5 1.0 copy-start.3
  12.6 0.8 copy-start.14
  13.4 0.8 copy-start.15
  14.2 23.2 %copy-start.1 = (f32[10,32,1024]{2,1,0:T(8,128)S(1)}, f32[10,32,1024]{2,1,0:T(8,128)}, u32[]{:S(2)}) copy-start(f32[10,32,1024]{2,1,0:T(8,128)} %members.3) | copy-start | bytes 3932164
  14.2 32.7 %all-to-all-start = ((f32[8,288,128]{2,1,0:T(8,128)}), f32[8,288,128]{2,1,0:T(8,128)S(1)}, u32[]{:S(2)}, u32[]{:S(2)}) async-start(f32[8,288,128]{2,1,0:T(8,128)} %bitcast.9), calls=%async_computation | async-start | bytes 2359296 | tf_op jit(solution)/shard_map/all_to_all | solution.py:626
  19.4 17.9 %collective-permute-start = (f32[8,136,128]{2,1,0:T(8,128)}, f32[8,136,128]{2,1,0:T(8,128)S(1)}, u32[]{:S(2)}, u32[]{:S(2)}) collective-permute-start(f32[8,136,128]{2,1,0:T(8,128)} %copy-done.15), channel_id=1, source_target_pairs={{0,2},{2,4},{4,6},{6,8},{8,10},{10,12},{12,14},{14,16},{16,18},{18... | collective-permute-start | bytes 1671176 | tf_op jit(solution)/shard_map/ppermute | solution.py:571
  21.3 16.1 %collective-permute-start.1 = (f32[8,136,128]{2,1,0:T(8,128)}, f32[8,136,128]{2,1,0:T(8,128)S(1)}, u32[]{:S(2)}, u32[]{:S(2)}) collective-permute-start(f32[8,136,128]{2,1,0:T(8,128)} %copy-done.14), channel_id=1, source_target_pairs={{2,0},{4,2},{6,4},{8,6},{10,8},{12,10},{14,12},{16,14},{18,16},{20... | collective-permute-start | bytes 1671176 | tf_op jit(solution)/shard_map/ppermute | solution.py:572
  37.4 0.9 copy-start.5
  38.3 0.9 copy-start.7
  45.2 1.0 %copy-start.2 = (f32[8,12,24,128]{3,2,1,0:T(8,128)}, f32[8,12,24,128]{3,2,1,0:T(8,128)S(1)}, u32[]{:S(2)}) copy-start(f32[8,12,24,128]{3,2,1,0:T(8,128)S(1)} %get-tuple-element.18) | copy-start | bytes 3538948
  46.2 0.7 copy-start.8
  46.9 8.9 %copy-start.16 = (s32[9,2]{0,1:T(2,128)S(1)}, s32[9,2]{0,1:T(2,128)}, u32[]{:S(2)}) copy-start(s32[9,2]{0,1:T(2,128)} %param.14) | copy-start | bytes 220
  46.9 21.1 %copy-start.13 = (f32[9]{0:T(128)S(1)}, f32[9]{0:T(128)}, u32[]{:S(2)}) copy-start(f32[9]{0:T(128)} %weights.1) | copy-start | bytes 112
  47.0 21.0 %all-to-all-start.1 = ((f32[8,288,128]{2,1,0:T(8,128)}), f32[8,288,128]{2,1,0:T(8,128)S(1)}, u32[]{:S(2)}, u32[]{:S(2)}) async-start(f32[8,288,128]{2,1,0:T(8,128)} %bitcast.8), calls=%async_computation.1 | async-start | bytes 2359296 | tf_op jit(solution)/shard_map/all_to_all | solution.py:626
  68.0 34.6 %copy-start.9 = (f32[10,8,8,128]{3,2,1,0:T(8,128)S(1)}, f32[10,8,8,128]{3,2,1,0:T(8,128)}, u32[]{:S(2)}) copy-start(f32[10,8,8,128]{3,2,1,0:T(8,128)} %copy-done.8) | copy-start | bytes 983044

commit v2 on v1

--- a/solution.py
+++ b/solution.py
@@ -26,6 +26,7 @@
 MID = 24
 RIM = (TALL - MID) // 2
 VMEM = 48 * 1024 * 1024
+ALL_VMEM = 60 * 1024 * 1024
 
 
 def lane_ids(rows):
@@ -65,20 +66,21 @@
                 buffer[member, side] = nothing
 
 
-def advance(source, target, coefs, starts):
+def advance(source, target, coefs, starts, homes=None):
+    homes = starts if homes is None else homes
     lane = lane_ids(8)
     first, last = lane == 0, lane == LANES - 1
 
     @pl.loop(0, GROUPS)
     def _(block):
-        for low in starts:
+        for low, home in zip(starts, homes):
             rows = slice(low, low + 8)
             k_mid, k_up, k_down, k_left, k_right = (coefs[kind, block, rows, :] for kind in range(5))
             for member in range(LOCAL):
                 mid = source[member, block + 1, rows, :]
                 before = source[member, block, rows, :]
                 after = source[member, block + 2, rows, :]
-                target[member, block + 1, rows, :] = (
+                target[member, block + 1, home : home + 8, :] = (
                     k_mid * mid
                     + k_up * source[member, block + 1, low - 1 : low + 7, :]
                     + k_down * source[member, block + 1, low + 1 : low + 9, :]
@@ -105,16 +107,13 @@
     return plan
 
 
-def pack(final, pieces_of_rows, fields, rolled, send):
+def pack(final, fields, rolled, blocks, send, sems):
     @pl.loop(0, GROUPS)
     def _(block):
         for member in range(LOCAL):
             shift = (member * WIDE + REACH) % LANES
-            for there, here, count in pieces_of_rows:
-                value = final[member, block + 1, there : there + count, :]
-                rolled[member, block + 1, here : here + count, :] = (
-                    pltpu.roll(value, shift, 1) if shift else value
-                )
+            value = final[member, block + 1, 0:MID, :]
+            rolled[member, block + 1] = pltpu.roll(value, shift, 1) if shift else value
 
     lane = lane_ids(MID)
     ends = jnp.where(
@@ -134,44 +133,31 @@
                     value = part
                 else:
                     value = jnp.where((lane >= low) & (lane < high), part, value)
-            send[block, slot] = value
-
-
-TOP = 16
-HEIGHT = 56
-
-
-def inner_kernel(
+            blocks[block, slot] = value
+        pltpu.make_async_copy(blocks.at[block], send.at[block], sems.at[block]).start()
+
+
+def finish_pack(blocks, send, sems):
+    for block in range(GROUPS):
+        pltpu.make_async_copy(blocks.at[block], send.at[block], sems.at[block]).wait()
+
+
+def message_kernel(
     members, courant_x, courant_y, cell, innov, weight,
-    up, down, fields, out, send,
-    old, new, courants, coefs, rolled, cells, values, member_sems, sems,
+    up, down, fields, own, courants, cells, values, member_sems, sems,
 ):
-    own = slice(TOP, TOP + ROWS)
     small = [
         pltpu.make_async_copy(cell, cells, sems.at[0]),
         pltpu.make_async_copy(innov, values.at[0], sems.at[1]),
         pltpu.make_async_copy(weight, values.at[1], sems.at[2]),
     ]
-    large, wind = [], []
-    for copy in small:
+    large = [
+        pltpu.make_async_copy(members, own, member_sems.at[0]),
+        pltpu.make_async_copy(courant_x, courants.at[0], member_sems.at[1]),
+        pltpu.make_async_copy(courant_y, courants.at[1], member_sems.at[2]),
+    ]
+    for copy in small + large:
         copy.start()
-    for block in range(GROUPS):
-        lanes = slice(block * LANES, (block + 1) * LANES)
-        for kind, source in enumerate((courant_x, courant_y)):
-            wind.append(
-                pltpu.make_async_copy(
-                    source.at[:, lanes], courants.at[kind, block, own, :],
-                    sems.at[3 + 2 * block + kind],
-                )
-            )
-        large.append(
-            pltpu.make_async_copy(
-                members.at[:, :, lanes], old.at[:, block + 1, own, :], member_sems.at[block]
-            )
-        )
-    for copy in wind + large:
-        copy.start()
-    clear_sides((old, new, rolled))
     for copy in small:
         copy.wait()
 
@@ -192,25 +178,6 @@
             + sums[base + ROWS : base + 2 * ROWS]
             + sums[base + 2 * ROWS : base + 3 * ROWS]
         )
-
-    for copy in wind:
-        copy.wait()
-    set_coefs(courants, coefs, range(TOP, TOP + ROWS, 8))
-    for copy in large:
-        copy.wait()
-
-    @pl.loop(0, GROUPS)
-    def _(block):
-        for field in range(LOCAL + 2):
-            span = slice(field * EDGE, (field + 1) * EDGE)
-            if field < LOCAL:
-                up[block, span, :] = old[field, block + 1, TOP : TOP + EDGE, :]
-                down[block, span, :] = old[field, block + 1, TOP + ROWS - EDGE : TOP + ROWS, :]
-            else:
-                kind = field - LOCAL
-                up[block, span, :] = courants[kind, block, TOP : TOP + EDGE, :]
-                down[block, span, :] = courants[kind, block, TOP + ROWS - EDGE : TOP + ROWS, :]
-
     base = (LOCAL + 2) * EDGE
     for row in range(REACH):
         for kind in range(2):
@@ -220,16 +187,59 @@
             ]
         up[row, base + 2 : HALO, :] = jnp.zeros((HALO - base - 2, LANES), F32)
         down[row, base + 2 : HALO, :] = jnp.zeros((HALO - base - 2, LANES), F32)
-
+    for copy in large:
+        copy.wait()
+    for field in range(LOCAL + 2):
+        span = slice(field * EDGE, (field + 1) * EDGE)
+        source = own.at[field] if field < LOCAL else courants.at[field - LOCAL]
+        first, last = source[0:EDGE, :], source[ROWS - EDGE : ROWS, :]
+        for block in range(GROUPS):
+            lanes = slice(block * LANES, (block + 1) * LANES)
+            up[block, span, :] = first[:, lanes]
+            down[block, span, :] = last[:, lanes]
+
+
+TOP = 16
+HEIGHT = 56
+
+
+def inner_kernel(
+    members, courant_x, courant_y, fields, out, send,
+    old, new, courants, coefs, rolled, final, blocks, member_sems, wind_sems, sems,
+):
+    own = slice(TOP, TOP + ROWS)
+    large, wind = [], []
+    for block in range(GROUPS):
+        lanes = slice(block * LANES, (block + 1) * LANES)
+        for kind, source in enumerate((courant_x, courant_y)):
+            wind.append(
+                pltpu.make_async_copy(
+                    source.at[:, lanes], courants.at[kind, block, own, :], wind_sems.at[kind, block]
+                )
+            )
+        large.append(
+            pltpu.make_async_copy(
+                members.at[:, :, lanes], old.at[:, block + 1, own, :], member_sems.at[block]
+            )
+        )
+    for copy in wind + large:
+        copy.start()
+    clear_sides((old, new, rolled))
+    for copy in wind:
+        copy.wait()
+    set_coefs(courants, coefs, range(TOP, TOP + ROWS, 8))
+    for copy in large:
+        copy.wait()
     advance(old, new, coefs, range(TOP, TOP + ROWS, 8))
     advance(new, old, coefs, range(TOP, TOP + ROWS, 8))
     skip = (ROWS - MID) // 2
-    advance(old, new, coefs, range(TOP + skip, TOP + skip + MID, 8))
-    for member in range(LOCAL):
-        for block in range(GROUPS):
-            out[member, block] = new[member, block + 1, TOP + skip : TOP + skip + MID, :]
+    advance(old, final, coefs, range(TOP + skip, TOP + skip + MID, 8), range(0, MID, 8))
+    whole = pltpu.make_async_copy(final.at[:, pl.ds(1, GROUPS), pl.ds(0, MID), :], out, sems.at[GROUPS])
+    whole.start()
     middle = [fields[kind, skip : skip + MID, :] for kind in range(2)]
-    pack(new, ((TOP + skip, 0, MID),), middle, rolled, send)
+    pack(final, middle, rolled, blocks, send, sems)
+    finish_pack(blocks, send, sems)
+    whole.wait()
 
 
 LOW = 8
@@ -238,7 +248,7 @@
 def outer_kernel(
     members, courant_x, courant_y, above, below, fields,
     out, send, fields_tall,
-    old, new, courants, coefs, rolled, rims, member_sems, sems,
+    old, new, courants, coefs, rolled, final, blocks, rims, member_sems, wind_sems, sems,
 ):
     top, end = slice(TOP, TOP + 8), slice(ROWS - 8 + LOW, ROWS + LOW)
     copies = []
@@ -256,7 +266,7 @@
                 copies.append(
                     pltpu.make_async_copy(
                         source.at[rows, lanes], courants.at[kind, block, span, :],
-                        sems.at[kind, part, block],
+                        wind_sems.at[kind, part, block],
                     )
                 )
     for copy in copies:
@@ -290,17 +300,22 @@
     set_coefs(courants, coefs, range(0, HEIGHT, 8))
     for step in range(3):
         high, low = TOP - EDGE + 1 + step, ROWS - 6 + step + LOW
-        pair = (old, new) if step % 2 == 0 else (new, old)
-        advance(*pair, coefs, (high, high + 8, low, low + 8))
-    keep = (ROWS - MID) // 2
-    low = ROWS - keep + LOW
-    for member in range(LOCAL):
-        for block in range(GROUPS):
-            out[member, block, 0:keep, :] = new[member, block + 1, TOP : TOP + keep, :]
-            out[member, block, keep : 2 * keep, :] = new[member, block + 1, low : low + keep, :]
-    pack(new, ((TOP - REACH, 0, RIM), (low, RIM, RIM)), rims, rolled, send)
-
-
+        starts = (high, high + 8, low, low + 8)
+        if step < 2:
+            pair = (old, new) if step == 0 else (new, old)
+            advance(*pair, coefs, starts)
+        else:
+            advance(old, final, coefs, starts, (0, 8, RIM, RIM + 8))
+    whole = pltpu.make_async_copy(
+        final.at[:, pl.ds(1, GROUPS), pl.ds(REACH, 8), :], out, sems.at[GROUPS]
+    )
+    whole.start()
+    pack(final, rims, rolled, blocks, send, sems)
+    finish_pack(blocks, send, sems)
+    whole.wait()
+
+
+COPIES = 4
 DEEP = 56
 MID_ROWS = ((RIM, 0, MID),)
 RIM_ROWS = ((0, 0, RIM), (TALL - RIM, RIM, RIM))
@@ -337,26 +352,24 @@
         store(slot, slots[slot])
 
 
-def shifted_copies(copies, slots, low, rows):
-    lane = lane_ids(rows)
-
-    for slot in range(slots):
-        mid = copies[RADIUS, slot, low : low + rows, :]
-        after = copies[RADIUS, min(slot + 1, SLOTS - 1), low : low + rows, :]
-        before = copies[RADIUS, max(slot - 1, 0), low : low + rows, :]
-        for shift in (1, 2):
-            copies[RADIUS + shift, slot, low : low + rows, :] = pltpu.roll(
-                jnp.where(lane < shift, after, mid), LANES - shift, 1
-            )
-            copies[RADIUS - shift, slot, low : low + rows, :] = pltpu.roll(
-                jnp.where(lane >= LANES - shift, before, mid), shift, 1
-            )
+def shifted(before, mid, after, lane):
+    found = {0: mid}
+    for shift in (1, 2):
+        found[shift] = pltpu.roll(jnp.where(lane < shift, after, mid), LANES - shift, 1)
+        found[-shift] = pltpu.roll(jnp.where(lane >= LANES - shift, before, mid), shift, 1)
+    return found
+
+
+def put(target, span, found):
+    for shift, value in found.items():
+        target[RADIUS + shift, span, :] = value
 
 
 def analysis_kernel(
     place, offsets, weights, got_mid, got_rim, fields, increment, spread_copies,
-    spread, averages, gains, inside, products, localized, total, plane, ends,
+    spread, averages, gains, inside, total, plane, ends, *copies,
 ):
+    first_copies, second_copies = copies[: len(copies) // 2], copies[len(copies) // 2 :]
     tile, block = place[0], place[1]
     lane = lane_ids(TALL)
     entries = offsets.shape[0]
@@ -429,35 +442,43 @@
     def store_gain(slot, value):
         gains[slot] = value
 
+    def taps(source, sign, low, rows):
+        value = None
+        for entry in range(entries):
+            term = tap[entry] * source[
+                RADIUS + sign * tap_col[entry], pl.ds(low + sign * tap_row[entry], rows), :
+            ]
+            value = term if value is None else value + term
+        return value
+
     def sweep(slots, multiplier, y_rows, z_low, z_rows, x_low, x_rows, finish):
-        @pl.loop(0, slots)
-        def _(slot):
-            products[RADIUS, slot, 0:TALL, :] = multiplier(slot)
-
-        shifted_copies(products, slots, z_low - RADIUS, y_rows)
-
-        @pl.loop(0, slots)
-        def _(slot):
-            value = None
-            for entry in range(entries):
-                term = tap[entry] * products[
-                    RADIUS - tap_col[entry], slot, pl.ds(z_low - tap_row[entry], z_rows), :
-                ]
-                value = term if value is None else value + term
-            rows = slice(z_low, z_low + z_rows)
-            localized[RADIUS, slot, rows, :] = value * inside[slot, rows, :]
-
-        shifted_copies(localized, slots, z_low, z_rows)
-
-        @pl.loop(0, slots)
-        def _(slot):
-            value = None
-            for entry in range(entries):
-                term = tap[entry] * localized[
-                    RADIUS + tap_col[entry], slot, pl.ds(x_low + tap_row[entry], x_rows), :
-                ]
-                value = term if value is None else value + term
-            finish(slot, value)
+        y_span = slice(z_low - RADIUS, z_low - RADIUS + y_rows)
+        z_span = slice(z_low, z_low + z_rows)
+        y_lane, z_lane = lane_ids(y_rows), lane_ids(z_rows)
+        products, localized = {}, {}
+
+        def copies_of(held, slot, lane_here):
+            mid = held[slot]
+            return shifted(held.get(slot - 1, mid), mid, held.get(slot + 1, mid), lane_here)
+
+        products[0], products[1] = multiplier(0, y_span), multiplier(1, y_span)
+        put(first_copies[0], y_span, copies_of(products, 0, y_lane))
+        for slot in range(slots + 3):
+            if slot + 1 < slots:
+                if slot + 2 < slots:
+                    products[slot + 2] = multiplier(slot + 2, y_span)
+                ahead = copies_of(products, slot + 1, y_lane)
+            if slot < slots:
+                value = taps(first_copies[slot % COPIES], -1, z_low, z_rows)
+                localized[slot] = value * inside[slot, z_span, :]
+            if slot + 1 < slots:
+                put(first_copies[(slot + 1) % COPIES], y_span, ahead)
+            if 1 < slot < slots + 2:
+                behind = copies_of(localized, slot - 2, z_lane)
+            if slot > 2:
+                finish(slot - 3, taps(second_copies[(slot - 3) % COPIES], 1, x_low, x_rows))
+            if 1 < slot < slots + 2:
+                put(second_copies[(slot - 2) % COPIES], z_span, behind)
 
     def apply(near, far, y_rows, z_low, z_rows, x_low, x_rows):
         spread_out(near, far, lane, store_gain)
@@ -466,7 +487,7 @@
         def finish_ones(slot, value):
             plane[slot, 0:x_rows, :] = value
 
-        sweep(2, lambda slot: gains[slot], y_rows, z_low, z_rows, x_low, x_rows, finish_ones)
+        sweep(2, lambda slot, rows: gains[slot, rows, :], y_rows, z_low, z_rows, x_low, x_rows, finish_ones)
 
         @pl.loop(0, SLOTS)
         def _(slot):
@@ -478,17 +499,12 @@
                 total[slot, 0:x_rows, :] += value * spread[source, slot, x_low : x_low + x_rows, :]
 
             sweep(
-                SLOTS, lambda slot: gains[slot] * spread[source, slot],
+                SLOTS, lambda slot, rows: gains[slot, rows, :] * spread[source, slot, rows, :],
                 y_rows, z_low, z_rows, x_low, x_rows, finish,
             )
 
         near, far = folded(lambda slot: total[slot, 0:x_rows, :], lane_ids(x_rows))
         return (near + plane[0, 0:x_rows, :]) * scale, (far + plane[1, 0:x_rows, :]) * scale
-
-    for slot in range(SLOTS):
-        for kind in range(2 * RADIUS + 1):
-            products[kind, slot, TALL:DEEP, :] = jnp.zeros((DEEP - TALL, LANES), F32)
-        localized[RADIUS, slot] = jnp.zeros((DEEP, LANES), F32)
 
     (near_v, far_v), (near_w, far_w) = planes
     near, far = apply(near_v, far_v, 48, 2, 48, 4, 40)
@@ -537,39 +553,50 @@
 ):
     both = ("member", "grp")
     params = pltpu.CompilerParams(vmem_limit_bytes=VMEM)
+    crowded = pltpu.CompilerParams(vmem_limit_bytes=ALL_VMEM)
+    cost = pl.CostEstimate(flops=10_000_000, bytes_accessed=60_000_000, transcendentals=0)
     tiles = lax.axis_size("tile")
     keep = (ROWS - MID) // 2
+    sems = pltpu.SemaphoreType.DMA
     buffers = [
         pltpu.VMEM((LOCAL, GROUPS + 2, HEIGHT, LANES), F32),
         pltpu.VMEM((LOCAL, GROUPS + 2, HEIGHT, LANES), F32),
         pltpu.VMEM((2, GROUPS, HEIGHT, LANES), F32),
         pltpu.VMEM((5, GROUPS, HEIGHT, LANES), F32),
         pltpu.VMEM((LOCAL, GROUPS + 2, MID, LANES), F32),
+        pltpu.VMEM((LOCAL, GROUPS + 2, MID + 8, LANES), F32),
+        pltpu.VMEM((GROUPS, SLOTS, MID, LANES), F32),
     ]
-    up, down, fields, middle, send_mid = pl.pallas_call(
-        inner_kernel,
-        out_shape=[
-            array(GROUPS, HALO, LANES),
-            array(GROUPS, HALO, LANES),
-            array(2, ROWS, LANES),
-            array(LOCAL, GROUPS, MID, LANES),
-            array(GROUPS, SLOTS, MID, LANES),
-        ],
+    up, down, fields = pl.pallas_call(
+        message_kernel,
+        out_shape=[array(GROUPS, HALO, LANES), array(GROUPS, HALO, LANES), array(2, ROWS, LANES)],
         in_specs=in_hbm(6),
-        out_specs=on_vmem(5),
-        scratch_shapes=buffers
-        + [
+        out_specs=on_vmem(3),
+        scratch_shapes=[
+            pltpu.VMEM(members.shape, F32),
+            pltpu.VMEM((2, ROWS, COLS), F32),
             pltpu.VMEM((1, 1, 1024), jnp.int32),
             pltpu.VMEM((2, 1, 1, 1024), F32),
-            pltpu.SemaphoreType.DMA((GROUPS,)),
-            pltpu.SemaphoreType.DMA((3 + 2 * GROUPS,)),
+            sems((3,)),
+            sems((3,)),
         ],
-        compiler_params=params,
-        name="inner",
+        compiler_params=crowded,
+        name="messages",
     )(members, courant_x, courant_y, obs_cell, innovation, obs_weight)
-    got_mid = exchanged(send_mid, both)
     above = lax.ppermute(down, "tile", [(i, i + 1) for i in range(tiles - 1)])
     below = lax.ppermute(up, "tile", [(i + 1, i) for i in range(tiles - 1)])
+    middle, send_mid = pl.pallas_call(
+        inner_kernel,
+        out_shape=[array(LOCAL, GROUPS, MID, LANES), array(GROUPS, SLOTS, MID, LANES)],
+        in_specs=in_hbm(3) + on_vmem(1),
+        out_specs=in_hbm(2),
+        scratch_shapes=buffers + [sems((GROUPS,)), sems((2, GROUPS)), sems((GROUPS + 1,))],
+        compiler_params=crowded,
+        cost_estimate=cost,
+        name="inner",
+    )(members, courant_x, courant_y, fields)
+    send_mid, above, below = lax.optimization_barrier((send_mid, above, below))
+    got_mid = exchanged(send_mid, both)
     rim, send_rim, fields_tall = pl.pallas_call(
         outer_kernel,
         out_shape=[
@@ -578,16 +605,19 @@
             array(2, TALL, LANES),
         ],
         in_specs=in_hbm(3) + on_vmem(3),
-        out_specs=on_vmem(3),
+        out_specs=in_hbm(2) + on_vmem(1),
         scratch_shapes=buffers
         + [
             pltpu.VMEM((2, MID, LANES), F32),
-            pltpu.SemaphoreType.DMA((2, GROUPS)),
-            pltpu.SemaphoreType.DMA((2, 2, GROUPS)),
+            sems((2, GROUPS)),
+            sems((2, 2, GROUPS)),
+            sems((GROUPS + 1,)),
         ],
-        compiler_params=params,
+        compiler_params=crowded,
+        cost_estimate=cost,
         name="outer",
     )(members, courant_x, courant_y, above, below, fields)
+    send_rim, got_mid = lax.optimization_barrier((send_rim, got_mid))
     got_rim = exchanged(send_rim, both)
     place = jnp.stack([lax.axis_index("tile"), lax.axis_index(both)]).astype(jnp.int32)
     increment, copies = pl.pallas_call(
@@ -600,12 +630,11 @@
             pltpu.VMEM((SLOTS, TALL, LANES), F32),
             pltpu.VMEM((SLOTS, TALL, LANES), F32),
             pltpu.VMEM((SLOTS, DEEP, LANES), F32),
-            pltpu.VMEM((2 * RADIUS + 1, SLOTS, DEEP, LANES), F32),
-            pltpu.VMEM((2 * RADIUS + 1, SLOTS, DEEP, LANES), F32),
             pltpu.VMEM((SLOTS, TALL, LANES), F32),
             pltpu.VMEM((4, TALL, LANES), F32),
             pltpu.VMEM((2, TALL, LANES), F32),
-        ],
+        ]
+        + [pltpu.VMEM((2 * RADIUS + 1, DEEP, LANES), F32)] * (2 * COPIES),
         compiler_params=params,
         name="analysis",
     )(place, stencil_offsets, stencil_weights, got_mid, got_rim, fields_tall)

time: 105 us -> 93.8 us (0.89)
  the two profiles are of different devices: /device:TPU:16 before, /device:TPU:64 now
where the time goes in v2:
time: 93.8 us; the launch traced here: 93.2 us
  Pallas kernels  38.1 us (41%)
  waiting for transfers between devices  29.8 us (32%)
  starting transfers between devices  14.6 us (16%)
  blocking collectives  8.79 us (9%)
  local copies, waits for them, and re-layouts  1.1 us (1%)
    all_to_all x2, waiting for transfers between devices, exchanged(): return lax.all_to_all(flat, axes, 0, 0, tiled=True).reshape(blocks.shape)  29.8 us
    pallas_call x1, Pallas kernels, on_device(): pl.pallas_call(analysis_kernel, out_shape=[array(ROWS, LANES), array(GROU...  17.1 us
    pallas_call x1, Pallas kernels, on_device(): pl.pallas_call(outer_kernel, out_shape=[array(LOCAL, GROUPS, 2 * keep, LA...  9.27 us
    all_to_all x2, starting transfers between devices, exchanged(): return lax.all_to_all(flat, axes, 0, 0, tiled=True).reshape(blocks.shape)  9.01 us
    all_to_all x1, blocking collectives, on_device(): increments = lax.all_to_all(copies, both, 0, 0, tiled=True)  8.79 us
    pallas_call x1, Pallas kernels, on_device(): pl.pallas_call(inner_kernel, out_shape=[array(LOCAL, GROUPS, MID, LANES),...  7.93 us
    ppermute x1, starting transfers between devices, on_device(): below = lax.ppermute(up, 'tile', [(i + 1, i) for i in range(tiles - 1)])  3.64 us
    pallas_call x1, Pallas kernels, on_device(): pl.pallas_call(message_kernel, out_shape=[array(GROUPS, HALO, LANES), arr...  2.57 us
  transfers between devices with their start and end apart: 4, of which 2 were waited for; matrix products, arithmetic and copies ran while one was open for 0% of the time, Pallas kernels for 18%

profile of v2, /device:TPU:64, one launch (start us, length us, event | category | flops | bytes accessed | tf_op | source)
XLA Modules:
  0.0 93.2 jit_solution(15794146810244584307)
XLA Ops:
  0.6 2.6 %messages.1 = (f32[8,136,128]{2,1,0:T(8,128)}, f32[8,136,128]{2,1,0:T(8,128)}, f32[2,32,128]{2,1,0:T(8,128)}) custom-call(f32[10,32,1024]{2,1,0:T(8,128)} %members.5, f32[32,1024]{1,0:T(8,128)} %courant_x.5, f32[32,1024]{1,0:T(8,128)} %courant_y.5, s32[1,1,1024]{2,1,0:T(1,128)} %cell.1, f32[1,1,1024]{2,1,0:T(1,128)} %innov.1, f32[1,1,1024]{2,1,0:T(1,128)} %weight.1), custom_call_target="tpu_custom_call" | custom-call | tf_op jit(solution)/shard_map/messages/pallas_call | solution.py:570
  3.2 1.9 %collective-permute-start = (f32[8,136,128]{2,1,0:T(8,128)}, f32[8,136,128]{2,1,0:T(8,128)S(1)}, u32[]{:S(2)}, u32[]{:S(2)}) collective-permute-start(f32[8,136,128]{2,1,0:T(8,128)} %get-tuple-element.20), channel_id=1, source_target_pairs={{0,2},{2,4},{4,6},{6,8},{8,10},{10,12},{12,14},{14,16},{16,18},{18... | collective-permute-start | bytes 1671176 | tf_op jit(solution)/shard_map/ppermute | solution.py:586
  5.1 3.6 %collective-permute-start.1 = (f32[8,136,128]{2,1,0:T(8,128)}, f32[8,136,128]{2,1,0:T(8,128)S(1)}, u32[]{:S(2)}, u32[]{:S(2)}) collective-permute-start(f32[8,136,128]{2,1,0:T(8,128)} %get-tuple-element.21), channel_id=1, source_target_pairs={{2,0},{4,2},{6,4},{8,6},{10,8},{12,10},{14,12},{16,14},{18,16},{20... | collective-permute-start | bytes 1671176 | tf_op jit(solution)/shard_map/ppermute | solution.py:587
  8.8 7.9 %inner.1 = (f32[10,8,24,128]{3,2,1,0:T(8,128)}, f32[8,12,24,128]{3,2,1,0:T(8,128)}) custom-call(f32[10,32,1024]{2,1,0:T(8,128)} %members.5, f32[32,1024]{1,0:T(8,128)} %courant_x.5, f32[32,1024]{1,0:T(8,128)} %courant_y.5, f32[2,32,128]{2,1,0:T(8,128)} %get-tuple-element.17.fields), custom_call_target="tpu_custom_call" | custom-call | flops 10000000 | bytes 60000000 | tf_op jit(solution)/shard_map/inner/pallas_call | solution.py:588
  16.7 0.0 collective-permute-done.above
  16.7 0.0 copy-start.4
  16.7 0.0 collective-permute-done.1.below
  16.8 0.0 copy-start.5
  16.8 0.8 copy-done.4
  17.5 0.2 copy-done.5
  17.7 5.3 %all-to-all-start = ((f32[8,288,128]{2,1,0:T(8,128)}), f32[8,288,128]{2,1,0:T(8,128)S(1)}, u32[]{:S(2)}, u32[]{:S(2)}) async-start(f32[8,288,128]{2,1,0:T(8,128)} %bitcast.9), calls=%async_computation | async-start | bytes 2359296 | tf_op jit(solution)/shard_map/all_to_all | solution.py:655
  23.1 9.3 %outer.1 = (f32[10,8,8,128]{3,2,1,0:T(8,128)}, f32[8,12,24,128]{3,2,1,0:T(8,128)}, f32[2,48,128]{2,1,0:T(8,128)}) custom-call(f32[10,32,1024]{2,1,0:T(8,128)} %members.5, f32[32,1024]{1,0:T(8,128)} %courant_x.5, f32[32,1024]{1,0:T(8,128)} %courant_y.5, f32[8,136,128]{2,1,0:T(8,128)} %copy-done.4, f32[8,136,128]{2,1,0:T(8,128)} %copy-done.5, ...), custom_call_target="tpu_custom_call" | custom-call | flops 10000000 | bytes 60000000 | tf_op jit(solution)/shard_map/outer/pallas_call | solution.py:600
  32.3 10.9 %all-to-all-done = f32[8,288,128]{2,1,0:T(8,128)S(1)} async-done(((f32[8,288,128]{2,1,0:T(8,128)}), f32[8,288,128]{2,1,0:T(8,128)S(1)}, u32[]{:S(2)}, u32[]{:S(2)}) %all-to-all-start) | async-done | bytes 1179680 | tf_op jit(solution)/shard_map/all_to_all | solution.py:655
  43.3 0.0 copy-start.6
  43.3 0.0 copy-start.2
  43.3 0.0 copy-start.3
  43.3 3.7 %all-to-all-start.1 = ((f32[8,288,128]{2,1,0:T(8,128)}), f32[8,288,128]{2,1,0:T(8,128)S(1)}, u32[]{:S(2)}, u32[]{:S(2)}) async-start(f32[8,288,128]{2,1,0:T(8,128)} %bitcast.8), calls=%async_computation.1 | async-start | bytes 2359296 | tf_op jit(solution)/shard_map/all_to_all | solution.py:655
  47.0 0.0 copy-done.6
  47.0 0.1 copy.10.offsets
  47.1 0.1 pad_add_fusion.place
  47.2 18.8 %all-to-all-done.1 = f32[8,288,128]{2,1,0:T(8,128)S(1)} async-done(((f32[8,288,128]{2,1,0:T(8,128)}), f32[8,288,128]{2,1,0:T(8,128)S(1)}, u32[]{:S(2)}, u32[]{:S(2)}) %all-to-all-start.1) | async-done | bytes 1179680 | tf_op jit(solution)/shard_map/all_to_all | solution.py:655
  66.0 0.0 copy-done.2
  66.0 0.0 copy-done.3
  66.0 0.0 copy-start
  66.0 0.0 copy-start.1
  66.0 17.1 %analysis.1 = (f32[32,128]{1,0:T(8,128)}, f32[8,32,128]{2,1,0:T(8,128)S(1)}) custom-call(s32[2]{0:T(128)S(1)} %pad_add_fusion.place, s32[9,2]{1,0:T(8,128)S(1)} %copy.10.offsets, f32[9]{0:T(128)S(1)} %copy-done.3, f32[8,12,24,128]{3,2,1,0:T(8,128)S(1)} %bitcast.6, f32[8,12,24,128]{3,2,1,0:T(8,128)S(1)} %bitcast.7, f32[2,48,128]{2,1,0:T(8,128)S(1)} %copy-done.2), custom_call_target="tpu_custom_call" | custom-call | tf_op jit(solution)/shard_map/analysis/pallas_call | solution.py:623
  83.1 8.8 %all_to_all.15.increments = f32[8,32,128]{2,1,0:T(8,128)S(1)} all-to-all(f32[8,32,128]{2,1,0:T(8,128)S(1)} %get-tuple-element.30), channel_id=1, replica_groups=mesh['member'=4,'tile'=32,'grp'=2] {'member','grp'}, dimensions={0} | all-to-all | bytes 262144 | tf_op jit(solution)/shard_map/all_to_all | solution.py:641
  91.9 0.0 copy-done
  91.9 0.0 copy-done.1
  91.9 1.3 %recentre.1 = f32[10,32,1024]{2,1,0:T(8,128)} custom-call(f32[10,8,24,128]{3,2,1,0:T(8,128)S(1)} %copy-done, f32[10,8,8,128]{3,2,1,0:T(8,128)S(1)} %copy-done.1, f32[8,32,128]{2,1,0:T(8,128)S(1)} %all_to_all.15.increments), custom_call_target="tpu_custom_call" | custom-call | tf_op jit(solution)/shard_map/recentre/pallas_call | solution.py:642
Async XLA Ops:
  3.2 13.5 %collective-permute-start = (f32[8,136,128]{2,1,0:T(8,128)}, f32[8,136,128]{2,1,0:T(8,128)S(1)}, u32[]{:S(2)}, u32[]{:S(2)}) collective-permute-start(f32[8,136,128]{2,1,0:T(8,128)} %get-tuple-element.20), channel_id=1, source_target_pairs={{0,2},{2,4},{4,6},{6,8},{8,10},{10,12},{12,14},{14,16},{16,18},{18... | collective-permute-start | bytes 1671176 | tf_op jit(solution)/shard_map/ppermute | solution.py:586
  5.1 11.6 %collective-permute-start.1 = (f32[8,136,128]{2,1,0:T(8,128)}, f32[8,136,128]{2,1,0:T(8,128)S(1)}, u32[]{:S(2)}, u32[]{:S(2)}) collective-permute-start(f32[8,136,128]{2,1,0:T(8,128)} %get-tuple-element.21), channel_id=1, source_target_pairs={{2,0},{4,2},{6,4},{8,6},{10,8},{12,10},{14,12},{16,14},{18,16},{20... | collective-permute-start | bytes 1671176 | tf_op jit(solution)/shard_map/ppermute | solution.py:587
  16.7 0.8 copy-start.4
  16.8 1.0 %copy-start.5 = (f32[8,136,128]{2,1,0:T(8,128)}, f32[8,136,128]{2,1,0:T(8,128)S(1)}, u32[]{:S(2)}) copy-start(f32[8,136,128]{2,1,0:T(8,128)S(1)} %collective-permute-done.1.below) | copy-start | bytes 1671172
  17.7 25.5 %all-to-all-start = ((f32[8,288,128]{2,1,0:T(8,128)}), f32[8,288,128]{2,1,0:T(8,128)S(1)}, u32[]{:S(2)}, u32[]{:S(2)}) async-start(f32[8,288,128]{2,1,0:T(8,128)} %bitcast.9), calls=%async_computation | async-start | bytes 2359296 | tf_op jit(solution)/shard_map/all_to_all | solution.py:655
  43.3 3.7 %copy-start.6 = (s32[9,2]{0,1:T(2,128)S(1)}, s32[9,2]{0,1:T(2,128)}, u32[]{:S(2)}) copy-start(s32[9,2]{0,1:T(2,128)} %param.14) | copy-start | bytes 220
  43.3 22.7 %copy-start.2 = (f32[2,48,128]{2,1,0:T(8,128)S(1)}, f32[2,48,128]{2,1,0:T(8,128)}, u32[]{:S(2)}) copy-start(f32[2,48,128]{2,1,0:T(8,128)} %get-tuple-element.29.fields) | copy-start | bytes 147460
  43.3 22.7 %copy-start.3 = (f32[9]{0:T(128)S(1)}, f32[9]{0:T(128)}, u32[]{:S(2)}) copy-start(f32[9]{0:T(128)} %weights.1) | copy-start | bytes 112
  43.3 22.7 %all-to-all-start.1 = ((f32[8,288,128]{2,1,0:T(8,128)}), f32[8,288,128]{2,1,0:T(8,128)S(1)}, u32[]{:S(2)}, u32[]{:S(2)}) async-start(f32[8,288,128]{2,1,0:T(8,128)} %bitcast.8), calls=%async_computation.1 | async-start | bytes 2359296 | tf_op jit(solution)/shard_map/all_to_all | solution.py:655
  66.0 25.9 %copy-start = (f32[10,8,24,128]{3,2,1,0:T(8,128)S(1)}, f32[10,8,24,128]{3,2,1,0:T(8,128)}, u32[]{:S(2)}) copy-start(f32[10,8,24,128]{3,2,1,0:T(8,128)} %get-tuple-element.18.middle) | copy-start | bytes 2949124
  66.0 25.9 %copy-start.1 = (f32[10,8,8,128]{3,2,1,0:T(8,128)S(1)}, f32[10,8,8,128]{3,2,1,0:T(8,128)}, u32[]{:S(2)}) copy-start(f32[10,8,8,128]{3,2,1,0:T(8,128)} %get-tuple-element.24.rim) | copy-start | bytes 983044

commit v3 on v2

--- a/solution.py
+++ b/solution.py
@@ -25,7 +25,7 @@
 HALO = 136
 MID = 24
 RIM = (TALL - MID) // 2
-VMEM = 48 * 1024 * 1024
+VMEM = 16 * 1024 * 1024
 ALL_VMEM = 60 * 1024 * 1024
 
 
@@ -71,7 +71,7 @@
     lane = lane_ids(8)
     first, last = lane == 0, lane == LANES - 1
 
-    @pl.loop(0, GROUPS)
+    @pl.loop(0, GROUPS, unroll=4)
     def _(block):
         for low, home in zip(starts, homes):
             rows = slice(low, low + 8)
@@ -108,7 +108,7 @@
 
 
 def pack(final, fields, rolled, blocks, send, sems):
-    @pl.loop(0, GROUPS)
+    @pl.loop(0, GROUPS, unroll=8)
     def _(block):
         for member in range(LOCAL):
             shift = (member * WIDE + REACH) % LANES
@@ -317,8 +317,6 @@
 
 COPIES = 4
 DEEP = 56
-MID_ROWS = ((RIM, 0, MID),)
-RIM_ROWS = ((0, 0, RIM), (TALL - RIM, RIM, RIM))
 
 
 def member_place(member):
@@ -365,13 +363,7 @@
         target[RADIUS + shift, span, :] = value
 
 
-def analysis_kernel(
-    place, offsets, weights, got_mid, got_rim, fields, increment, spread_copies,
-    spread, averages, gains, inside, total, plane, ends, *copies,
-):
-    first_copies, second_copies = copies[: len(copies) // 2], copies[len(copies) // 2 :]
-    tile, block = place[0], place[1]
-    lane = lane_ids(TALL)
+def localizer(offsets, weights, inside, copies):
     entries = offsets.shape[0]
     tap_row = [offsets[entry, 0] for entry in range(entries)]
     tap_col = [offsets[entry, 1] for entry in range(entries)]
@@ -380,67 +372,7 @@
     for entry in range(1, entries):
         weight_sum = weight_sum + tap[entry]
     scale = 1.0 / jnp.full((1, LANES), weight_sum, F32)
-    scale = scale * scale
-
-    @pl.loop(0, SLOTS)
-    def _(slot):
-        for got, parts in ((got_mid, MID_ROWS), (got_rim, RIM_ROWS)):
-            value = got[0, slot]
-            for source in range(1, GROUPS):
-                value = value + got[source, slot]
-            for here, there, count in parts:
-                averages[slot, here : here + count, :] = value[there : there + count]
-
-    near, far = folded(lambda slot: averages[slot], lane)
-    count = GROUPS * LOCAL
-
-    def store_average(slot, value):
-        averages[slot] = value
-
-    spread_out(near / count, far / count, lane, store_average)
-    deviation = 1.0 / math.sqrt(count - 1)
-
-    @pl.loop(0, SLOTS)
-    def _(slot):
-        for got, parts in ((got_mid, MID_ROWS), (got_rim, RIM_ROWS)):
-            for here, there, count in parts:
-                average = averages[slot, here : here + count, :]
-                for source in range(GROUPS):
-                    value = got[source, slot, there : there + count, :]
-                    spread[source, slot, here : here + count, :] = (value - average) * deviation
-
-    row = lax.broadcasted_iota(jnp.int32, (TALL, LANES), 0) + (tile * ROWS - REACH)
-    col = lane + (block * LANES - REACH)
-    row_ok = (row >= 0) & (row < ROWS * 32)
-    near_ok = row_ok & (col >= 0) & (col < COLS)
-    far_ok = row_ok & (col + LANES < COLS)
-
-    def store_inside(slot, value):
-        inside[slot, 0:TALL, :] = value
-        inside[slot, TALL:DEEP, :] = jnp.zeros((DEEP - TALL, LANES), F32)
-
-    spread_out(near_ok.astype(F32), far_ok.astype(F32), lane, store_inside)
-
-    for got, parts in ((got_mid, MID_ROWS), (got_rim, RIM_ROWS)):
-        for here, there, count in parts:
-            rows = slice(there, there + count)
-            ends[0, here : here + count, :] = got[jnp.maximum(block - 1, 0), SLOTS - 1, rows, :]
-            ends[1, here : here + count, :] = got[
-                jnp.minimum(block + 1, GROUPS - 1), SLOTS - 1, rows, :
-            ]
-    left_ends = jnp.where(block > 0, ends[0], 0.0)
-    right_ends = jnp.where(block < GROUPS - 1, ends[1], 0.0)
-    planes = []
-    for kind in range(2):
-        back = LANES - SPARE - 2 * REACH * kind
-        own = pltpu.roll(fields[kind], REACH, 1)
-        near = jnp.where(lane < REACH, pltpu.roll(left_ends, back, 1), own)
-        far = jnp.where(lane < REACH, own, pltpu.roll(right_ends, back, 1))
-        far = jnp.where(lane < 2 * REACH, far, 0.0)
-        planes.append((near, far))
-
-    def store_gain(slot, value):
-        gains[slot] = value
+    first_copies, second_copies = copies[: len(copies) // 2], copies[len(copies) // 2 :]
 
     def taps(source, sign, low, rows):
         value = None
@@ -451,72 +383,229 @@
             value = term if value is None else value + term
         return value
 
-    def sweep(slots, multiplier, y_rows, z_low, z_rows, x_low, x_rows, finish):
-        y_span = slice(z_low - RADIUS, z_low - RADIUS + y_rows)
-        z_span = slice(z_low, z_low + z_rows)
-        y_lane, z_lane = lane_ids(y_rows), lane_ids(z_rows)
-        products, localized = {}, {}
-
-        def copies_of(held, slot, lane_here):
-            mid = held[slot]
-            return shifted(held.get(slot - 1, mid), mid, held.get(slot + 1, mid), lane_here)
-
-        products[0], products[1] = multiplier(0, y_span), multiplier(1, y_span)
-        put(first_copies[0], y_span, copies_of(products, 0, y_lane))
+    def sweep(slots, multiplier, bands, finish):
+        def copies_of(held, slot):
+            found = []
+            for at, mid in enumerate(held[slot]):
+                before = held.get(slot - 1, held[slot])[at]
+                after = held.get(slot + 1, held[slot])[at]
+                found.append(shifted(before, mid, after, lane_ids(mid.shape[0])))
+            return found
+
+        def put_all(target, found, kind):
+            for band, values in zip(bands, found):
+                low, rows = band[kind]
+                put(target, slice(low, low + rows), values)
+
+        def entering(slot):
+            return [multiplier(slot, slice(band[0][0], sum(band[0]))) for band in bands]
+
+        products, localized = {0: entering(0), 1: entering(1)}, {}
+        put_all(first_copies[0], copies_of(products, 0), 0)
         for slot in range(slots + 3):
             if slot + 1 < slots:
                 if slot + 2 < slots:
-                    products[slot + 2] = multiplier(slot + 2, y_span)
-                ahead = copies_of(products, slot + 1, y_lane)
+                    products[slot + 2] = entering(slot + 2)
+                ahead = copies_of(products, slot + 1)
             if slot < slots:
-                value = taps(first_copies[slot % COPIES], -1, z_low, z_rows)
-                localized[slot] = value * inside[slot, z_span, :]
+                localized[slot] = [
+                    taps(first_copies[slot % COPIES], -1, *band[1])
+                    * inside[slot, band[1][0] : sum(band[1]), :]
+                    for band in bands
+                ]
             if slot + 1 < slots:
-                put(first_copies[(slot + 1) % COPIES], y_span, ahead)
+                put_all(first_copies[(slot + 1) % COPIES], ahead, 0)
             if 1 < slot < slots + 2:
-                behind = copies_of(localized, slot - 2, z_lane)
+                behind = copies_of(localized, slot - 2)
             if slot > 2:
-                finish(slot - 3, taps(second_copies[(slot - 3) % COPIES], 1, x_low, x_rows))
+                done = slot - 3
+                finish(done, [taps(second_copies[done % COPIES], 1, *band[2]) for band in bands])
             if 1 < slot < slots + 2:
-                put(second_copies[(slot - 2) % COPIES], z_span, behind)
-
-    def apply(near, far, y_rows, z_low, z_rows, x_low, x_rows):
-        spread_out(near, far, lane, store_gain)
-        ones = []
-
-        def finish_ones(slot, value):
-            plane[slot, 0:x_rows, :] = value
-
-        sweep(2, lambda slot, rows: gains[slot, rows, :], y_rows, z_low, z_rows, x_low, x_rows, finish_ones)
-
-        @pl.loop(0, SLOTS)
-        def _(slot):
-            total[slot, 0:x_rows, :] = jnp.zeros((x_rows, LANES), F32)
-
-        @pl.loop(0, GROUPS)
-        def _(source):
-            def finish(slot, value):
-                total[slot, 0:x_rows, :] += value * spread[source, slot, x_low : x_low + x_rows, :]
-
-            sweep(
-                SLOTS, lambda slot, rows: gains[slot, rows, :] * spread[source, slot, rows, :],
-                y_rows, z_low, z_rows, x_low, x_rows, finish,
-            )
-
-        near, far = folded(lambda slot: total[slot, 0:x_rows, :], lane_ids(x_rows))
-        return (near + plane[0, 0:x_rows, :]) * scale, (far + plane[1, 0:x_rows, :]) * scale
-
-    (near_v, far_v), (near_w, far_w) = planes
-    near, far = apply(near_v, far_v, 48, 2, 48, 4, 40)
+                put_all(second_copies[(slot - 2) % COPIES], behind, 1)
+
+    return sweep, scale * scale
+
+
+def applied(sweep, scale, near, far, bands, spread, gains, total, plane):
+    spots, rows = [], 0
+    for band in bands:
+        spots.append((slice(rows, rows + band[2][1]), slice(band[2][0], sum(band[2]))))
+        rows += band[2][1]
+
+    def store_gain(slot, value):
+        gains[slot] = value
+
+    spread_out(near, far, lane_ids(near.shape[0]), store_gain)
+
+    def finish_ones(slot, values):
+        for (here, _), value in zip(spots, values):
+            plane[slot, here, :] = value
+
+    sweep(2, lambda slot, span: gains[slot, span, :], bands, finish_ones)
+
+    @pl.loop(0, SLOTS)
+    def _(slot):
+        total[slot, 0:rows, :] = jnp.zeros((rows, LANES), F32)
+
+    @pl.loop(0, GROUPS)
+    def _(source):
+        def finish(slot, values):
+            for (here, there), value in zip(spots, values):
+                total[slot, here, :] += value * spread(source, slot, there)
+
+        sweep(
+            SLOTS, lambda slot, span: gains[slot, span, :] * spread(source, slot, span),
+            bands, finish,
+        )
+
+    near, far = folded(lambda slot: total[slot, 0:rows, :], lane_ids(rows))
+    return (near + plane[0, 0:rows, :]) * scale, (far + plane[1, 0:rows, :]) * scale
+
+
+def set_spread(got, parts, averages, spread):
+    count = GROUPS * LOCAL
+    deviation = 1.0 / math.sqrt(count - 1)
+    rows = parts[0][2] * len(parts)
+
+    @pl.loop(0, SLOTS)
+    def _(slot):
+        value = got[0, slot]
+        for source in range(1, GROUPS):
+            value = value + got[source, slot]
+        averages[slot, 0:rows, :] = value
+
+    lane = lane_ids(rows)
+    near, far = folded(lambda slot: averages[slot, 0:rows, :], lane)
+
+    def store_average(slot, value):
+        averages[slot, 0:rows, :] = value
+
+    spread_out(near / count, far / count, lane, store_average)
+
+    @pl.loop(0, SLOTS)
+    def _(slot):
+        average = averages[slot, 0:rows, :]
+        for source in range(GROUPS):
+            value = (got[source, slot] - average) * deviation
+            for here, there, number in parts:
+                spread[source, slot, here : here + number, :] = value[there : there + number]
+
+
+def block_ends(got, parts, block, ends):
+    for here, there, count in parts:
+        rows = slice(there, there + count)
+        ends[0, here : here + count, :] = got[jnp.maximum(block - 1, 0), SLOTS - 1, rows, :]
+        ends[1, here : here + count, :] = got[
+            jnp.minimum(block + 1, GROUPS - 1), SLOTS - 1, rows, :
+        ]
+
+
+def with_margins(own, kind, block, ends, rows):
+    lane = lane_ids(rows.stop - rows.start)
+    back = LANES - SPARE - 2 * REACH * kind
+    left_ends = jnp.where(block > 0, ends[0, rows, :], 0.0)
+    right_ends = jnp.where(block < GROUPS - 1, ends[1, rows, :], 0.0)
+    own = pltpu.roll(own, REACH, 1)
+    near = jnp.where(lane < REACH, pltpu.roll(left_ends, back, 1), own)
+    far = jnp.where(lane < REACH, own, pltpu.roll(right_ends, back, 1))
+    return near, jnp.where(lane < 2 * REACH, far, 0.0)
+
+
+EARLY = 16
+EARLY_BAND = ((RIM, MID), (RIM + RADIUS, MID), (RIM + 2 * RADIUS, EARLY))
+
+
+SPREAD_ROWS = GROUPS * SLOTS * MID
+SHARED = SLOTS + 5
+
+
+def handed_on(rows):
+    spread = rows.at[pl.ds(0, SPREAD_ROWS)].reshape(GROUPS, SLOTS, MID, LANES)
+    return spread, rows.at[pl.ds(SPREAD_ROWS, SHARED * TALL)].reshape(SHARED, TALL, LANES)
+
+
+def early_kernel(
+    place, offsets, weights, got, fields, handed,
+    averages, gains, total, plane, ends, *copies,
+):
+    spread, shared = handed_on(handed)
+    tile, block = place[0], place[1]
+    lane = lane_ids(TALL)
+    set_spread(got, ((0, 0, MID),), averages, spread)
+
+    row = lax.broadcasted_iota(jnp.int32, (TALL, LANES), 0) + (tile * ROWS - REACH)
+    col = lane + (block * LANES - REACH)
+    row_ok = (row >= 0) & (row < ROWS * 32)
+    near_ok = row_ok & (col >= 0) & (col < COLS)
+    far_ok = row_ok & (col + LANES < COLS)
+
+    def store_inside(slot, value):
+        shared[slot] = value
+
+    spread_out(near_ok.astype(F32), far_ok.astype(F32), lane, store_inside)
+    sweep, scale = localizer(offsets, weights, shared, copies)
+    ends[...] = jnp.zeros(ends.shape, F32)
+    block_ends(got, ((RIM, 0, MID),), block, ends)
+    near, far = with_margins(fields[0], 0, block, ends, slice(0, TALL))
+
+    def at(source, slot, rows):
+        return spread[source, slot, rows.start - RIM : rows.stop - RIM, :]
+
+    near, far = applied(sweep, scale, near, far, (EARLY_BAND,), at, gains, total, plane)
     for part, value in enumerate((near, far)):
-        plane[2 + part, 0:TALL, :] = jnp.zeros((TALL, LANES), F32)
-        plane[2 + part, 4:44, :] = value
-    near = (STEP_SIZE * near_w) * plane[2, 0:TALL, :] - (2.0 - STEP_SIZE) * near_v
-    far = (STEP_SIZE * far_w) * plane[3, 0:TALL, :] - (2.0 - STEP_SIZE) * far_v
-    far = jnp.where(lane < 2 * REACH, far, 0.0)
-    near, far = apply(near, far, 40, 6, 40, 8, 32)
-    short_lane = lane_ids(ROWS)
-    result = pltpu.roll(jnp.where(short_lane < REACH, far, near), LANES - REACH, 1) * -STEP_SIZE
+        shared[SLOTS, part * EARLY : (part + 1) * EARLY, :] = value
+    shared[SLOTS, 2 * EARLY : TALL, :] = jnp.zeros((TALL - 2 * EARLY, LANES), F32)
+    for kind in range(2):
+        shared[SLOTS + 1 + kind] = ends[kind]
+        shared[SLOTS + 3 + kind] = fields[kind]
+
+
+RIM_BANDS = (
+    ((0, MID), (RADIUS, EARLY), (2 * RADIUS, EARLY)),
+    ((MID, MID), (TALL - RADIUS - EARLY, EARLY), (TALL - 2 * RADIUS - EARLY, EARLY)),
+)
+LAST_BAND = ((2 * RADIUS, 40), (3 * RADIUS, 40), (REACH, ROWS))
+
+
+def analysis_kernel(
+    place, offsets, weights, got, handed, increment, spread_copies,
+    spread, averages, gains, total, plane, ends, *copies,
+):
+    spread_mid, shared = handed_on(handed)
+    block = place[1]
+    set_spread(got, ((0, 0, RIM), (TALL - RIM, RIM, RIM)), averages, spread)
+
+    @pl.loop(0, SLOTS)
+    def _(slot):
+        for source in range(GROUPS):
+            spread[source, slot, RIM : RIM + MID, :] = spread_mid[source, slot]
+
+    def at(source, slot, rows):
+        return spread[source, slot, rows, :]
+
+    sweep, scale = localizer(offsets, weights, shared, copies)
+    for kind in range(2):
+        ends[kind] = shared[SLOTS + 1 + kind]
+    block_ends(got, ((0, 0, RIM), (TALL - RIM, RIM, RIM)), block, ends)
+    rows = slice(0, TALL)
+    near_v, far_v = with_margins(shared[SLOTS + 3], 0, block, ends, rows)
+    near_w, far_w = with_margins(shared[SLOTS + 4], 1, block, ends, rows)
+
+    values = applied(sweep, scale, near_v, far_v, RIM_BANDS, at, gains, total, plane)
+    for part in range(2):
+        plane[2 + part] = jnp.zeros((TALL, LANES), F32)
+        low = 2 * RADIUS
+        plane[2 + part, low : low + EARLY, :] = values[part][0:EARLY]
+        plane[2 + part, TALL - low - EARLY : TALL - low, :] = values[part][EARLY : 2 * EARLY]
+        plane[2 + part, RIM + low : RIM + low + EARLY, :] = shared[
+            SLOTS, part * EARLY : (part + 1) * EARLY, :
+        ]
+    near = (STEP_SIZE * near_w) * plane[2] - (2.0 - STEP_SIZE) * near_v
+    far = (STEP_SIZE * far_w) * plane[3] - (2.0 - STEP_SIZE) * far_v
+    far = jnp.where(lane_ids(TALL) < 2 * REACH, far, 0.0)
+    near, far = applied(sweep, scale, near, far, (LAST_BAND,), at, gains, total, plane)
+    lane = lane_ids(ROWS)
+    result = pltpu.roll(jnp.where(lane < REACH, far, near), LANES - REACH, 1) * -STEP_SIZE
     increment[...] = result
     for target in range(GROUPS):
         spread_copies[target] = result
@@ -620,24 +709,31 @@
     send_rim, got_mid = lax.optimization_barrier((send_rim, got_mid))
     got_rim = exchanged(send_rim, both)
     place = jnp.stack([lax.axis_index("tile"), lax.axis_index(both)]).astype(jnp.int32)
+    tables = [pl.BlockSpec(memory_space=pltpu.SMEM)] * 3
+    held = pltpu.VMEM((SLOTS, TALL, LANES), F32)
+    work = [
+        held, held, held, pltpu.VMEM((4, TALL, LANES), F32), pltpu.VMEM((2, TALL, LANES), F32)
+    ]
+    shifts = [pltpu.VMEM((2 * RADIUS + 1, DEEP, LANES), F32)] * (2 * COPIES)
+    handed = pl.pallas_call(
+        early_kernel,
+        out_shape=array(SPREAD_ROWS + SHARED * TALL, LANES),
+        in_specs=tables + on_vmem(2),
+        out_specs=pl.BlockSpec(memory_space=pltpu.VMEM),
+        scratch_shapes=work + shifts,
+        compiler_params=params,
+        cost_estimate=cost,
+        name="early",
+    )(place, stencil_offsets, stencil_weights, got_mid, fields_tall)
     increment, copies = pl.pallas_call(
         analysis_kernel,
         out_shape=[array(ROWS, LANES), array(GROUPS, ROWS, LANES)],
-        in_specs=[pl.BlockSpec(memory_space=pltpu.SMEM)] * 3 + on_vmem(3),
+        in_specs=tables + on_vmem(2),
         out_specs=on_vmem(2),
-        scratch_shapes=[
-            pltpu.VMEM((GROUPS, SLOTS, TALL, LANES), F32),
-            pltpu.VMEM((SLOTS, TALL, LANES), F32),
-            pltpu.VMEM((SLOTS, TALL, LANES), F32),
-            pltpu.VMEM((SLOTS, DEEP, LANES), F32),
-            pltpu.VMEM((SLOTS, TALL, LANES), F32),
-            pltpu.VMEM((4, TALL, LANES), F32),
-            pltpu.VMEM((2, TALL, LANES), F32),
-        ]
-        + [pltpu.VMEM((2 * RADIUS + 1, DEEP, LANES), F32)] * (2 * COPIES),
+        scratch_shapes=[pltpu.VMEM((GROUPS, SLOTS, TALL, LANES), F32)] + work + shifts,
         compiler_params=params,
         name="analysis",
-    )(place, stencil_offsets, stencil_weights, got_mid, got_rim, fields_tall)
+    )(place, stencil_offsets, stencil_weights, got_rim, handed)
     increments = lax.all_to_all(copies, both, 0, 0, tiled=True)
     analysis = pl.pallas_call(
         recentre_kernel,

time: 93.8 us -> 92.6 us (0.987)
  the two profiles are of different devices: /device:TPU:64 before, /device:TPU:192 now
where the time goes in v3:
time: 92.6 us; the launch traced here: 92.1 us
  Pallas kernels  39.9 us (43%)
  waiting for transfers between devices  26.5 us (29%)
  starting transfers between devices  15.3 us (17%)
  blocking collectives  8.79 us (9%)
    all_to_all x2, waiting for transfers between devices, exchanged(): return lax.all_to_all(flat, axes, 0, 0, tiled=True).reshape(blocks.shape)  25.3 us
    pallas_call x1, Pallas kernels, on_device(): pl.pallas_call(analysis_kernel, out_shape=[array(ROWS, LANES), array(GROU...  16.2 us
    all_to_all x2, starting transfers between devices, exchanged(): return lax.all_to_all(flat, axes, 0, 0, tiled=True).reshape(blocks.shape)  9.7 us
    all_to_all x1, blocking collectives, on_device(): increments = lax.all_to_all(copies, both, 0, 0, tiled=True)  8.79 us
    pallas_call x1, Pallas kernels, on_device(): pl.pallas_call(outer_kernel, out_shape=[array(LOCAL, GROUPS, 2 * keep, LA...  7.54 us
    pallas_call x1, Pallas kernels, on_device(): pl.pallas_call(inner_kernel, out_shape=[array(LOCAL, GROUPS, MID, LANES),...  6.2 us
    pallas_call x1, Pallas kernels, on_device(): pl.pallas_call(early_kernel, out_shape=array(SPREAD_ROWS + SHARED * TALL,...  6.12 us
    ppermute x1, starting transfers between devices, on_device(): below = lax.ppermute(up, 'tile', [(i + 1, i) for i in range(tiles - 1)])  3.64 us
  transfers between devices with their start and end apart: 4, of which 3 were waited for; matrix products, arithmetic and copies ran while one was open for 0% of the time, Pallas kernels for 22%

profile of v3, /device:TPU:192, one launch (start us, length us, event | category | flops | bytes accessed | tf_op | source)
XLA Modules:
  0.0 92.1 jit_solution(2257976321918637725)
XLA Ops:
  0.6 2.6 %messages.1 = (f32[8,136,128]{2,1,0:T(8,128)}, f32[8,136,128]{2,1,0:T(8,128)}, f32[2,32,128]{2,1,0:T(8,128)}) custom-call(f32[10,32,1024]{2,1,0:T(8,128)} %members.5, f32[32,1024]{1,0:T(8,128)} %courant_x.5, f32[32,1024]{1,0:T(8,128)} %courant_y.5, s32[1,1,1024]{2,1,0:T(1,128)} %cell.1, f32[1,1,1024]{2,1,0:T(1,128)} %innov.1, f32[1,1,1024]{2,1,0:T(1,128)} %weight.1), custom_call_target="tpu_custom_call" | custom-call | tf_op jit(solution)/shard_map/messages/pallas_call | solution.py:659
  3.2 1.9 %collective-permute-start = (f32[8,136,128]{2,1,0:T(8,128)}, f32[8,136,128]{2,1,0:T(8,128)S(1)}, u32[]{:S(2)}, u32[]{:S(2)}) collective-permute-start(f32[8,136,128]{2,1,0:T(8,128)} %get-tuple-element.20), channel_id=1, source_target_pairs={{0,2},{2,4},{4,6},{6,8},{8,10},{10,12},{12,14},{14,16},{16,18},{18... | collective-permute-start | bytes 1671176 | tf_op jit(solution)/shard_map/ppermute | solution.py:675
  5.1 3.6 %collective-permute-start.1 = (f32[8,136,128]{2,1,0:T(8,128)}, f32[8,136,128]{2,1,0:T(8,128)S(1)}, u32[]{:S(2)}, u32[]{:S(2)}) collective-permute-start(f32[8,136,128]{2,1,0:T(8,128)} %get-tuple-element.21), channel_id=1, source_target_pairs={{2,0},{4,2},{6,4},{8,6},{10,8},{12,10},{14,12},{16,14},{18,16},{20... | collective-permute-start | bytes 1671176 | tf_op jit(solution)/shard_map/ppermute | solution.py:676
  8.8 6.2 %inner.1 = (f32[10,8,24,128]{3,2,1,0:T(8,128)}, f32[8,12,24,128]{3,2,1,0:T(8,128)}) custom-call(f32[10,32,1024]{2,1,0:T(8,128)} %members.5, f32[32,1024]{1,0:T(8,128)} %courant_x.5, f32[32,1024]{1,0:T(8,128)} %courant_y.5, f32[2,32,128]{2,1,0:T(8,128)} %get-tuple-element.17.fields), custom_call_target="tpu_custom_call" | custom-call | flops 10000000 | bytes 60000000 | tf_op jit(solution)/shard_map/inner/pallas_call | solution.py:677
  15.0 0.0 collective-permute-done.above
  15.0 0.0 copy-start.4
  15.0 1.1 %collective-permute-done.1.below = f32[8,136,128]{2,1,0:T(8,128)S(1)} collective-permute-done((f32[8,136,128]{2,1,0:T(8,128)}, f32[8,136,128]{2,1,0:T(8,128)S(1)}, u32[]{:S(2)}, u32[]{:S(2)}) %collective-permute-start.1) | collective-permute-done | bytes 557088 | tf_op jit(solution)/shard_map/ppermute | solution.py:676
  16.1 0.0 copy-start.5
  16.1 0.0 copy-done.4
  16.1 0.8 copy-done.5
  16.9 5.3 %all-to-all-start = ((f32[8,288,128]{2,1,0:T(8,128)}), f32[8,288,128]{2,1,0:T(8,128)S(1)}, u32[]{:S(2)}, u32[]{:S(2)}) async-start(f32[8,288,128]{2,1,0:T(8,128)} %bitcast.8), calls=%async_computation | async-start | bytes 2359296 | tf_op jit(solution)/shard_map/all_to_all | solution.py:751
  22.2 7.5 %outer.1 = (f32[10,8,8,128]{3,2,1,0:T(8,128)}, f32[8,12,24,128]{3,2,1,0:T(8,128)}, f32[2,48,128]{2,1,0:T(8,128)}) custom-call(f32[10,32,1024]{2,1,0:T(8,128)} %members.5, f32[32,1024]{1,0:T(8,128)} %courant_x.5, f32[32,1024]{1,0:T(8,128)} %courant_y.5, f32[8,136,128]{2,1,0:T(8,128)} %copy-done.4, f32[8,136,128]{2,1,0:T(8,128)} %copy-done.5, ...), custom_call_target="tpu_custom_call" | custom-call | flops 10000000 | bytes 60000000 | tf_op jit(solution)/shard_map/outer/pallas_call | solution.py:689
  29.8 12.7 %all-to-all-done = f32[8,288,128]{2,1,0:T(8,128)S(1)} async-done(((f32[8,288,128]{2,1,0:T(8,128)}), f32[8,288,128]{2,1,0:T(8,128)S(1)}, u32[]{:S(2)}, u32[]{:S(2)}) %all-to-all-start) | async-done | bytes 1179680 | tf_op jit(solution)/shard_map/all_to_all | solution.py:751
  42.5 0.0 copy-start.6
  42.5 0.0 copy-start.2
  42.5 0.0 copy-start.3
  42.5 4.4 %all-to-all-start.1 = ((f32[8,288,128]{2,1,0:T(8,128)}), f32[8,288,128]{2,1,0:T(8,128)}, u32[]{:S(2)}, u32[]{:S(2)}) async-start(f32[8,288,128]{2,1,0:T(8,128)} %bitcast.7), calls=%async_computation.1 | async-start | bytes 2359296 | tf_op jit(solution)/shard_map/all_to_all | solution.py:751
  46.9 0.0 copy-done.6
  46.9 0.1 copy.11.offsets
  47.0 0.1 pad_add_fusion.place
  47.1 0.0 copy-done.2
  47.1 0.0 copy-done.3
  47.1 6.1 %early.1.handed = f32[3120,128]{1,0:T(8,128)S(1)} custom-call(s32[2]{0:T(128)S(1)} %pad_add_fusion.place, s32[9,2]{1,0:T(8,128)S(1)} %copy.11.offsets, f32[9]{0:T(128)S(1)} %copy-done.3, f32[8,12,24,128]{3,2,1,0:T(8,128)S(1)} %bitcast.6, f32[2,48,128]{2,1,0:T(8,128)S(1)} %copy-done.2), custom_call_target="tpu_custom_call" | custom-call | flops 10000000 | bytes 60000000 | tf_op jit(solution)/shard_map/early/pallas_call | solution.py:718
  53.2 12.6 %all-to-all-done.1 = f32[8,288,128]{2,1,0:T(8,128)} async-done(((f32[8,288,128]{2,1,0:T(8,128)}), f32[8,288,128]{2,1,0:T(8,128)}, u32[]{:S(2)}, u32[]{:S(2)}) %all-to-all-start.1) | async-done | bytes 1179680 | tf_op jit(solution)/shard_map/all_to_all | solution.py:751
  65.8 0.0 copy-start
  65.8 0.0 copy-start.1
  65.8 16.2 %analysis.1 = (f32[32,128]{1,0:T(8,128)}, f32[8,32,128]{2,1,0:T(8,128)S(1)}) custom-call(s32[2]{0:T(128)S(1)} %pad_add_fusion.place, s32[9,2]{1,0:T(8,128)S(1)} %copy.11.offsets, f32[9]{0:T(128)S(1)} %copy-done.3, f32[8,12,24,128]{3,2,1,0:T(8,128)} %bitcast.5.got, f32[3120,128]{1,0:T(8,128)S(1)} %early.1.handed), custom_call_target="tpu_custom_call" | custom-call | tf_op jit(solution)/shard_map/analysis/pallas_call | solution.py:728
  82.1 8.8 %all_to_all.15.increments = f32[8,32,128]{2,1,0:T(8,128)S(1)} all-to-all(f32[8,32,128]{2,1,0:T(8,128)S(1)} %get-tuple-element.30), channel_id=1, replica_groups=mesh['member'=4,'tile'=32,'grp'=2] {'member','grp'}, dimensions={0} | all-to-all | bytes 262144 | tf_op jit(solution)/shard_map/all_to_all | solution.py:737
  90.9 0.0 copy-done
  90.9 0.0 copy-done.1
  90.9 1.3 %recentre.1 = f32[10,32,1024]{2,1,0:T(8,128)} custom-call(f32[10,8,24,128]{3,2,1,0:T(8,128)S(1)} %copy-done, f32[10,8,8,128]{3,2,1,0:T(8,128)S(1)} %copy-done.1, f32[8,32,128]{2,1,0:T(8,128)S(1)} %all_to_all.15.increments), custom_call_target="tpu_custom_call" | custom-call | tf_op jit(solution)/shard_map/recentre/pallas_call | solution.py:738
Async XLA Ops:
  3.2 11.8 %collective-permute-start = (f32[8,136,128]{2,1,0:T(8,128)}, f32[8,136,128]{2,1,0:T(8,128)S(1)}, u32[]{:S(2)}, u32[]{:S(2)}) collective-permute-start(f32[8,136,128]{2,1,0:T(8,128)} %get-tuple-element.20), channel_id=1, source_target_pairs={{0,2},{2,4},{4,6},{6,8},{8,10},{10,12},{12,14},{14,16},{16,18},{18... | collective-permute-start | bytes 1671176 | tf_op jit(solution)/shard_map/ppermute | solution.py:675
  5.1 11.0 %collective-permute-start.1 = (f32[8,136,128]{2,1,0:T(8,128)}, f32[8,136,128]{2,1,0:T(8,128)S(1)}, u32[]{:S(2)}, u32[]{:S(2)}) collective-permute-start(f32[8,136,128]{2,1,0:T(8,128)} %get-tuple-element.21), channel_id=1, source_target_pairs={{2,0},{4,2},{6,4},{8,6},{10,8},{12,10},{14,12},{16,14},{18,16},{20... | collective-permute-start | bytes 1671176 | tf_op jit(solution)/shard_map/ppermute | solution.py:676
  15.0 1.1 %copy-start.4 = (f32[8,136,128]{2,1,0:T(8,128)}, f32[8,136,128]{2,1,0:T(8,128)S(1)}, u32[]{:S(2)}) copy-start(f32[8,136,128]{2,1,0:T(8,128)S(1)} %collective-permute-done.above) | copy-start | bytes 1671172
  16.1 0.8 copy-start.5
  16.9 25.6 %all-to-all-start = ((f32[8,288,128]{2,1,0:T(8,128)}), f32[8,288,128]{2,1,0:T(8,128)S(1)}, u32[]{:S(2)}, u32[]{:S(2)}) async-start(f32[8,288,128]{2,1,0:T(8,128)} %bitcast.8), calls=%async_computation | async-start | bytes 2359296 | tf_op jit(solution)/shard_map/all_to_all | solution.py:751
  42.5 4.4 %copy-start.6 = (s32[9,2]{0,1:T(2,128)S(1)}, s32[9,2]{0,1:T(2,128)}, u32[]{:S(2)}) copy-start(s32[9,2]{0,1:T(2,128)} %param.14) | copy-start | bytes 220
  42.5 4.6 %copy-start.2 = (f32[2,48,128]{2,1,0:T(8,128)S(1)}, f32[2,48,128]{2,1,0:T(8,128)}, u32[]{:S(2)}) copy-start(f32[2,48,128]{2,1,0:T(8,128)} %get-tuple-element.29.fields) | copy-start | bytes 147460
  42.5 4.6 %copy-start.3 = (f32[9]{0:T(128)S(1)}, f32[9]{0:T(128)}, u32[]{:S(2)}) copy-start(f32[9]{0:T(128)} %weights.3) | copy-start | bytes 112
  42.5 23.4 %all-to-all-start.1 = ((f32[8,288,128]{2,1,0:T(8,128)}), f32[8,288,128]{2,1,0:T(8,128)}, u32[]{:S(2)}, u32[]{:S(2)}) async-start(f32[8,288,128]{2,1,0:T(8,128)} %bitcast.7), calls=%async_computation.1 | async-start | bytes 2359296 | tf_op jit(solution)/shard_map/all_to_all | solution.py:751
  65.8 25.0 %copy-start = (f32[10,8,24,128]{3,2,1,0:T(8,128)S(1)}, f32[10,8,24,128]{3,2,1,0:T(8,128)}, u32[]{:S(2)}) copy-start(f32[10,8,24,128]{3,2,1,0:T(8,128)} %get-tuple-element.18.middle) | copy-start | bytes 2949124
  65.8 25.0 %copy-start.1 = (f32[10,8,8,128]{3,2,1,0:T(8,128)S(1)}, f32[10,8,8,128]{3,2,1,0:T(8,128)}, u32[]{:S(2)}) copy-start(f32[10,8,8,128]{3,2,1,0:T(8,128)} %get-tuple-element.24.rim) | copy-start | bytes 983044

commit v4 on v3

--- a/solution.py
+++ b/solution.py
@@ -684,7 +684,7 @@
         cost_estimate=cost,
         name="inner",
     )(members, courant_x, courant_y, fields)
-    send_mid, above, below = lax.optimization_barrier((send_mid, above, below))
+    send_mid, _ = lax.optimization_barrier((send_mid, above))
     got_mid = exchanged(send_mid, both)
     rim, send_rim, fields_tall = pl.pallas_call(
         outer_kernel,

time: 92.6 us -> 90.9 us (0.982)
  the two profiles are of different devices: /device:TPU:192 before, /device:TPU:16 now
where the time goes in v4:
time: 90.9 us; the launch traced here: 90.4 us
  Pallas kernels  40.3 us (44%)
  waiting for transfers between devices  24.2 us (27%)
  starting transfers between devices  13.9 us (15%)
  blocking collectives  9.49 us (10%)
  local copies, waits for them, and re-layouts  1.75 us (2%)
    pallas_call x1, Pallas kernels, on_device(): pl.pallas_call(analysis_kernel, out_shape=[array(ROWS, LANES), array(GROU...  16.4 us
    ppermute x1, waiting for transfers between devices, on_device(): below = lax.ppermute(up, 'tile', [(i + 1, i) for i in range(tiles - 1)])  11.7 us
    all_to_all x2, starting transfers between devices, exchanged(): return lax.all_to_all(flat, axes, 0, 0, tiled=True).reshape(blocks.shape)  10 us
    all_to_all x1, blocking collectives, on_device(): increments = lax.all_to_all(copies, both, 0, 0, tiled=True)  9.49 us
    pallas_call x1, Pallas kernels, on_device(): pl.pallas_call(outer_kernel, out_shape=[array(LOCAL, GROUPS, 2 * keep, LA...  7.56 us
    ppermute x1, waiting for transfers between devices, on_device(): above = lax.ppermute(down, 'tile', [(i, i + 1) for i in range(tiles - 1)])  6.54 us
    pallas_call x1, Pallas kernels, on_device(): pl.pallas_call(early_kernel, out_shape=array(SPREAD_ROWS + SHARED * TALL,...  6.29 us
    pallas_call x1, Pallas kernels, on_device(): pl.pallas_call(inner_kernel, out_shape=[array(LOCAL, GROUPS, MID, LANES),...  6.2 us
  transfers between devices with their start and end apart: 4, of which 3 were waited for; matrix products, arithmetic and copies ran while one was open for 0% of the time, Pallas kernels for 22%

profile of v4, /device:TPU:16, one launch (start us, length us, event | category | flops | bytes accessed | tf_op | source)
XLA Modules:
  0.0 90.4 jit_solution(16933865292518056188)
XLA Ops:
  0.6 2.6 %messages.1 = (f32[8,136,128]{2,1,0:T(8,128)}, f32[8,136,128]{2,1,0:T(8,128)}, f32[2,32,128]{2,1,0:T(8,128)}) custom-call(f32[10,32,1024]{2,1,0:T(8,128)} %members.5, f32[32,1024]{1,0:T(8,128)} %courant_x.5, f32[32,1024]{1,0:T(8,128)} %courant_y.5, s32[1,1,1024]{2,1,0:T(1,128)} %cell.1, f32[1,1,1024]{2,1,0:T(1,128)} %innov.1, f32[1,1,1024]{2,1,0:T(1,128)} %weight.1), custom_call_target="tpu_custom_call" | custom-call | tf_op jit(solution)/shard_map/messages/pallas_call | solution.py:659
  3.2 1.9 %collective-permute-start = (f32[8,136,128]{2,1,0:T(8,128)}, f32[8,136,128]{2,1,0:T(8,128)S(1)}, u32[]{:S(2)}, u32[]{:S(2)}) collective-permute-start(f32[8,136,128]{2,1,0:T(8,128)} %get-tuple-element.17), channel_id=1, source_target_pairs={{0,2},{2,4},{4,6},{6,8},{8,10},{10,12},{12,14},{14,16},{16,18},{18... | collective-permute-start | bytes 1671176 | tf_op jit(solution)/shard_map/ppermute | solution.py:675
  5.1 6.2 %inner.1 = (f32[10,8,24,128]{3,2,1,0:T(8,128)}, f32[8,12,24,128]{3,2,1,0:T(8,128)}) custom-call(f32[10,32,1024]{2,1,0:T(8,128)} %members.5, f32[32,1024]{1,0:T(8,128)} %courant_x.5, f32[32,1024]{1,0:T(8,128)} %courant_y.5, f32[2,32,128]{2,1,0:T(8,128)} %get-tuple-element.15.fields), custom_call_target="tpu_custom_call" | custom-call | flops 10000000 | bytes 60000000 | tf_op jit(solution)/shard_map/inner/pallas_call | solution.py:677
  11.3 6.5 %collective-permute-done.above = f32[8,136,128]{2,1,0:T(8,128)S(1)} collective-permute-done((f32[8,136,128]{2,1,0:T(8,128)}, f32[8,136,128]{2,1,0:T(8,128)S(1)}, u32[]{:S(2)}, u32[]{:S(2)}) %collective-permute-start) | collective-permute-done | bytes 557088 | tf_op jit(solution)/shard_map/ppermute | solution.py:675
  17.9 0.0 copy-start.4
  17.9 0.0 copy-start.7
  17.9 0.8 copy-done.4
  18.7 5.6 %all-to-all-start = ((f32[8,288,128]{2,1,0:T(8,128)}), f32[8,288,128]{2,1,0:T(8,128)S(1)}, u32[]{:S(2)}, u32[]{:S(2)}) async-start(f32[8,288,128]{2,1,0:T(8,128)} %bitcast.8), calls=%async_computation | async-start | bytes 2359296 | tf_op jit(solution)/shard_map/all_to_all | solution.py:751
  24.3 0.0 copy-done.7
  24.3 1.9 %collective-permute-start.1 = (f32[8,136,128]{2,1,0:T(8,128)S(1)}, f32[8,136,128]{2,1,0:T(8,128)S(1)}, u32[]{:S(2)}, u32[]{:S(2)}) collective-permute-start(f32[8,136,128]{2,1,0:T(8,128)S(1)} %copy-done.7), channel_id=1, source_target_pairs={{2,0},{4,2},{6,4},{8,6},{10,8},{12,10},{14,12},{16,14},{18,16},{20... | collective-permute-start | bytes 1671176 | tf_op jit(solution)/shard_map/ppermute | solution.py:676
  26.3 11.7 %collective-permute-done.1.below = f32[8,136,128]{2,1,0:T(8,128)S(1)} collective-permute-done((f32[8,136,128]{2,1,0:T(8,128)S(1)}, f32[8,136,128]{2,1,0:T(8,128)S(1)}, u32[]{:S(2)}, u32[]{:S(2)}) %collective-permute-start.1) | collective-permute-done | bytes 557088 | tf_op jit(solution)/shard_map/ppermute | solution.py:676
  38.0 0.0 copy-start.5
  38.0 0.8 copy-done.5
  38.8 7.6 %outer.1 = (f32[10,8,8,128]{3,2,1,0:T(8,128)}, f32[8,12,24,128]{3,2,1,0:T(8,128)}, f32[2,48,128]{2,1,0:T(8,128)}) custom-call(f32[10,32,1024]{2,1,0:T(8,128)} %members.5, f32[32,1024]{1,0:T(8,128)} %courant_x.5, f32[32,1024]{1,0:T(8,128)} %courant_y.5, f32[8,136,128]{2,1,0:T(8,128)} %copy-done.4, f32[8,136,128]{2,1,0:T(8,128)} %copy-done.5, ...), custom_call_target="tpu_custom_call" | custom-call | flops 10000000 | bytes 60000000 | tf_op jit(solution)/shard_map/outer/pallas_call | solution.py:689
  46.3 0.0 all-to-all-done
  46.3 0.0 copy-start.6
  46.4 0.0 copy-start.2
  46.4 0.0 copy-start.3
  46.4 4.4 %all-to-all-start.1 = ((f32[8,288,128]{2,1,0:T(8,128)}), f32[8,288,128]{2,1,0:T(8,128)}, u32[]{:S(2)}, u32[]{:S(2)}) async-start(f32[8,288,128]{2,1,0:T(8,128)} %bitcast.7), calls=%async_computation.1 | async-start | bytes 2359296 | tf_op jit(solution)/shard_map/all_to_all | solution.py:751
  50.8 0.0 copy-done.6
  50.8 0.1 copy.11.offsets
  50.9 0.1 pad_add_fusion.place
  51.0 0.0 copy-done.2
  51.0 0.0 copy-done.3
  51.0 6.3 %early.1.handed = f32[3120,128]{1,0:T(8,128)S(1)} custom-call(s32[2]{0:T(128)S(1)} %pad_add_fusion.place, s32[9,2]{1,0:T(8,128)S(1)} %copy.11.offsets, f32[9]{0:T(128)S(1)} %copy-done.3, f32[8,12,24,128]{3,2,1,0:T(8,128)S(1)} %bitcast.6, f32[2,48,128]{2,1,0:T(8,128)S(1)} %copy-done.2), custom_call_target="tpu_custom_call" | custom-call | flops 10000000 | bytes 60000000 | tf_op jit(solution)/shard_map/early/pallas_call | solution.py:718
  57.3 6.0 %all-to-all-done.1 = f32[8,288,128]{2,1,0:T(8,128)} async-done(((f32[8,288,128]{2,1,0:T(8,128)}), f32[8,288,128]{2,1,0:T(8,128)}, u32[]{:S(2)}, u32[]{:S(2)}) %all-to-all-start.1) | async-done | bytes 1179680 | tf_op jit(solution)/shard_map/all_to_all | solution.py:751
  63.2 0.0 copy-start
  63.2 0.0 copy-start.1
  63.2 16.4 %analysis.1 = (f32[32,128]{1,0:T(8,128)}, f32[8,32,128]{2,1,0:T(8,128)S(1)}) custom-call(s32[2]{0:T(128)S(1)} %pad_add_fusion.place, s32[9,2]{1,0:T(8,128)S(1)} %copy.11.offsets, f32[9]{0:T(128)S(1)} %copy-done.3, f32[8,12,24,128]{3,2,1,0:T(8,128)} %bitcast.5.got, f32[3120,128]{1,0:T(8,128)S(1)} %early.1.handed), custom_call_target="tpu_custom_call" | custom-call | tf_op jit(solution)/shard_map/analysis/pallas_call | solution.py:728
  79.6 9.5 %all_to_all.15.increments = f32[8,32,128]{2,1,0:T(8,128)S(1)} all-to-all(f32[8,32,128]{2,1,0:T(8,128)S(1)} %get-tuple-element.26), channel_id=1, replica_groups=mesh['member'=4,'tile'=32,'grp'=2] {'member','grp'}, dimensions={0} | all-to-all | bytes 262144 | tf_op jit(solution)/shard_map/all_to_all | solution.py:737
  89.1 0.0 copy-done
  89.1 0.0 copy-done.1
  89.1 1.3 %recentre.1 = f32[10,32,1024]{2,1,0:T(8,128)} custom-call(f32[10,8,24,128]{3,2,1,0:T(8,128)S(1)} %copy-done, f32[10,8,8,128]{3,2,1,0:T(8,128)S(1)} %copy-done.1, f32[8,32,128]{2,1,0:T(8,128)S(1)} %all_to_all.15.increments), custom_call_target="tpu_custom_call" | custom-call | tf_op jit(solution)/shard_map/recentre/pallas_call | solution.py:738
Async XLA Ops:
  3.2 14.7 %collective-permute-start = (f32[8,136,128]{2,1,0:T(8,128)}, f32[8,136,128]{2,1,0:T(8,128)S(1)}, u32[]{:S(2)}, u32[]{:S(2)}) collective-permute-start(f32[8,136,128]{2,1,0:T(8,128)} %get-tuple-element.17), channel_id=1, source_target_pairs={{0,2},{2,4},{4,6},{6,8},{8,10},{10,12},{12,14},{14,16},{16,18},{18... | collective-permute-start | bytes 1671176 | tf_op jit(solution)/shard_map/ppermute | solution.py:675
  17.9 0.8 copy-start.4
  17.9 6.5 %copy-start.7 = (f32[8,136,128]{2,1,0:T(8,128)S(1)}, f32[8,136,128]{2,1,0:T(8,128)}, u32[]{:S(2)}) copy-start(f32[8,136,128]{2,1,0:T(8,128)} %get-tuple-element.18) | copy-start | bytes 1671172
  18.7 27.6 %all-to-all-start = ((f32[8,288,128]{2,1,0:T(8,128)}), f32[8,288,128]{2,1,0:T(8,128)S(1)}, u32[]{:S(2)}, u32[]{:S(2)}) async-start(f32[8,288,128]{2,1,0:T(8,128)} %bitcast.8), calls=%async_computation | async-start | bytes 2359296 | tf_op jit(solution)/shard_map/all_to_all | solution.py:751
  24.3 13.6 %collective-permute-start.1 = (f32[8,136,128]{2,1,0:T(8,128)S(1)}, f32[8,136,128]{2,1,0:T(8,128)S(1)}, u32[]{:S(2)}, u32[]{:S(2)}) collective-permute-start(f32[8,136,128]{2,1,0:T(8,128)S(1)} %copy-done.7), channel_id=1, source_target_pairs={{2,0},{4,2},{6,4},{8,6},{10,8},{12,10},{14,12},{16,14},{18,16},{20... | collective-permute-start | bytes 1671176 | tf_op jit(solution)/shard_map/ppermute | solution.py:676
  38.0 0.8 copy-start.5
  46.3 4.4 %copy-start.6 = (s32[9,2]{0,1:T(2,128)S(1)}, s32[9,2]{0,1:T(2,128)}, u32[]{:S(2)}) copy-start(s32[9,2]{0,1:T(2,128)} %param.14) | copy-start | bytes 220
  46.4 4.6 %copy-start.2 = (f32[2,48,128]{2,1,0:T(8,128)S(1)}, f32[2,48,128]{2,1,0:T(8,128)}, u32[]{:S(2)}) copy-start(f32[2,48,128]{2,1,0:T(8,128)} %get-tuple-element.25.fields) | copy-start | bytes 147460
  46.4 4.6 %copy-start.3 = (f32[9]{0:T(128)S(1)}, f32[9]{0:T(128)}, u32[]{:S(2)}) copy-start(f32[9]{0:T(128)} %weights.3) | copy-start | bytes 112
  46.4 16.9 %all-to-all-start.1 = ((f32[8,288,128]{2,1,0:T(8,128)}), f32[8,288,128]{2,1,0:T(8,128)}, u32[]{:S(2)}, u32[]{:S(2)}) async-start(f32[8,288,128]{2,1,0:T(8,128)} %bitcast.7), calls=%async_computation.1 | async-start | bytes 2359296 | tf_op jit(solution)/shard_map/all_to_all | solution.py:751
  63.2 25.9 %copy-start = (f32[10,8,24,128]{3,2,1,0:T(8,128)S(1)}, f32[10,8,24,128]{3,2,1,0:T(8,128)}, u32[]{:S(2)}) copy-start(f32[10,8,24,128]{3,2,1,0:T(8,128)} %get-tuple-element.16.middle) | copy-start | bytes 2949124
  63.2 25.9 %copy-start.1 = (f32[10,8,8,128]{3,2,1,0:T(8,128)S(1)}, f32[10,8,8,128]{3,2,1,0:T(8,128)}, u32[]{:S(2)}) copy-start(f32[10,8,8,128]{3,2,1,0:T(8,128)} %get-tuple-element.19.rim) | copy-start | bytes 983044

commit v5 on v4

--- a/solution.py
+++ b/solution.py
@@ -107,15 +107,15 @@
     return plan
 
 
-def pack(final, fields, rolled, blocks, send, sems):
+def pack(final, fields, rows, rolled, blocks, send, sems):
     @pl.loop(0, GROUPS, unroll=8)
     def _(block):
         for member in range(LOCAL):
             shift = (member * WIDE + REACH) % LANES
-            value = final[member, block + 1, 0:MID, :]
+            value = final[member, block + 1, 0:rows, :]
             rolled[member, block + 1] = pltpu.roll(value, shift, 1) if shift else value
 
-    lane = lane_ids(MID)
+    lane = lane_ids(rows)
     ends = jnp.where(
         lane < SPARE + 2 * REACH,
         pltpu.roll(fields[0], SPARE + REACH, 1),
@@ -133,34 +133,16 @@
                     value = part
                 else:
                     value = jnp.where((lane >= low) & (lane < high), part, value)
-            blocks[block, slot] = value
-        pltpu.make_async_copy(blocks.at[block], send.at[block], sems.at[block]).start()
+            blocks[block, slot * rows : (slot + 1) * rows, :] = value
+        pltpu.make_async_copy(blocks.at[block], send(block), sems.at[block]).start()
 
 
 def finish_pack(blocks, send, sems):
     for block in range(GROUPS):
-        pltpu.make_async_copy(blocks.at[block], send.at[block], sems.at[block]).wait()
-
-
-def message_kernel(
-    members, courant_x, courant_y, cell, innov, weight,
-    up, down, fields, own, courants, cells, values, member_sems, sems,
-):
-    small = [
-        pltpu.make_async_copy(cell, cells, sems.at[0]),
-        pltpu.make_async_copy(innov, values.at[0], sems.at[1]),
-        pltpu.make_async_copy(weight, values.at[1], sems.at[2]),
-    ]
-    large = [
-        pltpu.make_async_copy(members, own, member_sems.at[0]),
-        pltpu.make_async_copy(courant_x, courants.at[0], member_sems.at[1]),
-        pltpu.make_async_copy(courant_y, courants.at[1], member_sems.at[2]),
-    ]
-    for copy in small + large:
-        copy.start()
-    for copy in small:
-        copy.wait()
-
+        pltpu.make_async_copy(blocks.at[block], send(block), sems.at[block]).wait()
+
+
+def observed(cells, values, fields):
     row_hit = lax.broadcasted_iota(jnp.int32, (ROWS, 1024), 0) == lax.shift_right_logical(cells[0], 7)
     col_hit = lax.broadcasted_iota(jnp.int32, (LANES, 1024), 0) == lax.bitwise_and(
         cells[0], LANES - 1
@@ -178,6 +160,20 @@
             + sums[base + ROWS : base + 2 * ROWS]
             + sums[base + 2 * ROWS : base + 3 * ROWS]
         )
+
+
+def set_messages(members, courants, fields, up, down):
+    @pl.loop(0, GROUPS)
+    def _(block):
+        for field in range(LOCAL + 2):
+            span = slice(field * EDGE, (field + 1) * EDGE)
+            for target, low in ((up, TOP), (down, TOP + ROWS - EDGE)):
+                rows = slice(low, low + EDGE)
+                if field < LOCAL:
+                    target[block, span, :] = members[field, block + 1, rows, :]
+                else:
+                    target[block, span, :] = courants[field - LOCAL, block, rows, :]
+
     base = (LOCAL + 2) * EDGE
     for row in range(REACH):
         for kind in range(2):
@@ -187,16 +183,6 @@
             ]
         up[row, base + 2 : HALO, :] = jnp.zeros((HALO - base - 2, LANES), F32)
         down[row, base + 2 : HALO, :] = jnp.zeros((HALO - base - 2, LANES), F32)
-    for copy in large:
-        copy.wait()
-    for field in range(LOCAL + 2):
-        span = slice(field * EDGE, (field + 1) * EDGE)
-        source = own.at[field] if field < LOCAL else courants.at[field - LOCAL]
-        first, last = source[0:EDGE, :], source[ROWS - EDGE : ROWS, :]
-        for block in range(GROUPS):
-            lanes = slice(block * LANES, (block + 1) * LANES)
-            up[block, span, :] = first[:, lanes]
-            down[block, span, :] = last[:, lanes]
 
 
 TOP = 16
@@ -204,8 +190,9 @@
 
 
 def inner_kernel(
-    members, courant_x, courant_y, fields, out, send,
-    old, new, courants, coefs, rolled, final, blocks, member_sems, wind_sems, sems,
+    members, courant_x, courant_y, cell, innov, weight, up_out, down_out, out, send, fields,
+    old, new, courants, coefs, rolled, final, blocks, cells, values, up, down,
+    member_sems, wind_sems, sems, small_sems,
 ):
     own = slice(TOP, TOP + ROWS)
     large, wind = [], []
@@ -222,14 +209,29 @@
                 members.at[:, :, lanes], old.at[:, block + 1, own, :], member_sems.at[block]
             )
         )
-    for copy in wind + large:
+    small = [
+        pltpu.make_async_copy(cell, cells, small_sems.at[0]),
+        pltpu.make_async_copy(innov, values.at[0], small_sems.at[1]),
+        pltpu.make_async_copy(weight, values.at[1], small_sems.at[2]),
+    ]
+    for copy in small + wind + large:
         copy.start()
     clear_sides((old, new, rolled))
+    for copy in small:
+        copy.wait()
+    observed(cells, values, fields)
     for copy in wind:
         copy.wait()
     set_coefs(courants, coefs, range(TOP, TOP + ROWS, 8))
     for copy in large:
         copy.wait()
+    set_messages(old, courants, fields, up, down)
+    messages = [
+        pltpu.make_async_copy(up, up_out, small_sems.at[0]),
+        pltpu.make_async_copy(down, down_out, small_sems.at[1]),
+    ]
+    for copy in messages:
+        copy.start()
     advance(old, new, coefs, range(TOP, TOP + ROWS, 8))
     advance(new, old, coefs, range(TOP, TOP + ROWS, 8))
     skip = (ROWS - MID) // 2
@@ -237,82 +239,100 @@
     whole = pltpu.make_async_copy(final.at[:, pl.ds(1, GROUPS), pl.ds(0, MID), :], out, sems.at[GROUPS])
     whole.start()
     middle = [fields[kind, skip : skip + MID, :] for kind in range(2)]
-    pack(final, middle, rolled, blocks, send, sems)
-    finish_pack(blocks, send, sems)
-    whole.wait()
-
-
-LOW = 8
-
-
-def outer_kernel(
-    members, courant_x, courant_y, above, below, fields,
-    out, send, fields_tall,
-    old, new, courants, coefs, rolled, final, blocks, rims, member_sems, wind_sems, sems,
+    pack(final, middle, MID, rolled, blocks, lambda block: send.at[block], sems)
+    finish_pack(blocks, lambda block: send.at[block], sems)
+    for copy in messages + [whole]:
+        copy.wait()
+
+
+SIDE = SLOTS * RIM
+SHORT = 32
+
+
+def rim_rows(
+    lower, members, courant_x, courant_y, message, fields, out, send,
+    old, new, courants, coefs, rolled, final, blocks, rim, member_sems, wind_sems, sems,
 ):
-    top, end = slice(TOP, TOP + 8), slice(ROWS - 8 + LOW, ROWS + LOW)
+    own = slice(0, 8) if lower else slice(TOP, TOP + 8)
+    rows = slice(ROWS - 8, ROWS) if lower else slice(0, 8)
+    beside = 8 if lower else TOP - EDGE
     copies = []
     for block in range(GROUPS):
         lanes = slice(block * LANES, (block + 1) * LANES)
-        for part, span in enumerate((top, end)):
-            rows = slice(0, 8) if part == 0 else slice(ROWS - 8, ROWS)
+        copies.append(
+            pltpu.make_async_copy(
+                members.at[:, rows, lanes], old.at[:, block + 1, own, :], member_sems.at[block]
+            )
+        )
+        for kind, source in enumerate((courant_x, courant_y)):
             copies.append(
                 pltpu.make_async_copy(
-                    members.at[:, rows, lanes], old.at[:, block + 1, span, :],
-                    member_sems.at[part, block],
+                    source.at[rows, lanes], courants.at[kind, block, own, :],
+                    wind_sems.at[kind, block],
                 )
             )
-            for kind, source in enumerate((courant_x, courant_y)):
-                copies.append(
-                    pltpu.make_async_copy(
-                        source.at[rows, lanes], courants.at[kind, block, span, :],
-                        wind_sems.at[kind, part, block],
-                    )
-                )
     for copy in copies:
         copy.start()
     clear_sides((old, new, rolled))
-    base = (LOCAL + 2) * EDGE
 
     @pl.loop(0, GROUPS)
     def _(block):
         for field in range(LOCAL + 2):
-            span = slice(field * EDGE, (field + 1) * EDGE)
-            before, after = above[block, span, :], below[block, span, :]
+            value = message[block, field * EDGE : (field + 1) * EDGE, :]
             if field < LOCAL:
-                old[field, block + 1, TOP - EDGE : TOP, :] = before
-                old[field, block + 1, ROWS + LOW : ROWS + LOW + EDGE, :] = after
+                old[field, block + 1, beside : beside + EDGE, :] = value
             else:
-                courants[field - LOCAL, block, TOP - EDGE : TOP, :] = before
-                courants[field - LOCAL, block, ROWS + LOW : ROWS + LOW + EDGE, :] = after
-
+                courants[field - LOCAL, block, beside : beside + EDGE, :] = value
+
+    base, keep = (LOCAL + 2) * EDGE, RIM - REACH
     for kind in range(2):
         for row in range(REACH):
-            fields_tall[kind, row : row + 1, :] = above[row, base + kind : base + kind + 1, :]
-            fields_tall[kind, REACH + ROWS + row : REACH + ROWS + row + 1, :] = below[
-                row, base + kind : base + kind + 1, :
-            ]
-        fields_tall[kind, REACH : REACH + ROWS, :] = fields[kind]
-        rims[kind, 0:RIM, :] = fields_tall[kind, 0:RIM, :]
-        rims[kind, RIM:MID, :] = fields_tall[kind, TALL - RIM : TALL, :]
+            at = row + (keep if lower else 0)
+            rim[kind, at : at + 1, :] = message[row, base + kind : base + kind + 1, :]
+        if lower:
+            rim[kind, 0:keep, :] = fields[kind, ROWS - keep : ROWS, :]
+        else:
+            rim[kind, REACH:RIM, :] = fields[kind, 0:keep, :]
     for copy in copies:
         copy.wait()
-    set_coefs(courants, coefs, range(0, HEIGHT, 8))
-    for step in range(3):
-        high, low = TOP - EDGE + 1 + step, ROWS - 6 + step + LOW
-        starts = (high, high + 8, low, low + 8)
-        if step < 2:
-            pair = (old, new) if step == 0 else (new, old)
-            advance(*pair, coefs, starts)
-        else:
-            advance(old, final, coefs, starts, (0, 8, RIM, RIM + 8))
+    set_coefs(courants, coefs, range(0, SHORT, 8))
+    first = 2 if lower else TOP - EDGE + 1
+    advance(old, new, coefs, (first, first + 8))
+    advance(new, old, coefs, (first + 1, first + 9))
+    advance(old, final, coefs, (first + 2, first + 10), (0, 8))
+    low = 0 if lower else REACH
     whole = pltpu.make_async_copy(
-        final.at[:, pl.ds(1, GROUPS), pl.ds(REACH, 8), :], out, sems.at[GROUPS]
+        final.at[:, pl.ds(1, GROUPS), pl.ds(low, 8), :], out, sems.at[GROUPS]
     )
     whole.start()
-    pack(final, rims, rolled, blocks, send, sems)
-    finish_pack(blocks, send, sems)
+
+    def place(block):
+        return send.at[block, pl.ds(SIDE if lower else 0, SIDE), :]
+
+    pack(final, rim, RIM, rolled, blocks, place, sems)
+    finish_pack(blocks, place, sems)
     whole.wait()
+
+
+def upper_kernel(members, courant_x, courant_y, above, fields, out, send, rim, *rest):
+    work, sems = rest[:-3], rest[-3:]
+    rim_rows(
+        False, members, courant_x, courant_y, above, fields, out, send, *work, rim, *sems
+    )
+
+
+def lower_kernel(
+    members, courant_x, courant_y, below, fields, upper, sent, out, send, fields_tall, *rest
+):
+    del sent
+    work, rim, sems = rest[:-4], rest[-4], rest[-3:]
+    rim_rows(
+        True, members, courant_x, courant_y, below, fields, out, send, *work, rim, *sems
+    )
+    for kind in range(2):
+        fields_tall[kind, 0:RIM, :] = upper[kind]
+        fields_tall[kind, REACH : REACH + ROWS, :] = fields[kind]
+        fields_tall[kind, TALL - RIM : TALL, :] = rim[kind]
 
 
 COPIES = 4
@@ -462,42 +482,51 @@
     return (near + plane[0, 0:rows, :]) * scale, (far + plane[1, 0:rows, :]) * scale
 
 
-def set_spread(got, parts, averages, spread):
+def set_spread(loads, starts, rows, averages, spread):
     count = GROUPS * LOCAL
     deviation = 1.0 / math.sqrt(count - 1)
-    rows = parts[0][2] * len(parts)
-
-    @pl.loop(0, SLOTS)
-    def _(slot):
-        value = got[0, slot]
-        for source in range(1, GROUPS):
-            value = value + got[source, slot]
-        averages[slot, 0:rows, :] = value
-
     lane = lane_ids(rows)
-    near, far = folded(lambda slot: averages[slot, 0:rows, :], lane)
-
-    def store_average(slot, value):
-        averages[slot, 0:rows, :] = value
-
-    spread_out(near / count, far / count, lane, store_average)
-
-    @pl.loop(0, SLOTS)
-    def _(slot):
-        average = averages[slot, 0:rows, :]
-        for source in range(GROUPS):
-            value = (got[source, slot] - average) * deviation
-            for here, there, number in parts:
-                spread[source, slot, here : here + number, :] = value[there : there + number]
-
-
-def block_ends(got, parts, block, ends):
-    for here, there, count in parts:
-        rows = slice(there, there + count)
-        ends[0, here : here + count, :] = got[jnp.maximum(block - 1, 0), SLOTS - 1, rows, :]
-        ends[1, here : here + count, :] = got[
-            jnp.minimum(block + 1, GROUPS - 1), SLOTS - 1, rows, :
-        ]
+    for load, start in zip(loads, starts):
+        span = slice(start, start + rows)
+
+        @pl.loop(0, SLOTS)
+        def _(slot):
+            value = load(0, slot)
+            for source in range(1, GROUPS):
+                value = value + load(source, slot)
+            averages[slot, span, :] = value
+
+        near, far = folded(lambda slot: averages[slot, span, :], lane)
+
+        def store_average(slot, value):
+            averages[slot, span, :] = value
+
+        spread_out(near / count, far / count, lane, store_average)
+
+        @pl.loop(0, SLOTS)
+        def _(slot):
+            average = averages[slot, span, :]
+            for source in range(GROUPS):
+                spread[source, slot, span, :] = (load(source, slot) - average) * deviation
+
+
+def block_ends(loads, starts, rows, block, ends):
+    for load, start in zip(loads, starts):
+        span = slice(start, start + rows)
+        ends[0, span, :] = load(jnp.maximum(block - 1, 0), SLOTS - 1)
+        ends[1, span, :] = load(jnp.minimum(block + 1, GROUPS - 1), SLOTS - 1)
+
+
+def loads_of(got, rows, sides):
+    def load_from(side):
+        base = side * SLOTS * rows
+
+        def load(source, slot):
+            return got[source, pl.ds(base + slot * rows, rows), :]
+
+        return load
+
+    return [load_from(side) for side in range(sides)]
 
 
 def with_margins(own, kind, block, ends, rows):
@@ -531,7 +560,8 @@
     spread, shared = handed_on(handed)
     tile, block = place[0], place[1]
     lane = lane_ids(TALL)
-    set_spread(got, ((0, 0, MID),), averages, spread)
+    loads = loads_of(got, MID, 1)
+    set_spread(loads, (0,), MID, averages, spread)
 
     row = lax.broadcasted_iota(jnp.int32, (TALL, LANES), 0) + (tile * ROWS - REACH)
     col = lane + (block * LANES - REACH)
@@ -545,7 +575,7 @@
     spread_out(near_ok.astype(F32), far_ok.astype(F32), lane, store_inside)
     sweep, scale = localizer(offsets, weights, shared, copies)
     ends[...] = jnp.zeros(ends.shape, F32)
-    block_ends(got, ((RIM, 0, MID),), block, ends)
+    block_ends(loads, (RIM,), MID, block, ends)
     near, far = with_margins(fields[0], 0, block, ends, slice(0, TALL))
 
     def at(source, slot, rows):
@@ -573,7 +603,8 @@
 ):
     spread_mid, shared = handed_on(handed)
     block = place[1]
-    set_spread(got, ((0, 0, RIM), (TALL - RIM, RIM, RIM)), averages, spread)
+    loads, starts = loads_of(got, RIM, 2), (0, TALL - RIM)
+    set_spread(loads, starts, RIM, averages, spread)
 
     @pl.loop(0, SLOTS)
     def _(slot):
@@ -586,7 +617,7 @@
     sweep, scale = localizer(offsets, weights, shared, copies)
     for kind in range(2):
         ends[kind] = shared[SLOTS + 1 + kind]
-    block_ends(got, ((0, 0, RIM), (TALL - RIM, RIM, RIM)), block, ends)
+    block_ends(loads, starts, RIM, block, ends)
     rows = slice(0, TALL)
     near_v, far_v = with_margins(shared[SLOTS + 3], 0, block, ends, rows)
     near_w, far_w = with_margins(shared[SLOTS + 4], 1, block, ends, rows)
@@ -611,17 +642,17 @@
         spread_copies[target] = result
 
 
-def recentre_kernel(middle, rim, increments, out):
+def recentre_kernel(middle, upper, lower, increments, out):
     keep = (ROWS - MID) // 2
     for block in range(GROUPS):
         lanes = slice(block * LANES, (block + 1) * LANES)
         for member in range(LOCAL):
-            out[member, 0:keep, lanes] = rim[member, block, 0:keep, :] + increments[block, 0:keep, :]
+            out[member, 0:keep, lanes] = upper[member, block, 0:keep, :] + increments[block, 0:keep, :]
             out[member, keep : keep + MID, lanes] = (
                 middle[member, block] + increments[block, keep : keep + MID, :]
             )
             out[member, keep + MID : ROWS, lanes] = (
-                rim[member, block, keep : 2 * keep, :] + increments[block, keep + MID : ROWS, :]
+                lower[member, block, 0:keep, :] + increments[block, keep + MID : ROWS, :]
             )
 
 
@@ -647,65 +678,75 @@
     tiles = lax.axis_size("tile")
     keep = (ROWS - MID) // 2
     sems = pltpu.SemaphoreType.DMA
-    buffers = [
-        pltpu.VMEM((LOCAL, GROUPS + 2, HEIGHT, LANES), F32),
-        pltpu.VMEM((LOCAL, GROUPS + 2, HEIGHT, LANES), F32),
-        pltpu.VMEM((2, GROUPS, HEIGHT, LANES), F32),
-        pltpu.VMEM((5, GROUPS, HEIGHT, LANES), F32),
-        pltpu.VMEM((LOCAL, GROUPS + 2, MID, LANES), F32),
-        pltpu.VMEM((LOCAL, GROUPS + 2, MID + 8, LANES), F32),
-        pltpu.VMEM((GROUPS, SLOTS, MID, LANES), F32),
-    ]
-    up, down, fields = pl.pallas_call(
-        message_kernel,
-        out_shape=[array(GROUPS, HALO, LANES), array(GROUPS, HALO, LANES), array(2, ROWS, LANES)],
+
+    def buffers(height, rows, spare):
+        return [
+            pltpu.VMEM((LOCAL, GROUPS + 2, height, LANES), F32),
+            pltpu.VMEM((LOCAL, GROUPS + 2, height, LANES), F32),
+            pltpu.VMEM((2, GROUPS, height, LANES), F32),
+            pltpu.VMEM((5, GROUPS, height, LANES), F32),
+            pltpu.VMEM((LOCAL, GROUPS + 2, rows, LANES), F32),
+            pltpu.VMEM((LOCAL, GROUPS + 2, rows + spare, LANES), F32),
+            pltpu.VMEM((GROUPS, SLOTS * rows, LANES), F32),
+        ]
+
+    dma = [sems((GROUPS,)), sems((2, GROUPS)), sems((GROUPS + 1,))]
+    up, down, middle, send_mid, fields = pl.pallas_call(
+        inner_kernel,
+        out_shape=[
+            array(GROUPS, HALO, LANES),
+            array(GROUPS, HALO, LANES),
+            array(LOCAL, GROUPS, MID, LANES),
+            array(GROUPS, SLOTS * MID, LANES),
+            array(2, ROWS, LANES),
+        ],
         in_specs=in_hbm(6),
-        out_specs=on_vmem(3),
-        scratch_shapes=[
-            pltpu.VMEM(members.shape, F32),
-            pltpu.VMEM((2, ROWS, COLS), F32),
+        out_specs=in_hbm(4) + on_vmem(1),
+        scratch_shapes=buffers(HEIGHT, MID, 0)
+        + [
             pltpu.VMEM((1, 1, 1024), jnp.int32),
             pltpu.VMEM((2, 1, 1, 1024), F32),
-            sems((3,)),
-            sems((3,)),
-        ],
+            pltpu.VMEM((GROUPS, HALO, LANES), F32),
+            pltpu.VMEM((GROUPS, HALO, LANES), F32),
+        ]
+        + dma
+        + [sems((3,))],
         compiler_params=crowded,
-        name="messages",
+        cost_estimate=cost,
+        name="inner",
     )(members, courant_x, courant_y, obs_cell, innovation, obs_weight)
     above = lax.ppermute(down, "tile", [(i, i + 1) for i in range(tiles - 1)])
     below = lax.ppermute(up, "tile", [(i + 1, i) for i in range(tiles - 1)])
-    middle, send_mid = pl.pallas_call(
-        inner_kernel,
-        out_shape=[array(LOCAL, GROUPS, MID, LANES), array(GROUPS, SLOTS, MID, LANES)],
-        in_specs=in_hbm(3) + on_vmem(1),
-        out_specs=in_hbm(2),
-        scratch_shapes=buffers + [sems((GROUPS,)), sems((2, GROUPS)), sems((GROUPS + 1,))],
+    got_mid = exchanged(send_mid, both)
+    upper, send_upper, rim_fields = pl.pallas_call(
+        upper_kernel,
+        out_shape=[
+            array(LOCAL, GROUPS, 8, LANES),
+            array(GROUPS, 2 * SIDE, LANES),
+            array(2, RIM, LANES),
+        ],
+        in_specs=in_hbm(3) + on_vmem(2),
+        out_specs=in_hbm(2) + on_vmem(1),
+        scratch_shapes=buffers(SHORT, RIM, 4) + dma,
         compiler_params=crowded,
         cost_estimate=cost,
-        name="inner",
-    )(members, courant_x, courant_y, fields)
-    send_mid, _ = lax.optimization_barrier((send_mid, above))
-    got_mid = exchanged(send_mid, both)
-    rim, send_rim, fields_tall = pl.pallas_call(
-        outer_kernel,
+        name="upper",
+    )(members, courant_x, courant_y, above, fields)
+    lower, send_rim, fields_tall = pl.pallas_call(
+        lower_kernel,
         out_shape=[
-            array(LOCAL, GROUPS, 2 * keep, LANES),
-            array(GROUPS, SLOTS, MID, LANES),
+            array(LOCAL, GROUPS, 8, LANES),
+            array(GROUPS, 2 * SIDE, LANES),
             array(2, TALL, LANES),
         ],
-        in_specs=in_hbm(3) + on_vmem(3),
+        in_specs=in_hbm(3) + on_vmem(3) + in_hbm(1),
         out_specs=in_hbm(2) + on_vmem(1),
-        scratch_shapes=buffers
-        + [
-            pltpu.VMEM((2, MID, LANES), F32),
-            sems((2, GROUPS)),
-            sems((2, 2, GROUPS)),
-            sems((GROUPS + 1,)),
-        ],
+        scratch_shapes=buffers(SHORT, RIM, 4) + [pltpu.VMEM((2, RIM, LANES), F32)] + dma,
+        input_output_aliases={6: 1},
         compiler_params=crowded,
         cost_estimate=cost,
-        name="outer",
-    )(members, courant_x, courant_y, above, below, fields)
+        name="lower",
+    )(members, courant_x, courant_y, below, fields, rim_fields, send_upper)
     send_rim, got_mid = lax.optimization_barrier((send_rim, got_mid))
     got_rim = exchanged(send_rim, both)
     place = jnp.stack([lax.axis_index("tile"), lax.axis_index(both)]).astype(jnp.int32)
@@ -738,17 +779,16 @@
     analysis = pl.pallas_call(
         recentre_kernel,
         out_shape=array(*members.shape),
-        in_specs=on_vmem(3),
+        in_specs=on_vmem(4),
         out_specs=pl.BlockSpec(memory_space=pltpu.VMEM),
         compiler_params=params,
         name="recentre",
-    )(middle, rim, increments)
+    )(middle, upper, lower, increments)
     return analysis, increment
 
 
 def exchanged(blocks, axes):
-    flat = blocks.reshape(GROUPS, -1, LANES)
-    return lax.all_to_all(flat, axes, 0, 0, tiled=True).reshape(blocks.shape)
+    return lax.all_to_all(blocks, axes, 0, 0, tiled=True)
 
 
 def solution(mesh):

time: 90.9 us -> 90.2 us (level)
  waiting for transfers between devices: 24.2 us -> 14.6 us
  starting transfers between devices: 13.9 us -> 22.2 us
  Pallas kernels: 40.3 us -> 41.3 us
    ppermute x1, waiting for transfers between devices: 11.7 us -> 0.01 us  [on_device(): below = lax.ppermute(up, 'tile', [(i + 1, i) for i in range(tiles - 1)])]
    ppermute x1, starting transfers between devices: 1.92 us -> 7.26 us  [on_device(): below = lax.ppermute(up, 'tile', [(i + 1, i) for i in range(tiles - 1)])]
    all_to_all x2, starting transfers between devices: 10 us -> 13 us  [exchanged(): return lax.all_to_all(blocks, axes, 0, 0, tiled=True)]
    ppermute x1, waiting for transfers between devices: 6.54 us -> 8.65 us  [on_device(): above = lax.ppermute(down, 'tile', [(i, i + 1) for i in range(tiles - 1)])]
    pallas_call x3, Pallas kernels: 16.3 us -> 17.5 us  [the longest x1 6.24 us: on_device(): pl.pallas_call(inner_kernel, out_shape=[array(GROUPS, HALO, LANES), array...]
  transfers between devices with their start and end apart: 4 -> 4, of which waited for: 3 -> 2; matrix products, arithmetic and copies ran while one was open for 0% -> 0% of each run, Pallas kernels for 22% -> 20%
where the time goes in v5:
time: 90.2 us; the launch traced here: 89.6 us
  Pallas kernels  41.3 us (46%)
  starting transfers between devices  22.2 us (25%)
  waiting for transfers between devices  14.6 us (16%)
  blocking collectives  8.91 us (10%)
  local copies, waits for them, and re-layouts  1.76 us (2%)
    pallas_call x1, Pallas kernels, on_device(): pl.pallas_call(analysis_kernel, out_shape=[array(ROWS, LANES), array(GROU...  16.3 us
    all_to_all x2, starting transfers between devices, exchanged(): return lax.all_to_all(blocks, axes, 0, 0, tiled=True)  13 us
    all_to_all x1, blocking collectives, on_device(): increments = lax.all_to_all(copies, both, 0, 0, tiled=True)  8.91 us
    ppermute x1, waiting for transfers between devices, on_device(): above = lax.ppermute(down, 'tile', [(i, i + 1) for i in range(tiles - 1)])  8.65 us
    ppermute x1, starting transfers between devices, on_device(): below = lax.ppermute(up, 'tile', [(i + 1, i) for i in range(tiles - 1)])  7.26 us
    pallas_call x1, Pallas kernels, on_device(): pl.pallas_call(inner_kernel, out_shape=[array(GROUPS, HALO, LANES), array...  6.24 us
    pallas_call x1, Pallas kernels, on_device(): pl.pallas_call(early_kernel, out_shape=array(SPREAD_ROWS + SHARED * TALL,...  6.2 us
    all_to_all x2, waiting for transfers between devices, exchanged(): return lax.all_to_all(blocks, axes, 0, 0, tiled=True)  5.95 us
  transfers between devices with their start and end apart: 4, of which 2 were waited for; matrix products, arithmetic and copies ran while one was open for 0% of the time, Pallas kernels for 20%

profile of v5, /device:TPU:16, one launch (start us, length us, event | category | flops | bytes accessed | tf_op | source)
XLA Modules:
  0.0 89.6 jit_solution(887326070239098928)
XLA Ops:
  0.6 6.2 %inner.1 = (f32[8,136,128]{2,1,0:T(8,128)}, f32[8,136,128]{2,1,0:T(8,128)}, f32[10,8,24,128]{3,2,1,0:T(8,128)}, f32[8,288,128]{2,1,0:T(8,128)}, f32[2,32,128]{2,1,0:T(8,128)}) custom-call(f32[10,32,1024]{2,1,0:T(8,128)} %members.5, f32[32,1024]{1,0:T(8,128)} %courant_x.5, f32[32,1024]{1,0:T(8,128)} %courant_y.5, s32[1,1,1024]{2,1,0:T(1,128)} %cell.1, ...), custom_call_target="tpu_custom_call" | custom-call | flops 10000000 | bytes 60000000 | tf_op jit(solution)/shard_map/inner/pallas_call | solution.py:694
  6.9 0.0 copy-start.9
  6.9 0.0 copy-start.8
  6.9 5.2 %all-to-all-start = ((f32[8,288,128]{2,1,0:T(8,128)}), f32[8,288,128]{2,1,0:T(8,128)S(1)}, u32[]{:S(2)}, u32[]{:S(2)}) async-start(f32[8,288,128]{2,1,0:T(8,128)} %get-tuple-element.26), calls=%async_computation | async-start | bytes 2359296 | tf_op jit(solution)/shard_map/all_to_all | solution.py:791
  12.1 0.0 copy-done.9
  12.1 1.9 %collective-permute-start = (f32[8,136,128]{2,1,0:T(8,128)S(1)}, f32[8,136,128]{2,1,0:T(8,128)S(1)}, u32[]{:S(2)}, u32[]{:S(2)}) collective-permute-start(f32[8,136,128]{2,1,0:T(8,128)S(1)} %copy-done.9), channel_id=1, source_target_pairs={{0,2},{2,4},{4,6},{6,8},{8,10},{10,12},{12,14},{14,16},{16,18},{18... | collective-permute-start | bytes 1671176 | tf_op jit(solution)/shard_map/ppermute | solution.py:718
  14.0 0.0 copy-done.8
  14.0 7.3 %collective-permute-start.1 = (f32[8,136,128]{2,1,0:T(8,128)S(1)}, f32[8,136,128]{2,1,0:T(8,128)S(1)}, u32[]{:S(2)}, u32[]{:S(2)}) collective-permute-start(f32[8,136,128]{2,1,0:T(8,128)S(1)} %copy-done.8), channel_id=1, source_target_pairs={{2,0},{4,2},{6,4},{8,6},{10,8},{12,10},{14,12},{16,14},{18,16},{20... | collective-permute-start | bytes 1671176 | tf_op jit(solution)/shard_map/ppermute | solution.py:719
  21.3 8.7 %collective-permute-done.above = f32[8,136,128]{2,1,0:T(8,128)S(1)} collective-permute-done((f32[8,136,128]{2,1,0:T(8,128)S(1)}, f32[8,136,128]{2,1,0:T(8,128)S(1)}, u32[]{:S(2)}, u32[]{:S(2)}) %collective-permute-start) | collective-permute-done | bytes 557088 | tf_op jit(solution)/shard_map/ppermute | solution.py:718
  29.9 0.0 copy-start.6
  29.9 0.8 copy-done.6
  30.7 5.6 %upper.1 = (f32[10,8,8,128]{3,2,1,0:T(8,128)}, f32[8,288,128]{2,1,0:T(8,128)}, f32[2,12,128]{2,1,0:T(8,128)}) custom-call(f32[10,32,1024]{2,1,0:T(8,128)} %members.5, f32[32,1024]{1,0:T(8,128)} %courant_x.5, f32[32,1024]{1,0:T(8,128)} %courant_y.5, f32[8,136,128]{2,1,0:T(8,128)} %copy-done.6, f32[2,32,128]{2,1,0:T(8,128)} %get-tuple-element.19.fields), custom_call_target="tpu_custom_call" | custom-call | flops 10000000 | bytes 60000000 | tf_op jit(solution)/shard_map/upper/pallas_call | solution.py:721
  36.4 0.0 collective-permute-done.1.below
  36.4 0.0 copy-start.5
  36.4 0.8 copy-done.5
  37.2 5.7 %lower.1 = (f32[10,8,8,128]{3,2,1,0:T(8,128)}, f32[8,288,128]{2,1,0:T(8,128)}, f32[2,48,128]{2,1,0:T(8,128)}) custom-call(f32[10,32,1024]{2,1,0:T(8,128)} %members.5, f32[32,1024]{1,0:T(8,128)} %courant_x.5, f32[32,1024]{1,0:T(8,128)} %courant_y.5, f32[8,136,128]{2,1,0:T(8,128)} %copy-done.5, ...), custom_call_target="tpu_custom_call", output_to_operand_aliasing={{1}: (6, {})} | custom-call | flops 10000000 | bytes 60000000 | tf_op jit(solution)/shard_map/lower/pallas_call | solution.py:735
  42.9 0.0 all-to-all-done.got
  42.9 0.0 copy-start.7
  42.9 0.0 copy-start.3
  42.9 0.0 copy-start.4
  42.9 7.8 %all-to-all-start.1 = ((f32[8,288,128]{2,1,0:T(8,128)}), f32[8,288,128]{2,1,0:T(8,128)}, u32[]{:S(2)}, u32[]{:S(2)}) async-start(f32[8,288,128]{2,1,0:T(8,128)} %get-tuple-element.27), calls=%async_computation.1 | async-start | bytes 2359296 | tf_op jit(solution)/shard_map/all_to_all | solution.py:791
  50.8 0.0 copy-done.7
  50.8 0.1 copy.12.offsets
  50.9 0.1 pad_add_fusion.place
  50.9 0.0 copy-done.3
  50.9 0.0 copy-done.4
  50.9 6.2 %early.1.handed = f32[3120,128]{1,0:T(8,128)S(1)} custom-call(s32[2]{0:T(128)S(1)} %pad_add_fusion.place, s32[9,2]{1,0:T(8,128)S(1)} %copy.12.offsets, f32[9]{0:T(128)S(1)} %copy-done.4, f32[8,288,128]{2,1,0:T(8,128)S(1)} %all-to-all-done.got, f32[2,48,128]{2,1,0:T(8,128)S(1)} %copy-done.3), custom_call_target="tpu_custom_call" | custom-call | flops 10000000 | bytes 60000000 | tf_op jit(solution)/shard_map/early/pallas_call | solution.py:759
  57.1 0.0 copy-start
  57.2 0.0 copy-start.1
  57.2 0.0 copy-start.2
  57.2 5.9 %all-to-all-done.1.got = f32[8,288,128]{2,1,0:T(8,128)} async-done(((f32[8,288,128]{2,1,0:T(8,128)}), f32[8,288,128]{2,1,0:T(8,128)}, u32[]{:S(2)}, u32[]{:S(2)}) %all-to-all-start.1) | async-done | bytes 1179680 | tf_op jit(solution)/shard_map/all_to_all | solution.py:791
  63.1 16.3 %analysis.1 = (f32[32,128]{1,0:T(8,128)}, f32[8,32,128]{2,1,0:T(8,128)S(1)}) custom-call(s32[2]{0:T(128)S(1)} %pad_add_fusion.place, s32[9,2]{1,0:T(8,128)S(1)} %copy.12.offsets, f32[9]{0:T(128)S(1)} %copy-done.4, f32[8,288,128]{2,1,0:T(8,128)} %all-to-all-done.1.got, f32[3120,128]{1,0:T(8,128)S(1)} %early.1.handed), custom_call_target="tpu_custom_call" | custom-call | tf_op jit(solution)/shard_map/analysis/pallas_call | solution.py:769
  79.4 8.9 %all_to_all.15.increments = f32[8,32,128]{2,1,0:T(8,128)S(1)} all-to-all(f32[8,32,128]{2,1,0:T(8,128)S(1)} %get-tuple-element.30), channel_id=1, replica_groups=mesh['member'=4,'tile'=32,'grp'=2] {'member','grp'}, dimensions={0} | all-to-all | bytes 262144 | tf_op jit(solution)/shard_map/all_to_all | solution.py:778
  88.3 0.0 copy-done
  88.3 0.0 copy-done.1
  88.3 0.0 copy-done.2
  88.3 1.3 %recentre.1 = f32[10,32,1024]{2,1,0:T(8,128)} custom-call(f32[10,8,24,128]{3,2,1,0:T(8,128)S(1)} %copy-done, f32[10,8,8,128]{3,2,1,0:T(8,128)S(1)} %copy-done.1, f32[10,8,8,128]{3,2,1,0:T(8,128)S(1)} %copy-done.2, f32[8,32,128]{2,1,0:T(8,128)S(1)} %all_to_all.15.increments), custom_call_target="tpu_custom_call" | custom-call | tf_op jit(solution)/shard_map/recentre/pallas_call | solution.py:779
Async XLA Ops:
  6.9 5.2 %copy-start.9 = (f32[8,136,128]{2,1,0:T(8,128)S(1)}, f32[8,136,128]{2,1,0:T(8,128)}, u32[]{:S(2)}) copy-start(f32[8,136,128]{2,1,0:T(8,128)} %get-tuple-element.18) | copy-start | bytes 1671172
  6.9 7.1 %copy-start.8 = (f32[8,136,128]{2,1,0:T(8,128)S(1)}, f32[8,136,128]{2,1,0:T(8,128)}, u32[]{:S(2)}) copy-start(f32[8,136,128]{2,1,0:T(8,128)} %get-tuple-element.21) | copy-start | bytes 1671172
  6.9 36.0 %all-to-all-start = ((f32[8,288,128]{2,1,0:T(8,128)}), f32[8,288,128]{2,1,0:T(8,128)S(1)}, u32[]{:S(2)}, u32[]{:S(2)}) async-start(f32[8,288,128]{2,1,0:T(8,128)} %get-tuple-element.26), calls=%async_computation | async-start | bytes 2359296 | tf_op jit(solution)/shard_map/all_to_all | solution.py:791
  12.1 17.9 %collective-permute-start = (f32[8,136,128]{2,1,0:T(8,128)S(1)}, f32[8,136,128]{2,1,0:T(8,128)S(1)}, u32[]{:S(2)}, u32[]{:S(2)}) collective-permute-start(f32[8,136,128]{2,1,0:T(8,128)S(1)} %copy-done.9), channel_id=1, source_target_pairs={{0,2},{2,4},{4,6},{6,8},{8,10},{10,12},{12,14},{14,16},{16,18},{18... | collective-permute-start | bytes 1671176 | tf_op jit(solution)/shard_map/ppermute | solution.py:718
  14.0 22.4 %collective-permute-start.1 = (f32[8,136,128]{2,1,0:T(8,128)S(1)}, f32[8,136,128]{2,1,0:T(8,128)S(1)}, u32[]{:S(2)}, u32[]{:S(2)}) collective-permute-start(f32[8,136,128]{2,1,0:T(8,128)S(1)} %copy-done.8), channel_id=1, source_target_pairs={{2,0},{4,2},{6,4},{8,6},{10,8},{12,10},{14,12},{16,14},{18,16},{20... | collective-permute-start | bytes 1671176 | tf_op jit(solution)/shard_map/ppermute | solution.py:719
  29.9 0.8 copy-start.6
  36.4 0.8 copy-start.5
  42.9 7.9 %copy-start.7 = (s32[9,2]{0,1:T(2,128)S(1)}, s32[9,2]{0,1:T(2,128)}, u32[]{:S(2)}) copy-start(s32[9,2]{0,1:T(2,128)} %param.14) | copy-start | bytes 220
  42.9 8.0 %copy-start.3 = (f32[2,48,128]{2,1,0:T(8,128)S(1)}, f32[2,48,128]{2,1,0:T(8,128)}, u32[]{:S(2)}) copy-start(f32[2,48,128]{2,1,0:T(8,128)} %get-tuple-element.29.fields) | copy-start | bytes 147460
  42.9 8.0 %copy-start.4 = (f32[9]{0:T(128)S(1)}, f32[9]{0:T(128)}, u32[]{:S(2)}) copy-start(f32[9]{0:T(128)} %weights.3) | copy-start | bytes 112
  42.9 20.2 %all-to-all-start.1 = ((f32[8,288,128]{2,1,0:T(8,128)}), f32[8,288,128]{2,1,0:T(8,128)}, u32[]{:S(2)}, u32[]{:S(2)}) async-start(f32[8,288,128]{2,1,0:T(8,128)} %get-tuple-element.27), calls=%async_computation.1 | async-start | bytes 2359296 | tf_op jit(solution)/shard_map/all_to_all | solution.py:791
  57.1 31.2 %copy-start = (f32[10,8,24,128]{3,2,1,0:T(8,128)S(1)}, f32[10,8,24,128]{3,2,1,0:T(8,128)}, u32[]{:S(2)}) copy-start(f32[10,8,24,128]{3,2,1,0:T(8,128)} %get-tuple-element.17.middle) | copy-start | bytes 2949124
  57.2 31.2 %copy-start.1 = (f32[10,8,8,128]{3,2,1,0:T(8,128)S(1)}, f32[10,8,8,128]{3,2,1,0:T(8,128)}, u32[]{:S(2)}) copy-start(f32[10,8,8,128]{3,2,1,0:T(8,128)} %get-tuple-element.20.upper) | copy-start | bytes 983044
  57.2 31.2 %copy-start.2 = (f32[10,8,8,128]{3,2,1,0:T(8,128)S(1)}, f32[10,8,8,128]{3,2,1,0:T(8,128)}, u32[]{:S(2)}) copy-start(f32[10,8,8,128]{3,2,1,0:T(8,128)} %get-tuple-element.24.lower) | copy-start | bytes 983044

commit v6 on v5

--- a/solution.py
+++ b/solution.py
@@ -71,7 +71,7 @@
     lane = lane_ids(8)
     first, last = lane == 0, lane == LANES - 1
 
-    @pl.loop(0, GROUPS, unroll=4)
+    @pl.loop(0, GROUPS, unroll=8)
     def _(block):
         for low, home in zip(starts, homes):
             rows = slice(low, low + 8)

time: 90.2 us -> 89.8 us (level)
  transfers between devices with their start and end apart: 4 -> 4, of which waited for: 2 -> 2; matrix products, arithmetic and copies ran while one was open for 0% -> 0% of each run, Pallas kernels for 20% -> 19%
where the time goes in v6:
time: 89.8 us; the launch traced here: 89.1 us
  Pallas kernels  40.7 us (45%)
  starting transfers between devices  22.2 us (25%)
  waiting for transfers between devices  14.7 us (16%)
  blocking collectives  8.91 us (10%)
  local copies, waits for them, and re-layouts  1.76 us (2%)
    pallas_call x1, Pallas kernels, on_device(): pl.pallas_call(analysis_kernel, out_shape=[array(ROWS, LANES), array(GROU...  16.4 us
    all_to_all x2, starting transfers between devices, exchanged(): return lax.all_to_all(blocks, axes, 0, 0, tiled=True)  13 us
    all_to_all x1, blocking collectives, on_device(): increments = lax.all_to_all(copies, both, 0, 0, tiled=True)  8.91 us
    ppermute x1, waiting for transfers between devices, on_device(): above = lax.ppermute(down, 'tile', [(i, i + 1) for i in range(tiles - 1)])  8.65 us
    ppermute x1, starting transfers between devices, on_device(): below = lax.ppermute(up, 'tile', [(i + 1, i) for i in range(tiles - 1)])  7.26 us
    pallas_call x1, Pallas kernels, on_device(): pl.pallas_call(inner_kernel, out_shape=[array(GROUPS, HALO, LANES), array...  6.38 us
    pallas_call x1, Pallas kernels, on_device(): pl.pallas_call(early_kernel, out_shape=array(SPREAD_ROWS + SHARED * TALL,...  6.08 us
    all_to_all x2, waiting for transfers between devices, exchanged(): return lax.all_to_all(blocks, axes, 0, 0, tiled=True)  6.06 us
  transfers between devices with their start and end apart: 4, of which 2 were waited for; matrix products, arithmetic and copies ran while one was open for 0% of the time, Pallas kernels for 19%

profile of v6, /device:TPU:16, one launch (start us, length us, event | category | flops | bytes accessed | tf_op | source)
XLA Modules:
  0.0 89.1 jit_solution(10513583602523720130)
XLA Ops:
  0.6 6.4 %inner.1 = (f32[8,136,128]{2,1,0:T(8,128)}, f32[8,136,128]{2,1,0:T(8,128)}, f32[10,8,24,128]{3,2,1,0:T(8,128)}, f32[8,288,128]{2,1,0:T(8,128)}, f32[2,32,128]{2,1,0:T(8,128)}) custom-call(f32[10,32,1024]{2,1,0:T(8,128)} %members.5, f32[32,1024]{1,0:T(8,128)} %courant_x.5, f32[32,1024]{1,0:T(8,128)} %courant_y.5, s32[1,1,1024]{2,1,0:T(1,128)} %cell.1, ...), custom_call_target="tpu_custom_call" | custom-call | flops 10000000 | bytes 60000000 | tf_op jit(solution)/shard_map/inner/pallas_call | solution.py:694
  7.0 0.0 copy-start.9
  7.0 0.0 copy-start.8
  7.0 5.2 %all-to-all-start = ((f32[8,288,128]{2,1,0:T(8,128)}), f32[8,288,128]{2,1,0:T(8,128)S(1)}, u32[]{:S(2)}, u32[]{:S(2)}) async-start(f32[8,288,128]{2,1,0:T(8,128)} %get-tuple-element.26), calls=%async_computation | async-start | bytes 2359296 | tf_op jit(solution)/shard_map/all_to_all | solution.py:791
  12.2 0.0 copy-done.9
  12.2 1.9 %collective-permute-start = (f32[8,136,128]{2,1,0:T(8,128)S(1)}, f32[8,136,128]{2,1,0:T(8,128)S(1)}, u32[]{:S(2)}, u32[]{:S(2)}) collective-permute-start(f32[8,136,128]{2,1,0:T(8,128)S(1)} %copy-done.9), channel_id=1, source_target_pairs={{0,2},{2,4},{4,6},{6,8},{8,10},{10,12},{12,14},{14,16},{16,18},{18... | collective-permute-start | bytes 1671176 | tf_op jit(solution)/shard_map/ppermute | solution.py:718
  14.1 0.0 copy-done.8
  14.1 7.3 %collective-permute-start.1 = (f32[8,136,128]{2,1,0:T(8,128)S(1)}, f32[8,136,128]{2,1,0:T(8,128)S(1)}, u32[]{:S(2)}, u32[]{:S(2)}) collective-permute-start(f32[8,136,128]{2,1,0:T(8,128)S(1)} %copy-done.8), channel_id=1, source_target_pairs={{2,0},{4,2},{6,4},{8,6},{10,8},{12,10},{14,12},{16,14},{18,16},{20... | collective-permute-start | bytes 1671176 | tf_op jit(solution)/shard_map/ppermute | solution.py:719
  21.4 8.7 %collective-permute-done.above = f32[8,136,128]{2,1,0:T(8,128)S(1)} collective-permute-done((f32[8,136,128]{2,1,0:T(8,128)S(1)}, f32[8,136,128]{2,1,0:T(8,128)S(1)}, u32[]{:S(2)}, u32[]{:S(2)}) %collective-permute-start) | collective-permute-done | bytes 557088 | tf_op jit(solution)/shard_map/ppermute | solution.py:718
  30.1 0.0 copy-start.6
  30.1 0.8 copy-done.6
  30.9 5.2 %upper.1 = (f32[10,8,8,128]{3,2,1,0:T(8,128)}, f32[8,288,128]{2,1,0:T(8,128)}, f32[2,12,128]{2,1,0:T(8,128)}) custom-call(f32[10,32,1024]{2,1,0:T(8,128)} %members.5, f32[32,1024]{1,0:T(8,128)} %courant_x.5, f32[32,1024]{1,0:T(8,128)} %courant_y.5, f32[8,136,128]{2,1,0:T(8,128)} %copy-done.6, f32[2,32,128]{2,1,0:T(8,128)} %get-tuple-element.19.fields), custom_call_target="tpu_custom_call" | custom-call | flops 10000000 | bytes 60000000 | tf_op jit(solution)/shard_map/upper/pallas_call | solution.py:721
  36.1 0.0 collective-permute-done.1.below
  36.1 0.0 copy-start.5
  36.1 0.8 copy-done.5
  37.0 5.3 %lower.1 = (f32[10,8,8,128]{3,2,1,0:T(8,128)}, f32[8,288,128]{2,1,0:T(8,128)}, f32[2,48,128]{2,1,0:T(8,128)}) custom-call(f32[10,32,1024]{2,1,0:T(8,128)} %members.5, f32[32,1024]{1,0:T(8,128)} %courant_x.5, f32[32,1024]{1,0:T(8,128)} %courant_y.5, f32[8,136,128]{2,1,0:T(8,128)} %copy-done.5, ...), custom_call_target="tpu_custom_call", output_to_operand_aliasing={{1}: (6, {})} | custom-call | flops 10000000 | bytes 60000000 | tf_op jit(solution)/shard_map/lower/pallas_call | solution.py:735
  42.3 0.0 all-to-all-done.got
  42.3 0.0 copy-start.7
  42.3 0.0 copy-start.3
  42.3 0.0 copy-start.4
  42.3 7.8 %all-to-all-start.1 = ((f32[8,288,128]{2,1,0:T(8,128)}), f32[8,288,128]{2,1,0:T(8,128)}, u32[]{:S(2)}, u32[]{:S(2)}) async-start(f32[8,288,128]{2,1,0:T(8,128)} %get-tuple-element.27), calls=%async_computation.1 | async-start | bytes 2359296 | tf_op jit(solution)/shard_map/all_to_all | solution.py:791
  50.1 0.0 copy-done.7
  50.1 0.1 copy.12.offsets
  50.2 0.1 pad_add_fusion.place
  50.3 0.0 copy-done.3
  50.3 0.0 copy-done.4
  50.3 6.1 %early.1.handed = f32[3120,128]{1,0:T(8,128)S(1)} custom-call(s32[2]{0:T(128)S(1)} %pad_add_fusion.place, s32[9,2]{1,0:T(8,128)S(1)} %copy.12.offsets, f32[9]{0:T(128)S(1)} %copy-done.4, f32[8,288,128]{2,1,0:T(8,128)S(1)} %all-to-all-done.got, f32[2,48,128]{2,1,0:T(8,128)S(1)} %copy-done.3), custom_call_target="tpu_custom_call" | custom-call | flops 10000000 | bytes 60000000 | tf_op jit(solution)/shard_map/early/pallas_call | solution.py:759
  56.4 0.0 copy-start
  56.4 0.0 copy-start.1
  56.4 0.0 copy-start.2
  56.4 6.1 %all-to-all-done.1.got = f32[8,288,128]{2,1,0:T(8,128)} async-done(((f32[8,288,128]{2,1,0:T(8,128)}), f32[8,288,128]{2,1,0:T(8,128)}, u32[]{:S(2)}, u32[]{:S(2)}) %all-to-all-start.1) | async-done | bytes 1179680 | tf_op jit(solution)/shard_map/all_to_all | solution.py:791
  62.5 16.4 %analysis.1 = (f32[32,128]{1,0:T(8,128)}, f32[8,32,128]{2,1,0:T(8,128)S(1)}) custom-call(s32[2]{0:T(128)S(1)} %pad_add_fusion.place, s32[9,2]{1,0:T(8,128)S(1)} %copy.12.offsets, f32[9]{0:T(128)S(1)} %copy-done.4, f32[8,288,128]{2,1,0:T(8,128)} %all-to-all-done.1.got, f32[3120,128]{1,0:T(8,128)S(1)} %early.1.handed), custom_call_target="tpu_custom_call" | custom-call | tf_op jit(solution)/shard_map/analysis/pallas_call | solution.py:769
  78.9 8.9 %all_to_all.15.increments = f32[8,32,128]{2,1,0:T(8,128)S(1)} all-to-all(f32[8,32,128]{2,1,0:T(8,128)S(1)} %get-tuple-element.30), channel_id=1, replica_groups=mesh['member'=4,'tile'=32,'grp'=2] {'member','grp'}, dimensions={0} | all-to-all | bytes 262144 | tf_op jit(solution)/shard_map/all_to_all | solution.py:778
  87.8 0.0 copy-done
  87.8 0.0 copy-done.1
  87.8 0.0 copy-done.2
  87.8 1.3 %recentre.1 = f32[10,32,1024]{2,1,0:T(8,128)} custom-call(f32[10,8,24,128]{3,2,1,0:T(8,128)S(1)} %copy-done, f32[10,8,8,128]{3,2,1,0:T(8,128)S(1)} %copy-done.1, f32[10,8,8,128]{3,2,1,0:T(8,128)S(1)} %copy-done.2, f32[8,32,128]{2,1,0:T(8,128)S(1)} %all_to_all.15.increments), custom_call_target="tpu_custom_call" | custom-call | tf_op jit(solution)/shard_map/recentre/pallas_call | solution.py:779
Async XLA Ops:
  7.0 5.2 %copy-start.9 = (f32[8,136,128]{2,1,0:T(8,128)S(1)}, f32[8,136,128]{2,1,0:T(8,128)}, u32[]{:S(2)}) copy-start(f32[8,136,128]{2,1,0:T(8,128)} %get-tuple-element.18) | copy-start | bytes 1671172
  7.0 7.1 %copy-start.8 = (f32[8,136,128]{2,1,0:T(8,128)S(1)}, f32[8,136,128]{2,1,0:T(8,128)}, u32[]{:S(2)}) copy-start(f32[8,136,128]{2,1,0:T(8,128)} %get-tuple-element.21) | copy-start | bytes 1671172
  7.0 35.2 %all-to-all-start = ((f32[8,288,128]{2,1,0:T(8,128)}), f32[8,288,128]{2,1,0:T(8,128)S(1)}, u32[]{:S(2)}, u32[]{:S(2)}) async-start(f32[8,288,128]{2,1,0:T(8,128)} %get-tuple-element.26), calls=%async_computation | async-start | bytes 2359296 | tf_op jit(solution)/shard_map/all_to_all | solution.py:791
  12.2 17.9 %collective-permute-start = (f32[8,136,128]{2,1,0:T(8,128)S(1)}, f32[8,136,128]{2,1,0:T(8,128)S(1)}, u32[]{:S(2)}, u32[]{:S(2)}) collective-permute-start(f32[8,136,128]{2,1,0:T(8,128)S(1)} %copy-done.9), channel_id=1, source_target_pairs={{0,2},{2,4},{4,6},{6,8},{8,10},{10,12},{12,14},{14,16},{16,18},{18... | collective-permute-start | bytes 1671176 | tf_op jit(solution)/shard_map/ppermute | solution.py:718
  14.1 22.0 %collective-permute-start.1 = (f32[8,136,128]{2,1,0:T(8,128)S(1)}, f32[8,136,128]{2,1,0:T(8,128)S(1)}, u32[]{:S(2)}, u32[]{:S(2)}) collective-permute-start(f32[8,136,128]{2,1,0:T(8,128)S(1)} %copy-done.8), channel_id=1, source_target_pairs={{2,0},{4,2},{6,4},{8,6},{10,8},{12,10},{14,12},{16,14},{18,16},{20... | collective-permute-start | bytes 1671176 | tf_op jit(solution)/shard_map/ppermute | solution.py:719
  30.1 0.8 copy-start.6
  36.1 0.8 copy-start.5
  42.3 7.9 %copy-start.7 = (s32[9,2]{0,1:T(2,128)S(1)}, s32[9,2]{0,1:T(2,128)}, u32[]{:S(2)}) copy-start(s32[9,2]{0,1:T(2,128)} %param.14) | copy-start | bytes 220
  42.3 8.0 %copy-start.3 = (f32[2,48,128]{2,1,0:T(8,128)S(1)}, f32[2,48,128]{2,1,0:T(8,128)}, u32[]{:S(2)}) copy-start(f32[2,48,128]{2,1,0:T(8,128)} %get-tuple-element.29.fields) | copy-start | bytes 147460
  42.3 8.0 %copy-start.4 = (f32[9]{0:T(128)S(1)}, f32[9]{0:T(128)}, u32[]{:S(2)}) copy-start(f32[9]{0:T(128)} %weights.3) | copy-start | bytes 112
  42.3 20.2 %all-to-all-start.1 = ((f32[8,288,128]{2,1,0:T(8,128)}), f32[8,288,128]{2,1,0:T(8,128)}, u32[]{:S(2)}, u32[]{:S(2)}) async-start(f32[8,288,128]{2,1,0:T(8,128)} %get-tuple-element.27), calls=%async_computation.1 | async-start | bytes 2359296 | tf_op jit(solution)/shard_map/all_to_all | solution.py:791
  56.4 31.4 %copy-start = (f32[10,8,24,128]{3,2,1,0:T(8,128)S(1)}, f32[10,8,24,128]{3,2,1,0:T(8,128)}, u32[]{:S(2)}) copy-start(f32[10,8,24,128]{3,2,1,0:T(8,128)} %get-tuple-element.17.middle) | copy-start | bytes 2949124
  56.4 31.4 %copy-start.1 = (f32[10,8,8,128]{3,2,1,0:T(8,128)S(1)}, f32[10,8,8,128]{3,2,1,0:T(8,128)}, u32[]{:S(2)}) copy-start(f32[10,8,8,128]{3,2,1,0:T(8,128)} %get-tuple-element.20.upper) | copy-start | bytes 983044
  56.4 31.4 %copy-start.2 = (f32[10,8,8,128]{3,2,1,0:T(8,128)S(1)}, f32[10,8,8,128]{3,2,1,0:T(8,128)}, u32[]{:S(2)}) copy-start(f32[10,8,8,128]{3,2,1,0:T(8,128)} %get-tuple-element.24.lower) | copy-start | bytes 983044
